TPU v7x, 32 devices: a whole 2x2x4 slice. The times are simulated.
32 devices in a mesh: rows: 8 (over z, x), feat: 4 (over y, core).
Axes of the slice: x: 2, y: 2, z: 4, core: 2. Of those that a mesh axis runs over, the one named last changes fastest.
Arguments:
- band_feats: float32 [4096, 1024], P('rows', 'feat'), may hold values from -6 to 6
- head_feats: float32 [512, 1024], P('rows', 'feat'), may hold values from -6 to 6
- mix_weights: bfloat16 [2, 1024, 1024], P(None, None, 'feat'), may hold values from -0.1875 to 0.1875
- tile_place: int32 [256, 3], P('rows'), may hold values from -1 to 3, as said below
- tile_vals: bfloat16 [256, 128, 128], P('rows'), may hold values from -1 to 1
- arrow_cols: bfloat16 [4096, 512], P('rows'), may hold values from -1 to 1
- arrow_reach: int32 [4096], P('rows'), may hold values from 1 to 512
- arrow_rows: bfloat16 [512, 4096], P(None, 'rows'), may hold values from -0.5 to 0.5
- band_degree: int32 [4096], P('rows'), may hold values from 8 to 32
- head_degree: int32 [512], replicated, may hold values from 8 to 32
Outputs:
- band_out: float32 [4096, 1024], P('rows', 'feat')
- head_out: float32 [512, 1024], P('rows', 'feat')
Inputs may be any that keep to these rules, and one draw needn't show every extreme that they name: `tile_place`: row and column lie in 0 to 3 and the offset in -1 to 1; the 32 slots of every block hold offsets -1, 0 and 1.
All inputs are finite; a program needn't handle non-finite values.
Results may differ from a plain program's by a relative error of at most 0.0057.
Values may be sent and summed in bfloat16 or wider, within the bound.
No kernel may reach another device: no remote copies, remote signals or barrier semaphores. Data moves between devices by JAX's collectives and lax.ppermute only.
A program may use at most 64 MiB of HBM per device.

v0:
```python
import jax
import jax.numpy as jnp
from jax import lax
from jax.sharding import PartitionSpec as P


def extended(cells, sides, width):
    for axis, dim in sides:
        count = lax.axis_size(axis)
        ends = count - 1
        head = lax.slice_in_dim(cells, 0, width, axis=dim)
        tail = lax.slice_in_dim(cells, cells.shape[dim] - width, cells.shape[dim], axis=dim)
        cells = jnp.concatenate(
            [
                lax.ppermute(tail, axis, [(i, (i + 1) % count) for i in range(ends)]),
                cells,
                lax.ppermute(head, axis, [((i + 1) % count, i) for i in range(ends)]),
            ],
            axis=dim,
        )
    return cells


def body(
    band_feats,
    head_feats,
    mix_weights,
    tile_place,
    tile_vals,
    arrow_cols,
    arrow_reach,
    arrow_rows,
    band_degree,
    head_degree,
):
    rows_dev = band_feats.shape[0]
    head_dev = head_feats.shape[0]
    tile_size = tile_vals.shape[1]
    tile_rows = rows_dev // tile_size
    arrow_width = arrow_cols.shape[1]
    feat_dev = band_feats.shape[1]
    position = lax.axis_index("rows")
    reach_mask = lax.broadcasted_iota(jnp.int32, (rows_dev, arrow_width), 1) < arrow_reach[:, None]
    masked_cols = jnp.where(reach_mask, arrow_cols, jnp.zeros_like(arrow_cols))
    window_col = (tile_place[:, 2] + 1) * tile_rows + tile_place[:, 1]
    row_onehot = (
        tile_place[:, 0][None, :] == lax.broadcasted_iota(jnp.int32, (tile_rows, 1), 0)
    ).astype(jnp.float32)
    band_scale = lax.rsqrt(band_degree.astype(jnp.float32))[:, None]
    head_scale_all = lax.rsqrt(head_degree.astype(jnp.float32))[:, None]
    own_head_scale = lax.dynamic_slice_in_dim(head_scale_all, position * head_dev, head_dev, 0)
    band_state, head_state = (band_feats, head_feats)
    for layer_step in range(mix_weights.shape[0]):
        mixing = mix_weights[layer_step]
        zero_init = (
            jnp.zeros((rows_dev, feat_dev), jnp.float32),
            jnp.zeros((head_dev, feat_dev), jnp.float32),
        )

        def transform(totals, pieces, start, mixing=mixing):
            return (
                jnp.dot(pieces[0], mixing, preferred_element_type=jnp.float32),
                jnp.dot(pieces[1], mixing, preferred_element_type=jnp.float32),
            )

        band_x, head_x = transform(
            zero_init,
            (
                lax.all_gather(band_state.astype(jnp.bfloat16), "feat", axis=1, tiled=True),
                lax.all_gather(head_state.astype(jnp.bfloat16), "feat", axis=1, tiled=True),
            ),
            jnp.int32(0),
        )
        band_x = band_x.astype(jnp.bfloat16)
        head_x = head_x.astype(jnp.bfloat16)
        whole_head = lax.all_gather(head_x, "rows", axis=0, tiled=True)
        window = extended(band_x, (("rows", 0),), rows_dev)
        picked = window.reshape(3 * tile_rows, tile_size, feat_dev)[window_col]
        products = jnp.einsum("sij,sjf->sif", tile_vals, picked, preferred_element_type=jnp.float32)
        band_sum = jnp.einsum(
            "rs,sif->rif", row_onehot, products, precision=lax.Precision.HIGHEST
        ).reshape(rows_dev, feat_dev)
        band_sum = band_sum + jnp.dot(masked_cols, whole_head, preferred_element_type=jnp.float32)
        head_part = jnp.dot(arrow_rows, band_x, preferred_element_type=jnp.float32)
        head_total = lax.psum(head_part, "rows")
        head_sum = lax.dynamic_slice_in_dim(head_total, position * head_dev, head_dev, 0)
        band_state = jnp.maximum(band_sum * band_scale, 0.0)
        head_state = jnp.maximum(head_sum * own_head_scale, 0.0)
    return (band_state, head_state)


def solution(mesh):
    in_specs = (
        P("rows", "feat"),
        P("rows", "feat"),
        P(None, None, "feat"),
        P("rows", None),
        P("rows", None, None),
        P("rows", None),
        P("rows"),
        P(None, "rows"),
        P("rows"),
        P(),
    )
    out_specs = (P("rows", "feat"), P("rows", "feat"))
    return jax.shard_map(body, mesh=mesh, in_specs=in_specs, out_specs=out_specs, check_vma=False)
```

profile of v0, /device:TPU:0, one launch (start us, length us, event | category | flops | bytes accessed | tf_op | source)
XLA Modules:
  0.0 231.5 jit_solution(11819811561977603957)
XLA Ops:
  7.2 0.0 copy-start
  7.2 0.0 copy-start.2
  7.2 0.0 all-gather.3.cloned.1.call-start
  7.3 1.9 convert_element_type.31
  9.2 0.0 all-gather.3.cloned.1.call-update
  9.2 0.0 all-gather.5.cloned.1.call-start
  9.2 0.8 convert_element_type.33
  10.1 6.5 %all_gather.19 = bf16[64,1024]{1,0:T(8,128)(2,1)S(1)} all-gather(bf16[64,256]{1,0:T(8,128)(2,1)S(1)} %convert_element_type.33), channel_id=1, replica_groups=mesh['rows'=8,'feat'=4] {'feat'}, dimensions={1}, use_global_device_ids=true | all-gather | bytes 163840 | tf_op jit(solution)/shard_map/all_gather | solution.py:70
  16.6 1.2 convolution_convert_fusion.3
  17.8 31.5 %all_gather.20 = bf16[512,256]{1,0:T(8,128)(2,1)S(1)} all-gather(bf16[64,256]{1,0:T(8,128)(2,1)S(1)} %convolution_convert_fusion.3), channel_id=1, replica_groups=mesh['rows'=8,'feat'=4] {'rows'}, dimensions={0}, use_global_device_ids=true | all-gather | bytes 294912 | tf_op jit(solution)/shard_map/all_gather | solution.py:76
  49.4 0.0 all-gather.3.cloned.1.call-done
  49.4 1.7 convolution_convert_fusion.1
  51.1 3.3 %collective-permute-start = (bf16[512,256]{1,0:T(8,128)(2,1)S(1)}, bf16[512,256]{1,0:T(8,128)(2,1)S(1)}, u32[]{:S(2)}, u32[]{:S(2)}) collective-permute-start(bf16[512,256]{1,0:T(8,128)(2,1)S(1)} %convolution_convert_fusion.1), channel_id=1, source_target_pairs={{0,4},{4,8},{8,12},{12,16},{16,20},{20,24},{24,28},{1,5},{5,9},{9,... | collective-permute-start | bytes 786440 | tf_op jit(solution)/shard_map/ppermute | solution.py:15
  54.4 1.3 collective-permute-start.1
  55.7 2.5 %collective-permute-done = bf16[512,256]{1,0:T(8,128)(2,1)S(1)} collective-permute-done((bf16[512,256]{1,0:T(8,128)(2,1)S(1)}, bf16[512,256]{1,0:T(8,128)(2,1)S(1)}, u32[]{:S(2)}, u32[]{:S(2)}) %collective-permute-start) | collective-permute-done | bytes 262176 | tf_op jit(solution)/shard_map/ppermute | solution.py:15
  58.3 4.4 %collective-permute-done.1 = bf16[512,256]{1,0:T(8,128)(2,1)S(1)} collective-permute-done((bf16[512,256]{1,0:T(8,128)(2,1)S(1)}, bf16[512,256]{1,0:T(8,128)(2,1)S(1)}, u32[]{:S(2)}, u32[]{:S(2)}) %collective-permute-start.1) | collective-permute-done | bytes 262176 | tf_op jit(solution)/shard_map/ppermute | solution.py:17
  62.7 0.1 pad_maximum_fusion
  62.7 2.0 gather_fusion
  64.8 4.3 %fusion.28 = f32[32,256,128]{2,1,0:T(8,128)} fusion(bf16[32,128,256]{2,1,0:T(8,128)(2,1)} %gather_fusion, bf16[32,128,128]{2,1,0:T(8,128)(2,1)S(1)} %copy-done), kind=kOutput, calls=%fused_computation.45 | convolution fusion | flops 268435456 | bytes 7340032 | tf_op jit(solution)/shard_map/sij,sjf->sif/dot_general | solution.py:79
  69.0 5.5 %copy.16 = f32[32,256,128]{1,0,2:T(8,128)} copy(f32[32,256,128]{2,1,0:T(8,128)} %fusion.28) | data formatting | bytes 8388608 | tf_op jit(solution)/shard_map/sij,sjf->sif/dot_general | solution.py:79
  74.6 3.7 %fusion.2 = f32[4,128,256]{2,0,1:T(4,128)S(1)} fusion(f32[32,256,128]{1,0,2:T(8,128)} %copy.16, s32[32]{0:T(128)S(1)} %get-tuple-element.8), kind=kOutput, calls=%fused_computation.4 | convolution fusion | flops 50331776 | bytes 4718720 | tf_op jit(solution)/shard_map/rs,sif->rif/dot_general | solution.py:80
  78.2 0.0 copy-start.1
  78.2 0.1 copy.13
  78.4 1.0 fusion.8
  79.4 0.0 all-gather.5.cloned.1.call-update
  79.4 0.0 all-reduce.3.cloned.1.call-start
  79.5 1.1 convolution_bitcast_fusion.1
  80.6 15.8 %all-gather.5.cloned.1.call-done = bf16[512,1024]{1,0:T(8,128)(2,1)} async-done(((bf16[512,256]{1,0:T(8,128)(2,1)}), bf16[512,1024]{1,0:T(8,128)(2,1)}) %all-gather.5.cloned.1.call-update) | async-done | bytes 1048592 | tf_op jit(solution)/shard_map/all_gather | solution.py:69
  96.4 1.7 convolution_convert_fusion
  98.1 3.4 %collective-permute-start.2 = (bf16[512,256]{1,0:T(8,128)(2,1)S(1)}, bf16[512,256]{1,0:T(8,128)(2,1)S(1)}, u32[]{:S(2)}, u32[]{:S(2)}) collective-permute-start(bf16[512,256]{1,0:T(8,128)(2,1)S(1)} %convolution_convert_fusion), channel_id=1, source_target_pairs={{0,4},{4,8},{8,12},{12,16},{16,20},{20,24},{24,28},{1,5},{5,9},{9,... | collective-permute-start | bytes 786440 | tf_op jit(solution)/shard_map/ppermute | solution.py:15
  101.5 1.3 collective-permute-start.3
  102.8 1.2 convolution_bitcast_fusion
  103.9 0.0 all-reduce.3.cloned.1.call-update
  104.0 0.1 dynamic-slice.3
  104.1 11.0 %collective-permute-done.2 = bf16[512,256]{1,0:T(8,128)(2,1)S(1)} collective-permute-done((bf16[512,256]{1,0:T(8,128)(2,1)S(1)}, bf16[512,256]{1,0:T(8,128)(2,1)S(1)}, u32[]{:S(2)}, u32[]{:S(2)}) %collective-permute-start.2) | collective-permute-done | bytes 262176 | tf_op jit(solution)/shard_map/ppermute | solution.py:15
  115.1 1.0 pad_maximum_fusion.1
  116.1 2.0 gather_fusion.1
  118.1 4.3 %fusion.29 = f32[32,256,128]{2,1,0:T(8,128)} fusion(bf16[32,128,256]{2,1,0:T(8,128)(2,1)} %gather_fusion.1, bf16[32,128,128]{2,1,0:T(8,128)(2,1)S(1)} %copy-done), kind=kOutput, calls=%fused_computation.46 | convolution fusion | flops 268435456 | bytes 7340032 | tf_op jit(solution)/shard_map/sij,sjf->sif/dot_general | solution.py:79
  122.4 5.5 %copy.17 = f32[32,256,128]{1,0,2:T(8,128)} copy(f32[32,256,128]{2,1,0:T(8,128)} %fusion.29) | data formatting | bytes 8388608 | tf_op jit(solution)/shard_map/sij,sjf->sif/dot_general | solution.py:79
  127.9 3.6 %fusion = f32[4,128,256]{2,0,1:T(4,128)S(1)} fusion(f32[32,256,128]{1,0,2:T(8,128)} %copy.17, s32[32]{0:T(128)S(1)} %get-tuple-element.8), kind=kOutput, calls=%fused_computation.2 | convolution fusion | flops 50331776 | bytes 4718720 | tf_op jit(solution)/shard_map/rs,sif->rif/dot_general | solution.py:80
  131.6 0.1 copy.14
  131.7 52.5 %all-reduce.3.cloned.1.call-done = (f32[512,256]{0,1:T(8,128)}, f32[512,256]{0,1:T(8,128)}) async-done(((f32[512,256]{0,1:T(8,128)}, f32[512,256]{0,1:T(8,128)}), (f32[512,256]{0,1:T(8,128)}, f32[512,256]{0,1:T(8,128)})) %all-reduce.3.cloned.1.call-update) | async-done | bytes 1048592 | tf_op jit(solution)/shard_map/psum | solution.py:85
  184.2 1.1 multiply_maximum_fusion
  185.3 5.8 %all_gather.22 = bf16[64,1024]{0,1:T(8,128)(2,1)S(1)} all-gather(bf16[64,256]{0,1:T(8,128)(2,1)S(1)} %get-tuple-element.11), channel_id=1, replica_groups=mesh['rows'=8,'feat'=4] {'feat'}, dimensions={1}, use_global_device_ids=true | all-gather | bytes 163840 | tf_op jit(solution)/shard_map/all_gather | solution.py:70
  191.1 0.2 convolution_convert_fusion.2
  191.3 30.7 %all_gather.23 = bf16[512,256]{1,0:T(8,128)(2,1)S(1)} all-gather(bf16[64,256]{1,0:T(8,128)(2,1)S(1)} %convolution_convert_fusion.2), channel_id=1, replica_groups=mesh['rows'=8,'feat'=4] {'rows'}, dimensions={0}, use_global_device_ids=true | all-gather | bytes 294912 | tf_op jit(solution)/shard_map/all_gather | solution.py:76
  222.1 0.7 copy.15
  222.8 2.2 fusion.5
  (18 shorter events, 0.1 us)
Async XLA Ops:
  7.2 57.6 %copy-start = (bf16[32,128,128]{2,1,0:T(8,128)(2,1)S(1)}, bf16[32,128,128]{2,1,0:T(8,128)(2,1)}, u32[]{:S(2)}) copy-start(bf16[32,128,128]{2,1,0:T(8,128)(2,1)} %param.14) | copy-start | bytes 3145732
  7.2 42.2 %copy-start.2 = (bf16[2,1024,256]{2,1,0:T(8,128)(2,1)S(1)}, bf16[2,1024,256]{2,1,0:T(8,128)(2,1)}, u32[]{:S(2)}) copy-start(bf16[2,1024,256]{2,1,0:T(8,128)(2,1)} %param.12) | copy-start | bytes 3145732
  7.2 42.2 %copy-start.5 = (s32[32,3]{0,1:T(4,128)S(1)}, s32[32,3]{0,1:T(4,128)}, u32[]{:S(2)}) copy-start(s32[32,3]{0,1:T(4,128)} %param.13) | copy-start | bytes 1156
  7.2 48.5 %copy-start.3 = (s32[512]{0:T(512)S(1)}, s32[512]{0:T(512)}, u32[]{:S(2)}) copy-start(s32[512]{0:T(512)} %param.18) | copy-start | bytes 6148
  7.2 42.2 %all-gather.3.cloned.1.call-start = ((), (), s32[]{:S(2)}) async-start(), calls=%async_computation | async-start | bytes 1310720 | tf_op jit(solution)/shard_map/all_gather | solution.py:69
  9.2 87.2 %all-gather.5.cloned.1.call-start = ((), (), s32[]{:S(2)}) async-start(), calls=%async_computation.1 | async-start | bytes 1310720 | tf_op jit(solution)/shard_map/all_gather | solution.py:69
  51.1 7.2 %collective-permute-start = (bf16[512,256]{1,0:T(8,128)(2,1)S(1)}, bf16[512,256]{1,0:T(8,128)(2,1)S(1)}, u32[]{:S(2)}, u32[]{:S(2)}) collective-permute-start(bf16[512,256]{1,0:T(8,128)(2,1)S(1)} %convolution_convert_fusion.1), channel_id=1, source_target_pairs={{0,4},{4,8},{8,12},{12,16},{16,20},{20,24},{24,28},{1,5},{5,9},{9,... | collective-permute-start | bytes 786440 | tf_op jit(solution)/shard_map/ppermute | solution.py:15
  54.4 8.3 %collective-permute-start.1 = (bf16[512,256]{1,0:T(8,128)(2,1)S(1)}, bf16[512,256]{1,0:T(8,128)(2,1)S(1)}, u32[]{:S(2)}, u32[]{:S(2)}) collective-permute-start(bf16[512,256]{1,0:T(8,128)(2,1)S(1)} %convolution_convert_fusion.1), channel_id=1, source_target_pairs={{4,0},{8,4},{12,8},{16,12},{20,16},{24,20},{28,24},{5,1},{9,5},{13... | collective-permute-start | bytes 786440 | tf_op jit(solution)/shard_map/ppermute | solution.py:17
  74.5 3.8 %copy-start.6 = (bf16[512,512]{1,0:T(8,128)(2,1)S(1)}, bf16[512,512]{1,0:T(8,128)(2,1)}, u32[]{:S(2)}) copy-start(bf16[512,512]{1,0:T(8,128)(2,1)} %param.15) | copy-start | bytes 1572868
  74.5 3.8 %copy-start.7 = (s32[512]{0:T(512)S(1)}, s32[512]{0:T(512)}, u32[]{:S(2)}) copy-start(s32[512]{0:T(512)} %param.16) | copy-start | bytes 6148
  78.2 1.3 copy-start.1
  79.4 104.7 %all-reduce.3.cloned.1.call-start = ((), (), s32[]{:S(2)}) async-start(), calls=%async_computation.2 | async-start | bytes 2097152 | tf_op jit(solution)/shard_map/psum | solution.py:85
  80.6 23.3 %copy-start.4 = (s32[512]{0:T(512)S(1)}, s32[512]{0:T(512)}, u32[]{:S(2)}) copy-start(s32[512]{0:T(512)} %param.19) | copy-start | bytes 6148
  98.1 17.0 %collective-permute-start.2 = (bf16[512,256]{1,0:T(8,128)(2,1)S(1)}, bf16[512,256]{1,0:T(8,128)(2,1)S(1)}, u32[]{:S(2)}, u32[]{:S(2)}) collective-permute-start(bf16[512,256]{1,0:T(8,128)(2,1)S(1)} %convolution_convert_fusion), channel_id=1, source_target_pairs={{0,4},{4,8},{8,12},{12,16},{16,20},{20,24},{24,28},{1,5},{5,9},{9,... | collective-permute-start | bytes 786440 | tf_op jit(solution)/shard_map/ppermute | solution.py:15
  101.5 13.6 %collective-permute-start.3 = (bf16[512,256]{1,0:T(8,128)(2,1)S(1)}, bf16[512,256]{1,0:T(8,128)(2,1)}, u32[]{:S(2)}, u32[]{:S(2)}) collective-permute-start(bf16[512,256]{1,0:T(8,128)(2,1)S(1)} %convolution_convert_fusion), channel_id=1, source_target_pairs={{4,0},{8,4},{12,8},{16,12},{20,16},{24,20},{28,24},{5,1},{9,5},{13... | collective-permute-start | bytes 786440 | tf_op jit(solution)/shard_map/ppermute | solution.py:17
Sparse Core Ops, SparseCore 0:
  10.2 19.5 all-gather.2
  79.6 16.8 all-gather.4
  104.1 80.0 all-reduce.2
where the time goes:
time: 232 us
  waiting for transfers between devices  86.3 us (37%)
  blocking collectives  74.6 us (32%)
  matrix products  26.2 us (11%)
  local copies, waits for them, and re-layouts  16.1 us (7%)
  between operations  14 us (6%)
  starting transfers between devices  9.4 us (4%)
  other arithmetic  4.93 us (2%)
    all_gather x2, blocking collectives, body(): whole_head = lax.all_gather(head_x, 'rows', axis=0, tiled=True)  62.3 us
    psum x1, waiting for transfers between devices, body(): head_total = lax.psum(head_part, 'rows')  52.5 us
    all_gather x2, waiting for transfers between devices, body(): lax.all_gather(band_state.astype(jnp.bfloat16), 'feat', axis=1, tiled=True)  15.8 us
    ppermute x2, waiting for transfers between devices, extended(): lax.ppermute(tail, axis, [(i, (i + 1) % count) for i in range(ends)])  13.5 us
    all_gather x2, blocking collectives, body(): lax.all_gather(head_state.astype(jnp.bfloat16), 'feat', axis=1, tiled=True)  12.3 us
    dot_general x2, local copies, waits for them, and re-layouts, body(): jnp.einsum('sij,sjf->sif', tile_vals, picked, preferred_element_type=jnp....  11 us
    dot_general x2, matrix products, body(): jnp.einsum('sij,sjf->sif', tile_vals, picked, preferred_element_type=jnp....  8.59 us
    dot_general x2, matrix products, body(): jnp.einsum('rs,sif->rif', row_onehot, products, precision=lax.Precision.H...  7.29 us
  transfers between devices with their start and end apart: 7, of which 5 were waited for; matrix products, arithmetic and copies ran while one was open for 9% of the time, Pallas kernels for 0%

commit v1 on v0

v1 whole, which is shorter than its diff:
```python
import functools

import jax
import jax.numpy as jnp
from jax import lax
from jax.experimental import pallas as pl
from jax.experimental.pallas import tpu as pltpu
from jax.sharding import PartitionSpec as P

BF = jnp.bfloat16
F32 = jnp.float32
LIMIT = 28 * 1024 * 1024


def local(kernel, outs, scalars, args, scratch=(), flops=0):
    vmem = pl.BlockSpec(memory_space=pltpu.VMEM)
    smem = pl.BlockSpec(memory_space=pltpu.SMEM)
    moved = sum(a.size * a.dtype.itemsize for a in args)
    return pl.pallas_call(
        kernel,
        out_shape=[jax.ShapeDtypeStruct(s, d) for s, d in outs],
        in_specs=[smem] * len(scalars) + [vmem] * len(args),
        out_specs=[vmem] * len(outs),
        scratch_shapes=list(scratch),
        cost_estimate=pl.CostEstimate(flops=flops, bytes_accessed=moved, transcendentals=0),
        compiler_params=pltpu.CompilerParams(vmem_limit_bytes=LIMIT),
    )(*scalars, *args)


def mm(a, b):
    return jnp.dot(a, b, preferred_element_type=F32)


def swap(cells, axis, bit):
    count = lax.axis_size(axis)
    return lax.ppermute(cells, axis, [(i, i ^ bit) for i in range(count)])


def forward(cells):
    count = lax.axis_size("rows")
    pairs = []
    for i in range(count):
        if i % 2 == 0:
            pairs.append((i, i + 2 if i + 2 < count else i + 1))
        else:
            pairs.append((i, i - 2 if i > 1 else 0))
    return lax.ppermute(cells, "rows", pairs)


def spread(axis, cells, bits):
    pieces = {0: cells}
    for bit in bits:
        pieces.update({k | bit: swap(c, axis, bit) for k, c in list(pieces.items())})
    return pieces


def column(values, width):
    wide = jnp.broadcast_to(values.astype(F32), (128, values.shape[1]))
    tall = wide.T
    return jnp.concatenate([tall] * (width // 128), axis=1) if width > 128 else tall


def after(value, *others):
    return lax.optimization_barrier((value, *others))[0]


def split_partial(where, part, keep, send, head_dev):
    if not head_dev:
        keep[...] = part[...]
        return
    pair, parity = where[0] // 2, where[0] % 2
    for k in range(keep.shape[0] // head_dev):
        mine = pl.multiple_of((2 * (pair ^ k) + parity) * head_dev, head_dev)
        theirs = pl.multiple_of((2 * (pair ^ k) + 1 - parity) * head_dev, head_dev)
        keep[k * head_dev : (k + 1) * head_dev] = part[pl.ds(mine, head_dev)]
        send[k * head_dev : (k + 1) * head_dev] = part[pl.ds(theirs, head_dev)].astype(BF)


def begin_kernel(where, band, head, rows, out, head_out, keep, part, *, head_dev):
    size = band.shape[0]
    out[:size] = band[...].astype(BF)
    head_out[...] = head[...].astype(BF)
    part[...] = mm(rows[...], out[:size])
    split_partial(where, part, keep, out.at[size:] if head_dev else None, head_dev)


def dense_kernel(where, place, tiles, cols, reach, cells, near, pair, far, masked, own, window, *, blocks):
    tile = tiles.shape[1]
    rows = window.shape[0]
    tile_rows = rows // tile
    parity = where[0] % 2
    toward = 1 - 2 * parity
    inside = jnp.logical_and(where[0] != 0, where[0] != blocks - 1)
    window[...] = jnp.zeros_like(window)

    def add(s, carry):
        offset = place[s, 2]
        group = jnp.where(offset == 0, 0, jnp.where(offset == toward, 1, 2))

        @pl.when(jnp.logical_or(group != 2, inside))
        def _():
            r = pl.ds(pl.multiple_of(place[s, 0] * tile, tile), tile)
            c = pl.ds(pl.multiple_of((group * tile_rows + place[s, 1]) * tile, tile), tile)
            window[r, c] += tiles[s].astype(F32)

        return carry

    lax.fori_loop(0, tiles.shape[0], add, 0)
    near[...] = window[:, :rows].astype(BF)
    pair[...] = window[:, rows : 2 * rows].astype(BF)
    far[...] = window[:, 2 * rows :].astype(BF)
    limit = column(reach[...], 128)
    for g in range(cols.shape[1] // 128):
        here = slice(g * 128, (g + 1) * 128)
        lane = (lax.broadcasted_iota(jnp.int32, (rows, 128), 1) + g * 128).astype(F32)
        masked[:, here] = jnp.where(lane < limit, cols[:, here].astype(F32), 0.0).astype(BF)
    own[...] = mm(near[...], cells[:rows])


def near_kernel(near, cells, out):
    out[...] = mm(near[...], cells[: out.shape[0]])


def add_kernel(total, weight, cells, out):
    out[...] = total[...] + mm(weight[...], cells[: out.shape[0]])


def heads_kernel(where, total, masked, mine, theirs, out, heads, *, head_dev):
    whole_heads(where, mine, theirs, heads, head_dev)
    out[...] = total[...] + mm(masked[...], heads[...])


def fold_kernel(keep, arrived, onward, *outs):
    size = outs[0].shape[0]
    skip = onward.shape[0]
    onward[...] = arrived[:skip]
    for k, out in enumerate(outs):
        here = keep[k * size : (k + 1) * size]
        out[...] = (here + arrived[skip + k * size : skip + (k + 1) * size].astype(F32)).astype(out.dtype)


def join_kernel(*refs):
    size = refs[0].shape[0]
    for k, ref in enumerate(refs[:-1]):
        refs[-1][k * size : (k + 1) * size] = ref[...]


def whole_heads(where, mine, theirs, heads, head_dev):
    if not head_dev:
        heads[...] = mine[...]
        return
    pair, parity = where[0] // 2, where[0] % 2
    for k in range(mine.shape[0] // head_dev):
        here = slice(k * head_dev, (k + 1) * head_dev)
        a = pl.multiple_of((2 * (pair ^ k) + parity) * head_dev, head_dev)
        b = pl.multiple_of((2 * (pair ^ k) + 1 - parity) * head_dev, head_dev)
        heads[pl.ds(a, head_dev)] = mine[here]
        heads[pl.ds(b, head_dev)] = theirs[here]


def first_sum_kernel(total, far, other, *refs):
    parts, out = refs[:-1], refs[-1]
    rows = total.shape[0]
    out[:rows] = (total[...] + mm(far[...], other[...])).astype(BF)
    if parts:
        extra = parts[0][...]
        for part in parts[1:]:
            extra = extra + part[...].astype(F32)
        out[rows:] = extra.astype(BF)


def last_sum_kernel(total, far, other, scale, out):
    out[...] = jnp.maximum((total[...] + mm(far[...], other[...])) * scale[...], 0.0)


def mix_begin_kernel(where, *refs, order, early):
    pieces, shards, outs = refs[:early], refs[early : early + len(order)], refs[early + len(order) :]
    width = pieces[0].shape[1]
    for shard, out in zip(shards, outs):
        total = None
        for k, piece in zip(order, pieces):
            rows = pl.ds(pl.multiple_of((where[1] ^ k) * width, width), width)
            term = mm(piece[...], shard[rows])
            total = term if total is None else total + term
        out[...] = total


def mix_end_kernel(where, *refs, order, early, head_dev):
    count = len(order)
    late = count - early
    pieces, shards, begun = refs[:late], refs[late : late + count], refs[late + count : late + 2 * count]
    refs = refs[late + 2 * count :]
    if head_dev:
        weights, rows, degree, head_degree, out, keep, band_scale, head_out, part, scale, head_scale = refs
    else:
        weights, rows, degree, out, keep, band_scale, part, scale = refs
    band, width = band_scale.shape
    band_scale[...] = lax.rsqrt(column(degree[...], width))
    scale[:band] = band_scale[...]
    if head_dev:
        head_scale[...] = lax.rsqrt(column(head_degree[...], width))
        scale[band:] = head_scale[pl.ds(pl.multiple_of(where[0] * head_dev, head_dev), head_dev)]
    result = None
    for j, shard, total in zip(order, shards, begun):
        total = total[...]
        for k, piece in zip(order[early:], pieces):
            here = pl.ds(pl.multiple_of((where[1] ^ k) * width, width), width)
            total = total + mm(piece[...], shard[here])
        state = jnp.maximum(total * scale[...], 0.0).astype(BF)
        here = pl.ds(pl.multiple_of((where[1] ^ j) * width, width), width)
        term = mm(state, weights[1, here])
        result = term if result is None else result + term
    out[:band] = result[:band].astype(BF)
    if head_dev:
        head_out[...] = result[band:].astype(BF)
    part[...] = mm(rows[...], out[:band])
    split_partial(where, part, keep, out.at[band:] if head_dev else None, head_dev)


def head_out_kernel(where, own, *refs):
    arrived, (degree, out, scales) = refs[:-3], refs[-3:]
    total = own[...]
    for ref in arrived:
        total = total + ref[...].astype(F32)
    size = out.shape[0]
    scales[...] = lax.rsqrt(column(degree[...], out.shape[1]))
    out[...] = jnp.maximum(total * scales[pl.ds(pl.multiple_of(where[0] * size, size), size)], 0.0)


def body(
    band_feats,
    head_feats,
    mix_weights,
    tile_place,
    tile_vals,
    arrow_cols,
    arrow_reach,
    arrow_rows,
    band_degree,
    head_degree,
):
    rows_dev, width = band_feats.shape
    head_dev = head_feats.shape[0]
    heads = arrow_cols.shape[1]
    blocks = lax.axis_size("rows")
    pairs = blocks // 2
    top_bit = lax.axis_size("feat") // 2
    low_bits = [1 << n for n in reversed(range(top_bit.bit_length() - 1))]
    where = jnp.stack([lax.axis_index("rows"), lax.axis_index("feat")]).astype(jnp.int32)
    reach = arrow_reach[None, :]
    band_deg = band_degree[None, :]
    head_deg = head_degree[None, :]
    size = head_dev if pairs <= 4 and head_dev % 16 == 0 else 0
    part_rows = heads // 2 if size else heads
    part_scratch = pltpu.VMEM((heads, width), F32)
    head_scratch = pltpu.VMEM((heads, width), BF)
    band_sum = [((rows_dev, width), F32)]
    keep_shape = ((part_rows, width), F32)
    sent = ((rows_dev + (part_rows if size else 0), width), BF)
    heads_add = functools.partial(heads_kernel, head_dev=size)

    def z_pieces(parts):
        return [swap(parts[k], "rows", 2 * k) for k in range(1, pairs)]

    def gather_heads(own, before):
        if not size:
            everyone = lax.all_gather(own, "rows", axis=0, tiled=True)
            return everyone, everyone
        others = z_pieces([own] * pairs)
        (mine,) = local(join_kernel, [((part_rows, width), BF)], (), (after(own, before), *others))
        return mine, swap(mine, "rows", 1)

    def hand_on(keep, arrived, before):
        if not size:
            return forward(arrived), []
        keep = after(keep, before)
        outs = [((rows_dev, width), BF), ((size, width), F32)] + [((size, width), BF)] * (pairs - 1)
        onward, *parts = local(fold_kernel, outs, (), (keep, arrived))
        return forward(onward), [parts[0]] + z_pieces(parts)

    cells, head_cells, keep = local(
        functools.partial(begin_kernel, head_dev=size),
        [sent, ((head_dev, width), BF), keep_shape],
        (where,),
        (band_feats, head_feats, arrow_rows),
        [part_scratch],
    )
    first_part = keep
    pair_cells = swap(cells, "rows", 1)
    first = after(mix_weights, keep)[0]
    near, pair, far, masked, total = local(
        functools.partial(dense_kernel, blocks=blocks),
        [((rows_dev, rows_dev), BF)] * 3 + [((rows_dev, heads), BF), ((rows_dev, width), F32)],
        (where, tile_place),
        (tile_vals, arrow_cols, reach, cells),
        [pltpu.VMEM((rows_dev, 3 * rows_dev), F32)],
    )
    shards = spread("feat", first, [top_bit] + low_bits)
    mine, theirs = gather_heads(head_cells, total)
    far_cells, parts = hand_on(keep, pair_cells, mine)
    (total,) = local(add_kernel, band_sum, (), (after(total, *parts[:1]), pair, pair_cells))
    (total,) = local(heads_add, band_sum, (where,), (total, masked, mine, theirs), [head_scratch])
    (joined,) = local(
        first_sum_kernel, [((rows_dev + size, width), BF)], (), (total, far, far_cells, *parts)
    )

    near_pieces = spread("feat", joined, low_bits)
    opposite = swap(joined, "feat", top_bit)
    order = tuple(sorted(shards))
    weights = [shards[k] for k in order]
    early = len(near_pieces)
    begun = local(
        functools.partial(mix_begin_kernel, order=order, early=early),
        [((rows_dev + size, width), F32)] * len(order),
        (where,),
        (*[near_pieces[k] for k in order[:early]], *weights),
    )
    far_pieces = spread("feat", after(opposite, *begun), low_bits)
    degrees = (band_deg, head_deg) if size else (band_deg,)
    scratch = [part_scratch, pltpu.VMEM((rows_dev + size, width), F32)]
    cells, keep, scale, *head_x = local(
        functools.partial(mix_end_kernel, order=order, early=early, head_dev=size),
        [sent, keep_shape] + band_sum + ([((size, width), BF)] if size else []),
        (where,),
        (*[far_pieces[k ^ top_bit] for k in order[early:]], *weights, *begun, mix_weights, arrow_rows, *degrees),
        scratch + ([pltpu.VMEM((heads, width), F32)] if size else []),
    )
    if not size:
        own_scale = lax.dynamic_slice_in_dim(
            lax.rsqrt(head_degree.astype(F32)), lax.axis_index("rows") * head_dev, head_dev, 0
        )[:, None]
        summed = lax.psum_scatter(first_part, "rows", scatter_dimension=0, tiled=True).astype(BF)
        summed = lax.all_gather(summed, "feat", axis=1, tiled=True)
        full = lax.all_gather(mix_weights[0], "feat", axis=1, tiled=True)
        head_x = [mm(jnp.maximum(mm(summed, full) * own_scale, 0.0).astype(BF), mix_weights[1]).astype(BF)]

    pair_cells = swap(cells, "rows", 1)
    (total,) = local(near_kernel, band_sum, (), (near, cells))
    mine, theirs = gather_heads(head_x[0], total)
    far_cells, parts = hand_on(keep, pair_cells, mine)
    (total,) = local(add_kernel, band_sum, (), (after(total, *parts[:1]), pair, pair_cells))
    (total,) = local(heads_add, band_sum, (where,), (total, masked, mine, theirs), [head_scratch])
    (band_out,) = local(last_sum_kernel, band_sum, (), (total, far, far_cells, scale))
    if size:
        (head_out,) = local(
            head_out_kernel,
            [((head_dev, width), F32)],
            (where,),
            (*parts, head_deg),
            [pltpu.VMEM((heads, width), F32)],
        )
    else:
        head_out = jnp.maximum(lax.psum_scatter(keep, "rows", scatter_dimension=0, tiled=True) * own_scale, 0.0)
    return band_out, head_out


def solution(mesh):
    in_specs = (
        P("rows", "feat"),
        P("rows", "feat"),
        P(None, None, "feat"),
        P("rows", None),
        P("rows", None, None),
        P("rows", None),
        P("rows"),
        P(None, "rows"),
        P("rows"),
        P(),
    )
    out_specs = (P("rows", "feat"), P("rows", "feat"))
    return jax.shard_map(body, mesh=mesh, in_specs=in_specs, out_specs=out_specs, check_vma=False)
```

time: 232 us -> 76.4 us (0.33)
  blocking collectives: 74.6 us -> 0 us
  waiting for transfers between devices: 86.3 us -> 28.6 us
  matrix products: 26.2 us -> 0 us
  starting transfers between devices: 9.4 us -> 25.8 us
  Pallas kernels: 0 us -> 13.7 us
  between operations: 14 us -> 0.84 us
  local copies, waits for them, and re-layouts: 16.1 us -> 6.9 us
  other arithmetic: 4.93 us -> 0.08 us
    all_gather x4 -> x0, blocking collectives: 74.6 us -> none  [the longest x2 62.3 us: body(): whole_head = lax.all_gather(head_x, 'rows', axis=0, tiled=True)]
    psum x1 -> x0, waiting for transfers between devices: 52.5 us -> none  [body(): head_total = lax.psum(head_part, 'rows')]
    dot_general x12 -> x0, matrix products: 26.2 us -> none  [the longest x2 8.59 us: body(): jnp.einsum('sij,sjf->sif', tile_vals, picked, preferred_element_type=jnp....]
    ppermute x4 -> x24, starting transfers between devices: 9.28 us -> 25.8 us  [the longest x22 24 us: swap(): return lax.ppermute(cells, axis, [(i, i ^ bit) for i in range(count)])]
    all_gather x2 -> x0, waiting for transfers between devices: 15.8 us -> none  [body(): lax.all_gather(band_state.astype(jnp.bfloat16), 'feat', axis=1, tiled=True)]
    pallas_call x0 -> x16, Pallas kernels: none -> 13.7 us  [local(): pl.pallas_call(kernel, out_shape=[jax.ShapeDtypeStruct(s, d) for s, d in...]
    dot_general x4 -> x0, local copies, waits for them, and re-layouts: 11.2 us -> none  [the longest x2 11 us: body(): jnp.einsum('sij,sjf->sif', tile_vals, picked, preferred_element_type=jnp....]
    ppermute x4 -> x24, waiting for transfers between devices: 18 us -> 28.6 us  [the longest x22 28.6 us: swap(): return lax.ppermute(cells, axis, [(i, i ^ bit) for i in range(count)])]
  transfers between devices with their start and end apart: 7 -> 24, of which waited for: 5 -> 10; matrix products, arithmetic and copies ran while one was open for 9% -> 1% of each run, Pallas kernels for 0% -> 12%
where the time goes in v1:
time: 76.4 us; the launch traced here: 76 us
  waiting for transfers between devices  28.6 us (37%)
  starting transfers between devices  25.8 us (34%)
  Pallas kernels  13.7 us (18%)
  local copies, waits for them, and re-layouts  6.9 us (9%)
  between operations  0.84 us (1%)
    ppermute x22, waiting for transfers between devices, swap(): return lax.ppermute(cells, axis, [(i, i ^ bit) for i in range(count)])  28.6 us
    ppermute x22, starting transfers between devices, swap(): return lax.ppermute(cells, axis, [(i, i ^ bit) for i in range(count)])  24 us
    pallas_call x16, Pallas kernels, local(): pl.pallas_call(kernel, out_shape=[jax.ShapeDtypeStruct(s, d) for s, d in...  13.7 us
    unnamed x29, local copies, waits for them, and re-layouts  6.87 us
    ppermute x2, starting transfers between devices, forward(): return lax.ppermute(cells, 'rows', pairs)  1.82 us
  transfers between devices with their start and end apart: 24, of which 10 were waited for; matrix products, arithmetic and copies ran while one was open for 1% of the time, Pallas kernels for 12%

profile of v1, /device:TPU:0, one launch (start us, length us, event | category | flops | bytes accessed | tf_op | source)
XLA Modules:
  0.0 76.0 jit_solution(6403765753576732974)
XLA Ops:
  0.7 1.1 %copy-done.1 = bf16[512,512]{1,0:T(8,128)(2,1)S(1)} copy-done((bf16[512,512]{1,0:T(8,128)(2,1)S(1)}, bf16[512,512]{1,0:T(8,128)(2,1)}, u32[]{:S(2)}) %copy-start.1) | copy-done | bytes 524312
  1.8 1.0 %copy-done.5 = f32[512,256]{1,0:T(8,128)S(1)} copy-done((f32[512,256]{1,0:T(8,128)S(1)}, f32[512,256]{1,0:T(8,128)}, u32[]{:S(2)}) %copy-start.5) | copy-done | bytes 524312
  2.9 0.8 %copy-done.8 = f32[64,256]{1,0:T(8,128)S(1)} copy-done((f32[64,256]{1,0:T(8,128)S(1)}, f32[64,256]{1,0:T(8,128)}, u32[]{:S(2)}) %copy-start.8) | copy-done | bytes 65560
  3.7 1.6 %shard_map.113 = (bf16[768,256]{1,0:T(8,128)(2,1)}, bf16[64,256]{1,0:T(8,128)(2,1)}, f32[256,256]{1,0:T(8,128)S(1)}) custom-call(s32[2]{0:T(128)S(1)} %pad_add_fusion.where, f32[512,256]{1,0:T(8,128)S(1)} %copy-done.5, f32[64,256]{1,0:T(8,128)S(1)} %copy-done.8, bf16[512,512]{1,0:T(8,128)(2,1)S(1)} %copy-done.1), custom_call_target="tpu_custom_call" | custom-call | bytes 1114112 | tf_op jit(solution)/shard_map/pallas_call | solution.py:19
  5.3 0.7 copy-done.6
  6.1 3.0 %collective-permute-start.12 = (bf16[1024,256]{1,0:T(8,128)(2,1)S(1)}, bf16[1024,256]{1,0:T(8,128)(2,1)S(1)}, u32[]{:S(2)}, u32[]{:S(2)}) collective-permute-start(bf16[1024,256]{1,0:T(8,128)(2,1)S(1)} %slice_bitcast_fusion.refs_2_), channel_id=1, source_target_pairs={{0,2},{1,3},{2,0},{3,1},{4,6},{5,7},{6,4},{7,5},{8,10},{9,11},{10,... | collective-permute-start | bytes 1572872 | tf_op jit(solution)/shard_map/ppermute | solution.py:36
  9.1 1.5 %collective-permute-start.3 = (bf16[768,256]{1,0:T(8,128)(2,1)}, bf16[768,256]{1,0:T(8,128)(2,1)S(1)}, u32[]{:S(2)}, u32[]{:S(2)}) collective-permute-start(bf16[768,256]{1,0:T(8,128)(2,1)} %get-tuple-element.36.cells), channel_id=1, source_target_pairs={{0,4},{4,0},{8,12},{12,8},{16,20},{20,16},{24,28},{28,24},{1,5},{5... | collective-permute-start | bytes 1179656 | tf_op jit(solution)/shard_map/ppermute | solution.py:36
  10.6 3.6 %collective-permute-start.2 = (bf16[64,256]{1,0:T(8,128)(2,1)}, bf16[64,256]{1,0:T(8,128)(2,1)}, u32[]{:S(2)}, u32[]{:S(2)}) collective-permute-start(bf16[64,256]{1,0:T(8,128)(2,1)} %get-tuple-element.41.refs_0_), channel_id=1, source_target_pairs={{0,24},{4,28},{8,16},{12,20},{16,8},{20,12},{24,0},{28,4},{1,25},{... | collective-permute-start | bytes 98312 | tf_op jit(solution)/shard_map/ppermute | solution.py:36
  14.2 0.8 %collective-permute-start = (bf16[64,256]{1,0:T(8,128)(2,1)}, bf16[64,256]{1,0:T(8,128)(2,1)}, u32[]{:S(2)}, u32[]{:S(2)}) collective-permute-start(bf16[64,256]{1,0:T(8,128)(2,1)} %get-tuple-element.41.refs_0_), channel_id=1, source_target_pairs={{0,8},{4,12},{8,0},{12,4},{16,24},{20,28},{24,16},{28,20},{1,9},{5... | collective-permute-start | bytes 98312 | tf_op jit(solution)/shard_map/ppermute | solution.py:36
  15.0 0.8 %copy.12.place = s32[32,3]{1,0:T(8,128)S(1)} copy(s32[32,3]{0,1:T(4,128)} %param.13) | data formatting | bytes 768 | tf_op args[3]
  15.8 0.6 copy-done.10
  16.4 1.0 %copy-done.4 = bf16[512,512]{1,0:T(8,128)(2,1)S(1)} copy-done((bf16[512,512]{1,0:T(8,128)(2,1)S(1)}, bf16[512,512]{1,0:T(8,128)(2,1)}, u32[]{:S(2)}) %copy-start.4) | copy-done | bytes 524312
  17.4 0.7 copy-done.12
  18.1 2.4 %shard_map.114 = (bf16[512,512]{1,0:T(8,128)(2,1)S(1)}, bf16[512,512]{1,0:T(8,128)(2,1)S(1)}, bf16[512,512]{1,0:T(8,128)(2,1)S(1)}, bf16[512,512]{1,0:T(8,128)(2,1)S(1)}, f32[512,256]{1,0:T(8,128)S(1)}) custom-call(s32[2]{0:T(128)S(1)} %copy-done.10, s32[32,3]{1,0:T(8,128)S(1)} %copy.12.place, bf16[32,128,128]{2,1,0:T(8,128)(2,1)S(1)} %copy-done.3, ...), custom_call_target="tpu_custom_call" | custom-call | bytes 1968128 | tf_op jit(solution)/shard_map/pallas_call | solution.py:19
  20.6 0.9 %shard_map.115.mine = bf16[256,256]{1,0:T(8,128)(2,1)S(1)} custom-call(bf16[64,256]{1,0:T(8,128)(2,1)} %get-tuple-element.41.refs_0_, bf16[64,256]{1,0:T(8,128)(2,1)} %collective-permute-done.refs_1_, bf16[64,256]{1,0:T(8,128)(2,1)} %collective-permute-done.1.refs_2_, bf16[64,256]{1,0:T(8,128)(2,1)} %collective-permute-done.2.refs_3_), custom_call_target="tpu_custom_call" | custom-call | bytes 131072 | tf_op jit(solution)/shard_map/pallas_call | solution.py:19
  21.5 1.5 %collective-permute-start.5 = (bf16[512,256]{1,0:T(8,128)(2,1)S(1)}, bf16[512,256]{1,0:T(8,128)(2,1)S(1)}, u32[]{:S(2)}, u32[]{:S(2)}) collective-permute-start(bf16[512,256]{1,0:T(8,128)(2,1)S(1)} %get-tuple-element.48), channel_id=1, source_target_pairs={{0,8},{4,0},{8,16},{12,4},{16,24},{20,12},{24,28},{28,20},{1,9},{5... | collective-permute-start | bytes 786440 | tf_op jit(solution)/shard_map/ppermute | solution.py:47
  23.0 0.5 collective-permute-start.13
  23.5 0.6 collective-permute-start.4
  24.1 0.8 %collective-permute-start.6 = (bf16[64,256]{1,0:T(8,128)(2,1)S(1)}, bf16[64,256]{1,0:T(8,128)(2,1)S(1)}, u32[]{:S(2)}, u32[]{:S(2)}) collective-permute-start(bf16[64,256]{1,0:T(8,128)(2,1)S(1)} %get-tuple-element.49), channel_id=1, source_target_pairs={{0,8},{4,12},{8,0},{12,4},{16,24},{20,28},{24,16},{28,20},{1,9},{5... | collective-permute-start | bytes 98312 | tf_op jit(solution)/shard_map/ppermute | solution.py:36
  25.0 6.1 %collective-permute-done.4.theirs = bf16[256,256]{1,0:T(8,128)(2,1)S(1)} collective-permute-done((bf16[256,256]{1,0:T(8,128)(2,1)S(1)}, bf16[256,256]{1,0:T(8,128)(2,1)S(1)}, u32[]{:S(2)}, u32[]{:S(2)}) %collective-permute-start.4) | collective-permute-done | bytes 131104 | tf_op jit(solution)/shard_map/ppermute | solution.py:36
  31.1 0.7 collective-permute-start.7
  31.8 0.9 %collective-permute-start.8 = (bf16[64,256]{1,0:T(8,128)(2,1)S(1)}, bf16[64,256]{1,0:T(8,128)(2,1)S(1)}, u32[]{:S(2)}, u32[]{:S(2)}) collective-permute-start(bf16[64,256]{1,0:T(8,128)(2,1)S(1)} %get-tuple-element.51), channel_id=1, source_target_pairs={{0,24},{4,28},{8,16},{12,20},{16,8},{20,12},{24,0},{28,4},{1,25},{... | collective-permute-start | bytes 98312 | tf_op jit(solution)/shard_map/ppermute | solution.py:36
  32.8 0.3 shard_map.117.total
  33.1 0.9 %shard_map.118.total = f32[512,256]{1,0:T(8,128)S(1)} custom-call(s32[2]{0:T(128)S(1)} %copy-done.10, f32[512,256]{1,0:T(8,128)S(1)} %shard_map.117.total, bf16[512,512]{1,0:T(8,128)(2,1)S(1)} %get-tuple-element.46.masked, bf16[256,256]{1,0:T(8,128)(2,1)S(1)} %shard_map.115.mine, bf16[256,256]{1,0:T(8,128)(2,1)S(1)} %collective-permute-done.4.theirs), custom_call_target="tpu_custom_call" | custom-call | bytes 1310720 | tf_op jit(solution)/shard_map/pallas_call | solution.py:19
  33.9 2.0 %collective-permute-done.7.refs_2_ = bf16[64,256]{1,0:T(8,128)(2,1)S(1)} collective-permute-done((bf16[64,256]{1,0:T(8,128)(2,1)S(1)}, bf16[64,256]{1,0:T(8,128)(2,1)S(1)}, u32[]{:S(2)}, u32[]{:S(2)}) %collective-permute-start.7) | collective-permute-done | bytes 32800 | tf_op jit(solution)/shard_map/ppermute | solution.py:36
  35.9 1.6 %collective-permute-done.8.refs_3_ = bf16[64,256]{1,0:T(8,128)(2,1)S(1)} collective-permute-done((bf16[64,256]{1,0:T(8,128)(2,1)S(1)}, bf16[64,256]{1,0:T(8,128)(2,1)S(1)}, u32[]{:S(2)}, u32[]{:S(2)}) %collective-permute-start.8) | collective-permute-done | bytes 32800 | tf_op jit(solution)/shard_map/ppermute | solution.py:36
  37.6 0.3 shard_map.119.refs_0_
  38.0 0.6 collective-permute-start.9
  38.5 1.0 %collective-permute-done.10.refs_1_ = bf16[576,256]{1,0:T(8,128)(2,1)S(1)} collective-permute-done((bf16[576,256]{1,0:T(8,128)(2,1)S(1)}, bf16[576,256]{1,0:T(8,128)(2,1)S(1)}, u32[]{:S(2)}, u32[]{:S(2)}) %collective-permute-start.10) | collective-permute-done | bytes 294944 | tf_op jit(solution)/shard_map/ppermute | solution.py:36
  39.5 1.3 %shard_map.120 = (f32[576,256]{1,0:T(8,128)S(1)}, f32[576,256]{1,0:T(8,128)S(1)}, f32[576,256]{1,0:T(8,128)S(1)}, f32[576,256]{1,0:T(8,128)S(1)}) custom-call(s32[2]{0:T(128)S(1)} %copy-done.10, bf16[576,256]{1,0:T(8,128)(2,1)S(1)} %shard_map.119.refs_0_, bf16[576,256]{1,0:T(8,128)(2,1)S(1)} %collective-permute-done.10.refs_1_, ...), custom_call_target="tpu_custom_call" | custom-call | bytes 2686976 | tf_op jit(solution)/shard_map/pallas_call | solution.py:19
  40.9 6.5 %collective-permute-done.9.refs_0_ = bf16[576,256]{1,0:T(8,128)(2,1)S(1)} collective-permute-done((bf16[576,256]{1,0:T(8,128)(2,1)S(1)}, bf16[576,256]{1,0:T(8,128)(2,1)S(1)}, u32[]{:S(2)}, u32[]{:S(2)}) %collective-permute-start.9) | collective-permute-done | bytes 294944 | tf_op jit(solution)/shard_map/ppermute | solution.py:36
  47.4 1.6 %collective-permute-done.14.refs_1_ = bf16[576,256]{1,0:T(8,128)(2,1)S(1)} collective-permute-done((bf16[576,256]{1,0:T(8,128)(2,1)S(1)}, bf16[576,256]{1,0:T(8,128)(2,1)S(1)}, u32[]{:S(2)}, u32[]{:S(2)}) %collective-permute-start.14) | collective-permute-done | bytes 294944 | tf_op jit(solution)/shard_map/ppermute | solution.py:36
  49.0 2.1 %shard_map.121 = (bf16[768,256]{1,0:T(8,128)(2,1)S(1)}, f32[256,256]{1,0:T(8,128)S(1)}, f32[512,256]{1,0:T(8,128)S(1)}, bf16[64,256]{1,0:T(8,128)(2,1)S(1)}) custom-call(s32[2]{0:T(128)S(1)} %copy-done.10, bf16[576,256]{1,0:T(8,128)(2,1)S(1)} %collective-permute-done.9.refs_0_, bf16[576,256]{1,0:T(8,128)(2,1)S(1)} %collective-permute-done.14.refs_1_, ...), custom_call_target="tpu_custom_call" | custom-call | bytes 6623232 | tf_op jit(solution)/shard_map/pallas_call | solution.py:19
  51.1 0.3 collective-permute-start.18
  51.4 3.0 %collective-permute-start.17 = (bf16[64,256]{1,0:T(8,128)(2,1)S(1)}, bf16[64,256]{1,0:T(8,128)(2,1)S(1)}, u32[]{:S(2)}, u32[]{:S(2)}) collective-permute-start(bf16[64,256]{1,0:T(8,128)(2,1)S(1)} %get-tuple-element.61.refs_0_), channel_id=1, source_target_pairs={{0,24},{4,28},{8,16},{12,20},{16,8},{20,12},{24,0},{28,4},{1,25},{... | collective-permute-start | bytes 98312 | tf_op jit(solution)/shard_map/ppermute | solution.py:36
  54.7 1.1 %collective-permute-start.15 = (bf16[64,256]{1,0:T(8,128)(2,1)S(1)}, bf16[64,256]{1,0:T(8,128)(2,1)S(1)}, u32[]{:S(2)}, u32[]{:S(2)}) collective-permute-start(bf16[64,256]{1,0:T(8,128)(2,1)S(1)} %get-tuple-element.61.refs_0_), channel_id=1, source_target_pairs={{0,8},{4,12},{8,0},{12,4},{16,24},{20,28},{24,16},{28,20},{1,9},{5... | collective-permute-start | bytes 98312 | tf_op jit(solution)/shard_map/ppermute | solution.py:36
  55.8 0.3 shard_map.122.total
  56.1 1.1 %collective-permute-done.17.refs_3_ = bf16[64,256]{1,0:T(8,128)(2,1)S(1)} collective-permute-done((bf16[64,256]{1,0:T(8,128)(2,1)S(1)}, bf16[64,256]{1,0:T(8,128)(2,1)S(1)}, u32[]{:S(2)}, u32[]{:S(2)}) %collective-permute-start.17) | collective-permute-done | bytes 32800 | tf_op jit(solution)/shard_map/ppermute | solution.py:36
  57.2 2.0 %collective-permute-done.16.refs_2_ = bf16[64,256]{1,0:T(8,128)(2,1)S(1)} collective-permute-done((bf16[64,256]{1,0:T(8,128)(2,1)S(1)}, bf16[64,256]{1,0:T(8,128)(2,1)S(1)}, u32[]{:S(2)}, u32[]{:S(2)}) %collective-permute-start.16) | collective-permute-done | bytes 32800 | tf_op jit(solution)/shard_map/ppermute | solution.py:36
  59.3 3.0 %collective-permute-done.18.arrived.cells = bf16[768,256]{1,0:T(8,128)(2,1)S(1)} collective-permute-done((bf16[768,256]{1,0:T(8,128)(2,1)S(1)}, bf16[768,256]{1,0:T(8,128)(2,1)S(1)}, u32[]{:S(2)}, u32[]{:S(2)}) %collective-permute-start.18) | collective-permute-done | bytes 393248 | tf_op jit(solution)/shard_map/ppermute | solution.py:36
  62.3 0.4 collective-permute-start.20
  62.7 1.7 %collective-permute-start.19 = (bf16[256,256]{1,0:T(8,128)(2,1)S(1)}, bf16[256,256]{1,0:T(8,128)(2,1)S(1)}, u32[]{:S(2)}, u32[]{:S(2)}) collective-permute-start(bf16[256,256]{1,0:T(8,128)(2,1)S(1)} %shard_map.123.mine), channel_id=1, source_target_pairs={{0,4},{4,0},{8,12},{12,8},{16,20},{20,16},{24,28},{28,24},{1,5},{5... | collective-permute-start | bytes 393224 | tf_op jit(solution)/shard_map/ppermute | solution.py:36
  64.7 1.6 %collective-permute-start.22 = (bf16[64,256]{1,0:T(8,128)(2,1)S(1)}, bf16[64,256]{1,0:T(8,128)(2,1)S(1)}, u32[]{:S(2)}, u32[]{:S(2)}) collective-permute-start(bf16[64,256]{1,0:T(8,128)(2,1)S(1)} %get-tuple-element.68), channel_id=1, source_target_pairs={{0,16},{4,20},{8,24},{12,28},{16,0},{20,4},{24,8},{28,12},{1,17},{... | collective-permute-start | bytes 98312 | tf_op jit(solution)/shard_map/ppermute | solution.py:36
  66.3 2.5 %collective-permute-start.23 = (bf16[64,256]{1,0:T(8,128)(2,1)S(1)}, bf16[64,256]{1,0:T(8,128)(2,1)S(1)}, u32[]{:S(2)}, u32[]{:S(2)}) collective-permute-start(bf16[64,256]{1,0:T(8,128)(2,1)S(1)} %get-tuple-element.69), channel_id=1, source_target_pairs={{0,24},{4,28},{8,16},{12,20},{16,8},{20,12},{24,0},{28,4},{1,25},{... | collective-permute-start | bytes 98312 | tf_op jit(solution)/shard_map/ppermute | solution.py:36
  69.1 3.6 %collective-permute-done.19.theirs = bf16[256,256]{1,0:T(8,128)(2,1)S(1)} collective-permute-done((bf16[256,256]{1,0:T(8,128)(2,1)S(1)}, bf16[256,256]{1,0:T(8,128)(2,1)S(1)}, u32[]{:S(2)}, u32[]{:S(2)}) %collective-permute-start.19) | collective-permute-done | bytes 131104 | tf_op jit(solution)/shard_map/ppermute | solution.py:36
  72.7 0.9 %shard_map.126.total = f32[512,256]{1,0:T(8,128)S(1)} custom-call(s32[2]{0:T(128)S(1)} %copy-done.10, f32[512,256]{1,0:T(8,128)S(1)} %shard_map.125.total, bf16[512,512]{1,0:T(8,128)(2,1)S(1)} %get-tuple-element.46.masked, bf16[256,256]{1,0:T(8,128)(2,1)S(1)} %shard_map.123.mine, bf16[256,256]{1,0:T(8,128)(2,1)S(1)} %collective-permute-done.19.theirs), custom_call_target="tpu_custom_call" | custom-call | bytes 1310720 | tf_op jit(solution)/shard_map/pallas_call | solution.py:19
  73.6 1.3 %shard_map.128 = f32[64,256]{1,0:T(8,128)} custom-call(s32[2]{0:T(128)S(1)} %copy-done.10, f32[64,256]{1,0:T(8,128)S(1)} %get-tuple-element.63.own, bf16[64,256]{1,0:T(8,128)(2,1)S(1)} %collective-permute-done.21.refs_0_, bf16[64,256]{1,0:T(8,128)(2,1)S(1)} %collective-permute-done.22.refs_1_, bf16[64,256]{1,0:T(8,128)(2,1)S(1)} %collective-permute-done.23.refs_2_, ...), custom_call_target="tpu_custom_call" | custom-call | bytes 165888 | tf_op jit(solution)/shard_map/pallas_call | solution.py:19
  74.9 1.1 %shard_map.127 = f32[512,256]{1,0:T(8,128)} custom-call(f32[512,256]{1,0:T(8,128)S(1)} %shard_map.126.total, bf16[512,512]{1,0:T(8,128)(2,1)S(1)} %get-tuple-element.47.far, bf16[512,256]{1,0:T(8,128)(2,1)S(1)} %collective-permute-done.20.other, f32[512,256]{1,0:T(8,128)S(1)} %get-tuple-element.66.scale), custom_call_target="tpu_custom_call" | custom-call | bytes 1835008 | tf_op jit(solution)/shard_map/pallas_call | solution.py:19
  (47 shorter events, 1.2 us)
Async XLA Ops:
  0.6 5.4 %copy-start = (bf16[2,1024,256]{2,1,0:T(8,128)(2,1)S(1)}, bf16[2,1024,256]{2,1,0:T(8,128)(2,1)}, u32[]{:S(2)}) copy-start(bf16[2,1024,256]{2,1,0:T(8,128)(2,1)} %refs_10_.1) | copy-start | bytes 3145732
  0.7 1.1 %copy-start.1 = (bf16[512,512]{1,0:T(8,128)(2,1)S(1)}, bf16[512,512]{1,0:T(8,128)(2,1)}, u32[]{:S(2)}) copy-start(bf16[512,512]{1,0:T(8,128)(2,1)} %refs_11_.1) | copy-start | bytes 1572868
  1.8 1.0 %copy-start.5 = (f32[512,256]{1,0:T(8,128)S(1)}, f32[512,256]{1,0:T(8,128)}, u32[]{:S(2)}) copy-start(f32[512,256]{1,0:T(8,128)} %band.1) | copy-start | bytes 1572868
  2.9 0.8 %copy-start.8 = (f32[64,256]{1,0:T(8,128)S(1)}, f32[64,256]{1,0:T(8,128)}, u32[]{:S(2)}) copy-start(f32[64,256]{1,0:T(8,128)} %head.1) | copy-start | bytes 196612
  3.7 1.6 %copy-start.9 = (s32[2]{0:T(128)}, s32[2]{0:T(128)S(1)}, u32[]{:S(2)}) copy-start(s32[2]{0:T(128)S(1)} %pad_add_fusion.where) | copy-start | bytes 28
  3.7 12.0 %copy-start.3 = (bf16[32,128,128]{2,1,0:T(8,128)(2,1)S(1)}, bf16[32,128,128]{2,1,0:T(8,128)(2,1)}, u32[]{:S(2)}) copy-start(bf16[32,128,128]{2,1,0:T(8,128)(2,1)} %tiles.1) | copy-start | bytes 3145732
  5.3 0.7 copy-start.6
  6.1 16.9 %collective-permute-start.12 = (bf16[1024,256]{1,0:T(8,128)(2,1)S(1)}, bf16[1024,256]{1,0:T(8,128)(2,1)S(1)}, u32[]{:S(2)}, u32[]{:S(2)}) collective-permute-start(bf16[1024,256]{1,0:T(8,128)(2,1)S(1)} %slice_bitcast_fusion.refs_2_), channel_id=1, source_target_pairs={{0,2},{1,3},{2,0},{3,1},{4,6},{5,7},{6,4},{7,5},{8,10},{9,11},{10,... | collective-permute-start | bytes 1572872 | tf_op jit(solution)/shard_map/ppermute | solution.py:36
  9.1 12.3 %collective-permute-start.3 = (bf16[768,256]{1,0:T(8,128)(2,1)}, bf16[768,256]{1,0:T(8,128)(2,1)S(1)}, u32[]{:S(2)}, u32[]{:S(2)}) collective-permute-start(bf16[768,256]{1,0:T(8,128)(2,1)} %get-tuple-element.36.cells), channel_id=1, source_target_pairs={{0,4},{4,0},{8,12},{12,8},{16,20},{20,16},{24,28},{28,24},{1,5},{5... | collective-permute-start | bytes 1179656 | tf_op jit(solution)/shard_map/ppermute | solution.py:36
  10.6 9.9 %collective-permute-start.2 = (bf16[64,256]{1,0:T(8,128)(2,1)}, bf16[64,256]{1,0:T(8,128)(2,1)}, u32[]{:S(2)}, u32[]{:S(2)}) collective-permute-start(bf16[64,256]{1,0:T(8,128)(2,1)} %get-tuple-element.41.refs_0_), channel_id=1, source_target_pairs={{0,24},{4,28},{8,16},{12,20},{16,8},{20,12},{24,0},{28,4},{1,25},{... | collective-permute-start | bytes 98312 | tf_op jit(solution)/shard_map/ppermute | solution.py:36
  14.2 6.4 %collective-permute-start.1 = (bf16[64,256]{1,0:T(8,128)(2,1)}, bf16[64,256]{1,0:T(8,128)(2,1)}, u32[]{:S(2)}, u32[]{:S(2)}) collective-permute-start(bf16[64,256]{1,0:T(8,128)(2,1)} %get-tuple-element.41.refs_0_), channel_id=1, source_target_pairs={{0,16},{4,20},{8,24},{12,28},{16,0},{20,4},{24,8},{28,12},{1,17},{... | collective-permute-start | bytes 98312 | tf_op jit(solution)/shard_map/ppermute | solution.py:36
  14.2 6.4 %collective-permute-start = (bf16[64,256]{1,0:T(8,128)(2,1)}, bf16[64,256]{1,0:T(8,128)(2,1)}, u32[]{:S(2)}, u32[]{:S(2)}) collective-permute-start(bf16[64,256]{1,0:T(8,128)(2,1)} %get-tuple-element.41.refs_0_), channel_id=1, source_target_pairs={{0,8},{4,12},{8,0},{12,4},{16,24},{20,28},{24,16},{28,20},{1,9},{5... | collective-permute-start | bytes 98312 | tf_op jit(solution)/shard_map/ppermute | solution.py:36
  15.8 0.6 copy-start.10
  16.4 1.0 %copy-start.4 = (bf16[512,512]{1,0:T(8,128)(2,1)S(1)}, bf16[512,512]{1,0:T(8,128)(2,1)}, u32[]{:S(2)}) copy-start(bf16[512,512]{1,0:T(8,128)(2,1)} %cols.1) | copy-start | bytes 1572868
  17.4 0.7 copy-start.12
  20.5 1.0 %copy-start.7 = (f32[256,256]{1,0:T(8,128)S(1)}, f32[256,256]{1,0:T(8,128)}, u32[]{:S(2)}) copy-start(f32[256,256]{1,0:T(8,128)} %copy-done.6) | copy-start | bytes 786436
  21.5 16.0 %collective-permute-start.5 = (bf16[512,256]{1,0:T(8,128)(2,1)S(1)}, bf16[512,256]{1,0:T(8,128)(2,1)S(1)}, u32[]{:S(2)}, u32[]{:S(2)}) collective-permute-start(bf16[512,256]{1,0:T(8,128)(2,1)S(1)} %get-tuple-element.48), channel_id=1, source_target_pairs={{0,8},{4,0},{8,16},{12,4},{16,24},{20,12},{24,28},{28,20},{1,9},{5... | collective-permute-start | bytes 786440 | tf_op jit(solution)/shard_map/ppermute | solution.py:47
  23.0 15.5 %collective-permute-start.11 = (bf16[1024,256]{1,0:T(8,128)(2,1)S(1)}, bf16[1024,256]{1,0:T(8,128)(2,1)S(1)}, u32[]{:S(2)}, u32[]{:S(2)}) collective-permute-start(bf16[1024,256]{1,0:T(8,128)(2,1)S(1)} %slice_bitcast_fusion.refs_2_), channel_id=1, source_target_pairs={{0,1},{1,0},{2,3},{3,2},{4,5},{5,4},{6,7},{7,6},{8,9},{9,8},{10,11... | collective-permute-start | bytes 1572872 | tf_op jit(solution)/shard_map/ppermute | solution.py:36
  23.0 16.5 %collective-permute-start.13 = (bf16[1024,256]{1,0:T(8,128)(2,1)S(1)}, bf16[1024,256]{1,0:T(8,128)(2,1)S(1)}, u32[]{:S(2)}, u32[]{:S(2)}) collective-permute-start(bf16[1024,256]{1,0:T(8,128)(2,1)S(1)} %collective-permute-done.12.refs_4_), channel_id=1, source_target_pairs={{0,1},{1,0},{2,3},{3,2},{4,5},{5,4},{6,7},{7,6},{8,9},{9,8},{10,11... | collective-permute-start | bytes 1572872 | tf_op jit(solution)/shard_map/ppermute | solution.py:36
  23.5 7.6 %collective-permute-start.4 = (bf16[256,256]{1,0:T(8,128)(2,1)S(1)}, bf16[256,256]{1,0:T(8,128)(2,1)S(1)}, u32[]{:S(2)}, u32[]{:S(2)}) collective-permute-start(bf16[256,256]{1,0:T(8,128)(2,1)S(1)} %shard_map.115.mine), channel_id=1, source_target_pairs={{0,4},{4,0},{8,12},{12,8},{16,20},{20,16},{24,28},{28,24},{1,5},{5... | collective-permute-start | bytes 393224 | tf_op jit(solution)/shard_map/ppermute | solution.py:36
  24.1 7.7 %collective-permute-start.6 = (bf16[64,256]{1,0:T(8,128)(2,1)S(1)}, bf16[64,256]{1,0:T(8,128)(2,1)S(1)}, u32[]{:S(2)}, u32[]{:S(2)}) collective-permute-start(bf16[64,256]{1,0:T(8,128)(2,1)S(1)} %get-tuple-element.49), channel_id=1, source_target_pairs={{0,8},{4,12},{8,0},{12,4},{16,24},{20,28},{24,16},{28,20},{1,9},{5... | collective-permute-start | bytes 98312 | tf_op jit(solution)/shard_map/ppermute | solution.py:36
  31.1 4.8 %collective-permute-start.7 = (bf16[64,256]{1,0:T(8,128)(2,1)S(1)}, bf16[64,256]{1,0:T(8,128)(2,1)S(1)}, u32[]{:S(2)}, u32[]{:S(2)}) collective-permute-start(bf16[64,256]{1,0:T(8,128)(2,1)S(1)} %get-tuple-element.50), channel_id=1, source_target_pairs={{0,16},{4,20},{8,24},{12,28},{16,0},{20,4},{24,8},{28,12},{1,17},{... | collective-permute-start | bytes 98312 | tf_op jit(solution)/shard_map/ppermute | solution.py:36
  31.8 5.7 %collective-permute-start.8 = (bf16[64,256]{1,0:T(8,128)(2,1)S(1)}, bf16[64,256]{1,0:T(8,128)(2,1)S(1)}, u32[]{:S(2)}, u32[]{:S(2)}) collective-permute-start(bf16[64,256]{1,0:T(8,128)(2,1)S(1)} %get-tuple-element.51), channel_id=1, source_target_pairs={{0,24},{4,28},{8,16},{12,20},{16,8},{20,12},{24,0},{28,4},{1,25},{... | collective-permute-start | bytes 98312 | tf_op jit(solution)/shard_map/ppermute | solution.py:36
  37.9 11.1 %copy-start.2 = (bf16[512,512]{1,0:T(8,128)(2,1)S(1)}, bf16[512,512]{1,0:T(8,128)(2,1)}, u32[]{:S(2)}) copy-start(bf16[512,512]{1,0:T(8,128)(2,1)} %refs_11_.1) | copy-start | bytes 1572868
  37.9 1.6 %collective-permute-start.10 = (bf16[576,256]{1,0:T(8,128)(2,1)S(1)}, bf16[576,256]{1,0:T(8,128)(2,1)S(1)}, u32[]{:S(2)}, u32[]{:S(2)}) collective-permute-start(bf16[576,256]{1,0:T(8,128)(2,1)S(1)} %shard_map.119.refs_0_), channel_id=1, source_target_pairs={{0,1},{1,0},{2,3},{3,2},{4,5},{5,4},{6,7},{7,6},{8,9},{9,8},{10,11... | collective-permute-start | bytes 884744 | tf_op jit(solution)/shard_map/ppermute | solution.py:36
  38.0 9.4 %collective-permute-start.9 = (bf16[576,256]{1,0:T(8,128)(2,1)S(1)}, bf16[576,256]{1,0:T(8,128)(2,1)S(1)}, u32[]{:S(2)}, u32[]{:S(2)}) collective-permute-start(bf16[576,256]{1,0:T(8,128)(2,1)S(1)} %shard_map.119.refs_0_), channel_id=1, source_target_pairs={{0,2},{1,3},{2,0},{3,1},{4,6},{5,7},{6,4},{7,5},{8,10},{9,11},{10,... | collective-permute-start | bytes 884744 | tf_op jit(solution)/shard_map/ppermute | solution.py:36
  47.4 1.6 %copy-start.13 = (s32[512]{0:T(512)S(1)}, s32[512]{0:T(512)}, u32[]{:S(2)}) copy-start(s32[512]{0:T(512)} %param.18) | copy-start | bytes 6148
  47.4 1.6 %copy-start.11 = (s32[512]{0:T(512)S(1)}, s32[512]{0:T(512)}, u32[]{:S(2)}) copy-start(s32[512]{0:T(512)} %param.19) | copy-start | bytes 6148
  47.4 1.6 %collective-permute-start.14 = (bf16[576,256]{1,0:T(8,128)(2,1)S(1)}, bf16[576,256]{1,0:T(8,128)(2,1)S(1)}, u32[]{:S(2)}, u32[]{:S(2)}) collective-permute-start(bf16[576,256]{1,0:T(8,128)(2,1)S(1)} %collective-permute-done.9.refs_0_), channel_id=1, source_target_pairs={{0,1},{1,0},{2,3},{3,2},{4,5},{5,4},{6,7},{7,6},{8,9},{9,8},{10,11... | collective-permute-start | bytes 884744 | tf_op jit(solution)/shard_map/ppermute | solution.py:36
  51.1 11.2 %collective-permute-start.18 = (bf16[768,256]{1,0:T(8,128)(2,1)S(1)}, bf16[768,256]{1,0:T(8,128)(2,1)S(1)}, u32[]{:S(2)}, u32[]{:S(2)}) collective-permute-start(bf16[768,256]{1,0:T(8,128)(2,1)S(1)} %get-tuple-element.58.cells), channel_id=1, source_target_pairs={{0,4},{4,0},{8,12},{12,8},{16,20},{20,16},{24,28},{28,24},{1,5},{5... | collective-permute-start | bytes 1179656 | tf_op jit(solution)/shard_map/ppermute | solution.py:36
  51.4 5.8 %collective-permute-start.17 = (bf16[64,256]{1,0:T(8,128)(2,1)S(1)}, bf16[64,256]{1,0:T(8,128)(2,1)S(1)}, u32[]{:S(2)}, u32[]{:S(2)}) collective-permute-start(bf16[64,256]{1,0:T(8,128)(2,1)S(1)} %get-tuple-element.61.refs_0_), channel_id=1, source_target_pairs={{0,24},{4,28},{8,16},{12,20},{16,8},{20,12},{24,0},{28,4},{1,25},{... | collective-permute-start | bytes 98312 | tf_op jit(solution)/shard_map/ppermute | solution.py:36
  54.4 4.8 %collective-permute-start.16 = (bf16[64,256]{1,0:T(8,128)(2,1)S(1)}, bf16[64,256]{1,0:T(8,128)(2,1)S(1)}, u32[]{:S(2)}, u32[]{:S(2)}) collective-permute-start(bf16[64,256]{1,0:T(8,128)(2,1)S(1)} %get-tuple-element.61.refs_0_), channel_id=1, source_target_pairs={{0,16},{4,20},{8,24},{12,28},{16,0},{20,4},{24,8},{28,12},{1,17},{... | collective-permute-start | bytes 98312 | tf_op jit(solution)/shard_map/ppermute | solution.py:36
  54.7 4.6 %collective-permute-start.15 = (bf16[64,256]{1,0:T(8,128)(2,1)S(1)}, bf16[64,256]{1,0:T(8,128)(2,1)S(1)}, u32[]{:S(2)}, u32[]{:S(2)}) collective-permute-start(bf16[64,256]{1,0:T(8,128)(2,1)S(1)} %get-tuple-element.61.refs_0_), channel_id=1, source_target_pairs={{0,8},{4,12},{8,0},{12,4},{16,24},{20,28},{24,16},{28,20},{1,9},{5... | collective-permute-start | bytes 98312 | tf_op jit(solution)/shard_map/ppermute | solution.py:36
  62.3 12.6 %collective-permute-start.20 = (bf16[512,256]{1,0:T(8,128)(2,1)S(1)}, bf16[512,256]{1,0:T(8,128)(2,1)S(1)}, u32[]{:S(2)}, u32[]{:S(2)}) collective-permute-start(bf16[512,256]{1,0:T(8,128)(2,1)S(1)} %get-tuple-element.65), channel_id=1, source_target_pairs={{0,8},{4,0},{8,16},{12,4},{16,24},{20,12},{24,28},{28,20},{1,9},{5... | collective-permute-start | bytes 786440 | tf_op jit(solution)/shard_map/ppermute | solution.py:47
  62.7 10.0 %collective-permute-start.19 = (bf16[256,256]{1,0:T(8,128)(2,1)S(1)}, bf16[256,256]{1,0:T(8,128)(2,1)S(1)}, u32[]{:S(2)}, u32[]{:S(2)}) collective-permute-start(bf16[256,256]{1,0:T(8,128)(2,1)S(1)} %shard_map.123.mine), channel_id=1, source_target_pairs={{0,4},{4,0},{8,12},{12,8},{16,20},{20,16},{24,28},{28,24},{1,5},{5... | collective-permute-start | bytes 393224 | tf_op jit(solution)/shard_map/ppermute | solution.py:36
  64.4 9.2 %collective-permute-start.21 = (bf16[64,256]{1,0:T(8,128)(2,1)S(1)}, bf16[64,256]{1,0:T(8,128)(2,1)S(1)}, u32[]{:S(2)}, u32[]{:S(2)}) collective-permute-start(bf16[64,256]{1,0:T(8,128)(2,1)S(1)} %get-tuple-element.67), channel_id=1, source_target_pairs={{0,8},{4,12},{8,0},{12,4},{16,24},{20,28},{24,16},{28,20},{1,9},{5... | collective-permute-start | bytes 98312 | tf_op jit(solution)/shard_map/ppermute | solution.py:36
  64.7 8.9 %collective-permute-start.22 = (bf16[64,256]{1,0:T(8,128)(2,1)S(1)}, bf16[64,256]{1,0:T(8,128)(2,1)S(1)}, u32[]{:S(2)}, u32[]{:S(2)}) collective-permute-start(bf16[64,256]{1,0:T(8,128)(2,1)S(1)} %get-tuple-element.68), channel_id=1, source_target_pairs={{0,16},{4,20},{8,24},{12,28},{16,0},{20,4},{24,8},{28,12},{1,17},{... | collective-permute-start | bytes 98312 | tf_op jit(solution)/shard_map/ppermute | solution.py:36
  66.3 7.3 %collective-permute-start.23 = (bf16[64,256]{1,0:T(8,128)(2,1)S(1)}, bf16[64,256]{1,0:T(8,128)(2,1)S(1)}, u32[]{:S(2)}, u32[]{:S(2)}) collective-permute-start(bf16[64,256]{1,0:T(8,128)(2,1)S(1)} %get-tuple-element.69), channel_id=1, source_target_pairs={{0,24},{4,28},{8,16},{12,20},{16,8},{20,12},{24,0},{28,4},{1,25},{... | collective-permute-start | bytes 98312 | tf_op jit(solution)/shard_map/ppermute | solution.py:36

commit v2 on v1

v2 whole, which is shorter than its diff:
```python
import functools

import jax
import jax.numpy as jnp
from jax import lax
from jax.experimental import pallas as pl
from jax.experimental.pallas import tpu as pltpu
from jax.sharding import PartitionSpec as P

BF = jnp.bfloat16
F32 = jnp.float32
LIMIT = 16 * 1024 * 1024
COST = 500_000_000


def local(kernel, outs, scalars, args, scratch=(), flops=COST):
    vmem = pl.BlockSpec(memory_space=pltpu.VMEM)
    smem = pl.BlockSpec(memory_space=pltpu.SMEM)
    moved = sum(a.size * a.dtype.itemsize for a in args)
    return pl.pallas_call(
        kernel,
        out_shape=[jax.ShapeDtypeStruct(s, d) for s, d in outs],
        in_specs=[smem] * len(scalars) + [vmem] * len(args),
        out_specs=[vmem] * len(outs),
        scratch_shapes=list(scratch),
        cost_estimate=pl.CostEstimate(flops=flops, bytes_accessed=moved, transcendentals=0),
        compiler_params=pltpu.CompilerParams(vmem_limit_bytes=LIMIT),
    )(*scalars, *args)


def mm(a, b):
    return jnp.dot(a, b, preferred_element_type=F32)


def swap(cells, axis, bit):
    count = lax.axis_size(axis)
    return lax.ppermute(cells, axis, [(i, i ^ bit) for i in range(count)])


def forward(cells):
    count = lax.axis_size("rows")
    pairs = []
    for i in range(count):
        if i % 2 == 0:
            pairs.append((i, i + 2 if i + 2 < count else i + 1))
        else:
            pairs.append((i, i - 2 if i > 1 else 0))
    return lax.ppermute(cells, "rows", pairs)


def spread(axis, cells, bits):
    pieces = {0: cells}
    for bit in bits:
        pieces.update({k | bit: swap(c, axis, bit) for k, c in list(pieces.items())})
    return pieces


def column(values, width):
    wide = jnp.broadcast_to(values.astype(F32), (128, values.shape[1]))
    tall = wide.T
    return jnp.concatenate([tall] * (width // 128), axis=1) if width > 128 else tall


def after(value, *others):
    return lax.optimization_barrier((value, *others))[0]


def xor_order(count):
    order = [0]
    bit = count // 2
    while bit:
        order += [k | bit for k in order]
        bit //= 2
    return order


def split_partial(part, keep, send, head_dev):
    if not head_dev:
        keep[...] = part[...]
        send[...] = part[...].astype(BF)
        return
    pair, parity = lax.axis_index("rows") // 2, lax.axis_index("rows") % 2
    for n, k in enumerate(xor_order(keep.shape[0] // head_dev)):
        mine = pl.multiple_of((2 * (pair ^ k) + parity) * head_dev, head_dev)
        theirs = pl.multiple_of((2 * (pair ^ k) + 1 - parity) * head_dev, head_dev)
        keep[n * head_dev : (n + 1) * head_dev] = part[pl.ds(mine, head_dev)]
        send[n * head_dev : (n + 1) * head_dev] = part[pl.ds(theirs, head_dev)].astype(BF)


def cast_kernel(cells, out):
    out[...] = cells[...].astype(BF)


def partial_kernel(rows, cells, *refs, head_dev):
    keep, send, part = refs[-3:]
    if len(refs) > 3:
        refs[1][...] = refs[0][...].astype(BF)
    part[...] = mm(rows[...], cells[...])
    split_partial(part, keep, send, head_dev)


def dense_kernel(place, tiles, cols, reach, cells, near, pair, far, masked, own, window, *, blocks):
    tile = tiles.shape[1]
    rows = window.shape[0]
    tile_rows = rows // tile
    parity = lax.axis_index("rows") % 2
    toward = 1 - 2 * parity
    inside = jnp.logical_and(lax.axis_index("rows") != 0, lax.axis_index("rows") != blocks - 1)
    window[...] = jnp.zeros_like(window)

    def add(s, carry):
        offset = place[2, s]
        group = jnp.where(offset == 0, 0, jnp.where(offset == toward, 1, 2))

        @pl.when(jnp.logical_or(group != 2, inside))
        def _():
            r = pl.ds(pl.multiple_of(place[0, s] * tile, tile), tile)
            c = pl.ds(pl.multiple_of((group * tile_rows + place[1, s]) * tile, tile), tile)
            window[r, c] += tiles[s].astype(F32)

        return carry

    lax.fori_loop(0, tiles.shape[0], add, 0)
    near[...] = window[:, :rows].astype(BF)
    pair[...] = window[:, rows : 2 * rows].astype(BF)
    far[...] = window[:, 2 * rows :].astype(BF)
    limit = column(reach[...], 128)
    for g in range(cols.shape[1] // 128):
        here = slice(g * 128, (g + 1) * 128)
        lane = (lax.broadcasted_iota(jnp.int32, (rows, 128), 1) + g * 128).astype(F32)
        masked[:, here] = jnp.where(lane < limit, cols[:, here].astype(F32), 0.0).astype(BF)
    own[...] = mm(near[...], cells[...])


def near_kernel(near, cells, out):
    out[...] = mm(near[...], cells[...])


def sum_kernel(total, pair, cells, masked, mine, theirs, out, heads, *, head_dev):
    whole_heads(mine, theirs, heads, head_dev)
    out[...] = total[...] + mm(pair[...], cells[...]) + mm(masked[...], heads[...])


def fold_kernel(keep, arrived, kept, send):
    half = kept.shape[0]
    kept[...] = keep[:half] + arrived[:half].astype(F32)
    send[...] = (keep[half:] + arrived[half:].astype(F32)).astype(BF)


def join_kernel(*refs):
    size = refs[0].shape[0]
    for k, ref in enumerate(refs[:-1]):
        refs[-1][k * size : (k + 1) * size] = ref[...]


def whole_heads(mine, theirs, heads, head_dev):
    if not head_dev:
        heads[...] = mine[...]
        return
    pair, parity = lax.axis_index("rows") // 2, lax.axis_index("rows") % 2
    for n, k in enumerate(xor_order(mine.shape[0] // head_dev)):
        here = slice(n * head_dev, (n + 1) * head_dev)
        a = pl.multiple_of((2 * (pair ^ k) + parity) * head_dev, head_dev)
        b = pl.multiple_of((2 * (pair ^ k) + 1 - parity) * head_dev, head_dev)
        heads[pl.ds(a, head_dev)] = mine[here]
        heads[pl.ds(b, head_dev)] = theirs[here]


def first_sum_kernel(total, far, other, *refs):
    parts, out = refs[:-1], refs[-1]
    rows = total.shape[0]
    out[:rows] = (total[...] + mm(far[...], other[...])).astype(BF)
    if parts:
        extra = parts[0][...]
        for part in parts[1:]:
            extra = extra + part[...].astype(F32)
        out[rows:] = extra.astype(BF)


def last_sum_kernel(total, far, other, scale, out):
    out[...] = jnp.maximum((total[...] + mm(far[...], other[...])) * scale[...], 0.0)


def feature_rows(k, width):
    return pl.ds(pl.multiple_of((lax.axis_index("feat") ^ k) * width, width), width)


def mix_begin_kernel(*refs, early):
    pieces, shards, outs = refs[:early], refs[early : early + 2], refs[early + 2 :]
    for shard, out in zip(shards, outs):
        total = None
        for k, piece in enumerate(pieces):
            term = mm(piece[...], shard[feature_rows(k, out.shape[1])])
            total = term if total is None else total + term
        out[...] = total


def mix_end_kernel(*refs, early, order, head_dev):
    pieces, refs = refs[: 2 * early], refs[2 * early :]
    shards, refs = refs[: 2 * early], refs[2 * early :]
    begun, refs = refs[:2], refs[2:]
    weights, band_scale, head_scale, *outs, scale = refs
    band, width = band_scale.shape
    scale[:band] = band_scale[...]
    if head_dev:
        scale[band:] = head_scale[...]
    result = None
    for n, (j, shard) in enumerate(zip(order, shards)):
        total = begun[n][...] if n < 2 else None
        for k in range(early if n < 2 else 0, 2 * early):
            term = mm(pieces[k][...], shard[feature_rows(k, width)])
            total = term if total is None else total + term
        state = jnp.maximum(total * scale[...], 0.0).astype(BF)
        term = mm(state, weights[1, feature_rows(j, width)])
        result = term if result is None else result + term
    outs[0][...] = result[:band].astype(BF)
    if head_dev:
        outs[1][...] = result[band:].astype(BF)


def scale_kernel(degree, head_degree, scale, head_scale, all_scales):
    size = head_scale.shape[0]
    scale[...] = lax.rsqrt(column(degree[...], scale.shape[1]))
    all_scales[...] = lax.rsqrt(column(head_degree[...], scale.shape[1]))
    head_scale[...] = all_scales[pl.ds(pl.multiple_of(lax.axis_index("rows") * size, size), size)]


def wide_scale_kernel(degree, scale):
    scale[...] = lax.rsqrt(column(degree[...], scale.shape[1]))


def head_out_kernel(own, *refs):
    arrived, (scale, out) = refs[:-2], refs[-2:]
    total = own[...]
    for ref in arrived:
        total = total + ref[...].astype(F32)
    out[...] = jnp.maximum(total * scale[...], 0.0)


def body(
    band_feats,
    head_feats,
    mix_weights,
    tile_place,
    tile_vals,
    arrow_cols,
    arrow_reach,
    arrow_rows,
    band_degree,
    head_degree,
):
    rows_dev, width = band_feats.shape
    head_dev = head_feats.shape[0]
    heads = arrow_cols.shape[1]
    blocks = lax.axis_size("rows")
    pairs = blocks // 2
    top_bit = lax.axis_size("feat") // 2
    low_bits = [1 << n for n in reversed(range(top_bit.bit_length() - 1))]
    reach = arrow_reach[None, :]
    size = head_dev if pairs <= 4 and head_dev % 16 == 0 else 0
    part_rows = heads // 2 if size else heads
    part_scratch = pltpu.VMEM((heads, width), F32)
    head_scratch = pltpu.VMEM((heads, width), BF)
    band_sum = [((rows_dev, width), F32)]
    cells_shape = ((rows_dev, width), BF)
    head_sum = ((head_dev, width), F32)
    keep_shapes = [((part_rows, width), F32), ((part_rows, width), BF)]
    sum_up = functools.partial(sum_kernel, head_dev=size)

    def partial_sums(cells, *head):
        outs = [(h.shape, BF) for h in head] + keep_shapes
        add_up = functools.partial(partial_kernel, head_dev=size)
        return local(add_up, outs, (), (arrow_rows, cells, *head), [part_scratch])

    def gather_heads(own, before):
        if not size:
            everyone = lax.all_gather(own, "rows", axis=0, tiled=True)
            return everyone, everyone
        mine = own
        bit = pairs // 2
        while bit:
            other = swap(mine, "rows", 2 * bit)
            rows = 2 * mine.shape[0]
            (mine,) = local(join_kernel, [((rows, width), BF)], (), (after(mine, before), other))
            bit //= 2
        return mine, swap(mine, "rows", 1)

    def scatter_heads(keep, send, before):
        if not size:
            return []
        bit = 1
        while bit <= pairs:
            arrived = swap(send, "rows", bit)
            if bit < pairs:
                rows = keep.shape[0] // 2
                outs = [((rows, width), F32), ((rows, width), BF)]
                keep, send = local(fold_kernel, outs, (), (after(keep, before), arrived))
            bit *= 2
        return [keep, arrived]

    (cells,) = local(cast_kernel, [cells_shape], (), (band_feats,))
    pair_cells = swap(cells, "rows", 1)
    first = after(mix_weights, cells)[0]
    across = swap(first, "feat", top_bit)
    head_cells, keep, send = partial_sums(cells, head_feats)
    first_part = keep
    near, pair, far, masked, total = local(
        functools.partial(dense_kernel, blocks=blocks),
        [((rows_dev, rows_dev), BF)] * 3 + [((rows_dev, heads), BF), ((rows_dev, width), F32)],
        (tile_place.T,),
        (tile_vals, arrow_cols, reach, after(cells, keep)),
        [pltpu.VMEM((rows_dev, 3 * rows_dev), F32)],
    )
    mine, theirs = gather_heads(head_cells, total)
    far_cells = forward(after(pair_cells, mine))
    parts = scatter_heads(keep, send, mine)
    total = after(total, *parts[:1])
    (total,) = local(sum_up, band_sum, (), (total, pair, pair_cells, masked, mine, theirs), [head_scratch])
    tall = rows_dev + size
    (joined,) = local(
        first_sum_kernel, [((tall, width), BF)], (), (total, far, far_cells, *parts)
    )

    opposite = swap(joined, "feat", top_bit)
    band_degree = after(band_degree, joined)
    if size:
        scale, head_scale = local(
            scale_kernel,
            band_sum + [head_sum],
            (),
            (band_degree[None, :], head_degree[None, :]),
            [pltpu.VMEM((heads, width), F32)],
        )
    else:
        (scale,) = local(wide_scale_kernel, band_sum, (), (band_degree[None, :],))
        head_scale = lax.rsqrt(head_degree.astype(F32))[:, None] * jnp.ones((1, width), F32)
        head_scale = lax.dynamic_slice_in_dim(head_scale, lax.axis_index("rows") * head_dev, head_dev, 0)
    pieces = spread("feat", after(joined, scale), low_bits)
    early = len(pieces)
    pieces.update({k | top_bit: c for k, c in spread("feat", opposite, low_bits).items()})
    pieces = [pieces[k] for k in sorted(pieces)]
    shards = spread("feat", after(first, scale), low_bits)
    shards.update({k | top_bit: w for k, w in spread("feat", after(across, scale), low_bits).items()})
    order = [0, top_bit] + [k for k in sorted(shards) if k not in (0, top_bit)]
    begun = local(
        functools.partial(mix_begin_kernel, early=early),
        [((tall, width), F32)] * 2,
        (),
        (after(pieces[0], opposite), *pieces[1:early], shards[0], shards[top_bit]),
    )
    cells, *head_x = local(
        functools.partial(mix_end_kernel, early=early, order=order, head_dev=size),
        [cells_shape] + ([((size, width), BF)] if size else []),
        (),
        (*pieces, *[shards[k] for k in order], *begun, mix_weights, scale, head_scale),
        [pltpu.VMEM((tall, width), F32)],
    )
    if not size:
        summed = lax.psum_scatter(first_part, "rows", scatter_dimension=0, tiled=True).astype(BF)
        summed = lax.all_gather(summed, "feat", axis=1, tiled=True)
        full = lax.all_gather(mix_weights[0], "feat", axis=1, tiled=True)
        head_state = jnp.maximum(mm(summed, full) * head_scale[:, :1], 0.0).astype(BF)
        head_x = [mm(head_state, mix_weights[1]).astype(BF)]

    pair_cells = swap(cells, "rows", 1)
    keep, send = partial_sums(cells)
    (total,) = local(near_kernel, band_sum, (), (after(near, keep), cells))
    mine, theirs = gather_heads(after(head_x[0], keep), total)
    far_cells = forward(after(pair_cells, mine))
    parts = scatter_heads(keep, send, mine)
    (total,) = local(
        sum_up, band_sum, (), (after(total, *parts[:1]), pair, pair_cells, masked, mine, theirs), [head_scratch]
    )
    if size:
        (head_out,) = local(head_out_kernel, [head_sum], (), (after(parts[0], total), *parts[1:], head_scale))
    else:
        head_out = jnp.maximum(lax.psum_scatter(keep, "rows", scatter_dimension=0, tiled=True) * head_scale, 0.0)
    (band_out,) = local(last_sum_kernel, band_sum, (), (total, far, far_cells, scale))
    return band_out, head_out


def solution(mesh):
    in_specs = (
        P("rows", "feat"),
        P("rows", "feat"),
        P(None, None, "feat"),
        P("rows", None),
        P("rows", None, None),
        P("rows", None),
        P("rows"),
        P(None, "rows"),
        P("rows"),
        P(),
    )
    out_specs = (P("rows", "feat"), P("rows", "feat"))
    return jax.shard_map(body, mesh=mesh, in_specs=in_specs, out_specs=out_specs, check_vma=False)
```

time: 76.4 us -> 64.7 us (0.85)
  local copies, waits for them, and re-layouts: 6.9 us -> 1.88 us
  Pallas kernels: 13.7 us -> 9.03 us
  starting transfers between devices: 25.8 us -> 21.4 us
  waiting for transfers between devices: 28.6 us -> 31.4 us
    unnamed x29 -> x20, local copies, waits for them, and re-layouts: 6.87 us -> 1.85 us
    ppermute x22 -> x20, starting transfers between devices: 24 us -> 19 us  [swap(): return lax.ppermute(cells, axis, [(i, i ^ bit) for i in range(count)])]
    pallas_call x16 -> x21, Pallas kernels: 13.7 us -> 9.03 us  [local(): pl.pallas_call(kernel, out_shape=[jax.ShapeDtypeStruct(s, d) for s, d in...]
    ppermute x22 -> x20, waiting for transfers between devices: 28.6 us -> 31.4 us  [swap(): return lax.ppermute(cells, axis, [(i, i ^ bit) for i in range(count)])]
  transfers between devices with their start and end apart: 24 -> 22, of which waited for: 10 -> 12; matrix products, arithmetic and copies ran while one was open for 1% -> 0% of each run, Pallas kernels for 12% -> 9%
where the time goes in v2:
time: 64.7 us; the launch traced here: 64.5 us
  waiting for transfers between devices  31.4 us (49%)
  starting transfers between devices  21.4 us (33%)
  Pallas kernels  9.03 us (14%)
  local copies, waits for them, and re-layouts  1.88 us (3%)
  between operations  0.88 us (1%)
    ppermute x20, waiting for transfers between devices, swap(): return lax.ppermute(cells, axis, [(i, i ^ bit) for i in range(count)])  31.4 us
    ppermute x20, starting transfers between devices, swap(): return lax.ppermute(cells, axis, [(i, i ^ bit) for i in range(count)])  19 us
    pallas_call x21, Pallas kernels, local(): pl.pallas_call(kernel, out_shape=[jax.ShapeDtypeStruct(s, d) for s, d in...  9.03 us
    ppermute x2, starting transfers between devices, forward(): return lax.ppermute(cells, 'rows', pairs)  2.34 us
    unnamed x20, local copies, waits for them, and re-layouts  1.85 us
  transfers between devices with their start and end apart: 22, of which 12 were waited for; matrix products, arithmetic and copies ran while one was open for 0% of the time, Pallas kernels for 9%

profile of v2, /device:TPU:0, one launch (start us, length us, event | category | flops | bytes accessed | tf_op | source)
XLA Modules:
  0.0 64.5 jit_solution(7842385585658402456)
XLA Ops:
  0.6 1.0 %copy-done.2 = f32[512,256]{1,0:T(8,128)S(1)} copy-done((f32[512,256]{1,0:T(8,128)S(1)}, f32[512,256]{1,0:T(8,128)}, u32[]{:S(2)}) %copy-start.2) | copy-done | bytes 524312
  1.7 3.0 %collective-permute-start.4 = (bf16[512,256]{1,0:T(8,128)(2,1)S(1)}, bf16[512,256]{1,0:T(8,128)(2,1)S(1)}, u32[]{:S(2)}, u32[]{:S(2)}) collective-permute-start(bf16[512,256]{1,0:T(8,128)(2,1)S(1)} %shard_map.113.cells), channel_id=1, source_target_pairs={{0,4},{4,0},{8,12},{12,8},{16,20},{20,16},{24,28},{28,24},{1,5},{5... | collective-permute-start | bytes 786440 | tf_op jit(solution)/shard_map/ppermute | solution.py:37
  4.7 0.3 shard_map.114
  5.1 2.7 %collective-permute-start = (bf16[64,256]{1,0:T(8,128)(2,1)S(1)}, bf16[64,256]{1,0:T(8,128)(2,1)S(1)}, u32[]{:S(2)}, u32[]{:S(2)}) collective-permute-start(bf16[64,256]{1,0:T(8,128)(2,1)S(1)} %get-tuple-element.53.refs_0_), channel_id=1, source_target_pairs={{0,16},{4,20},{8,24},{12,28},{16,0},{20,4},{24,8},{28,12},{1,17},{... | collective-permute-start | bytes 98312 | tf_op jit(solution)/shard_map/ppermute | solution.py:37
  7.8 1.6 %collective-permute-start.11 = (bf16[1024,256]{1,0:T(8,128)(2,1)S(1)}, bf16[1024,256]{1,0:T(8,128)(2,1)S(1)}, u32[]{:S(2)}, u32[]{:S(2)}) collective-permute-start(bf16[1024,256]{1,0:T(8,128)(2,1)S(1)} %slice_bitcast_fusion.refs_2_.refs_4_), channel_id=1, source_target_pairs={{0,2},{1,3},{2,0},{3,1},{4,6},{5,7},{6,4},{7,5},{8,10},{9,11},{10,... | collective-permute-start | bytes 1572872 | tf_op jit(solution)/shard_map/ppermute | solution.py:37
  9.4 0.7 %copy-done.6 = s32[32,3]{0,1:T(4,128)S(1)} copy-done((s32[32,3]{0,1:T(4,128)S(1)}, s32[32,3]{0,1:T(4,128)}, u32[]{:S(2)}) %copy-start.6) | copy-done | bytes 408
  10.1 2.0 %shard_map.115 = (bf16[512,512]{1,0:T(8,128)(2,1)S(1)}, bf16[512,512]{1,0:T(8,128)(2,1)S(1)}, bf16[512,512]{1,0:T(8,128)(2,1)S(1)}, bf16[512,512]{1,0:T(8,128)(2,1)S(1)}, f32[512,256]{1,0:T(8,128)S(1)}) custom-call(s32[3,32]{1,0:T(4,128)S(1)} %bitcast.6, bf16[32,128,128]{2,1,0:T(8,128)(2,1)S(1)} %copy-done.1, bf16[512,512]{1,0:T(8,128)(2,1)S(1)} %copy-done.3, ...), custom_call_target="tpu_custom_call" | custom-call | flops 500000000 | bytes 1837056 | tf_op jit(solution)/shard_map/pallas_call | solution.py:20
  12.1 1.8 %collective-permute-start.1 = (bf16[128,256]{1,0:T(8,128)(2,1)S(1)}, bf16[128,256]{1,0:T(8,128)(2,1)S(1)}, u32[]{:S(2)}, u32[]{:S(2)}) collective-permute-start(bf16[128,256]{1,0:T(8,128)(2,1)S(1)} %shard_map.116.refs_0_), channel_id=1, source_target_pairs={{0,8},{4,12},{8,0},{12,4},{16,24},{20,28},{24,16},{28,20},{1,9},{5... | collective-permute-start | bytes 196616 | tf_op jit(solution)/shard_map/ppermute | solution.py:37
  13.9 0.9 %collective-permute-start.2 = (bf16[256,256]{1,0:T(8,128)(2,1)S(1)}, bf16[256,256]{1,0:T(8,128)(2,1)S(1)}, u32[]{:S(2)}, u32[]{:S(2)}) collective-permute-start(bf16[256,256]{1,0:T(8,128)(2,1)S(1)} %get-tuple-element.56), channel_id=1, source_target_pairs={{0,4},{4,0},{8,12},{12,8},{16,20},{20,16},{24,28},{28,24},{1,5},{5... | collective-permute-start | bytes 393224 | tf_op jit(solution)/shard_map/ppermute | solution.py:37
  14.8 1.6 %collective-permute-done.1.refs_1_ = bf16[128,256]{1,0:T(8,128)(2,1)S(1)} collective-permute-done((bf16[128,256]{1,0:T(8,128)(2,1)S(1)}, bf16[128,256]{1,0:T(8,128)(2,1)S(1)}, u32[]{:S(2)}, u32[]{:S(2)}) %collective-permute-start.1) | collective-permute-done | bytes 65568 | tf_op jit(solution)/shard_map/ppermute | solution.py:37
  16.5 1.8 %collective-permute-start.6 = (bf16[512,256]{1,0:T(8,128)(2,1)S(1)}, bf16[512,256]{1,0:T(8,128)(2,1)S(1)}, u32[]{:S(2)}, u32[]{:S(2)}) collective-permute-start(bf16[512,256]{1,0:T(8,128)(2,1)S(1)} %collective-permute-done.4.cells), channel_id=1, source_target_pairs={{0,8},{4,0},{8,16},{12,4},{16,24},{20,12},{24,28},{28,20},{1,9},{5... | collective-permute-start | bytes 786440 | tf_op jit(solution)/shard_map/ppermute | solution.py:48
  18.3 0.3 collective-permute-start.5
  18.6 1.7 %collective-permute-done.2.arrived = bf16[256,256]{1,0:T(8,128)(2,1)S(1)} collective-permute-done((bf16[256,256]{1,0:T(8,128)(2,1)S(1)}, bf16[256,256]{1,0:T(8,128)(2,1)S(1)}, u32[]{:S(2)}, u32[]{:S(2)}) %collective-permute-start.2) | collective-permute-done | bytes 131104 | tf_op jit(solution)/shard_map/ppermute | solution.py:37
  20.3 0.1 collective-permute-start.3
  20.4 4.6 %collective-permute-done.3.arrived = bf16[128,256]{1,0:T(8,128)(2,1)S(1)} collective-permute-done((bf16[128,256]{1,0:T(8,128)(2,1)S(1)}, bf16[128,256]{1,0:T(8,128)(2,1)S(1)}, u32[]{:S(2)}, u32[]{:S(2)}) %collective-permute-start.3) | collective-permute-done | bytes 65568 | tf_op jit(solution)/shard_map/ppermute | solution.py:37
  25.0 0.1 collective-permute-start.7
  25.1 2.0 %collective-permute-done.5.theirs = bf16[256,256]{1,0:T(8,128)(2,1)S(1)} collective-permute-done((bf16[256,256]{1,0:T(8,128)(2,1)S(1)}, bf16[256,256]{1,0:T(8,128)(2,1)S(1)}, u32[]{:S(2)}, u32[]{:S(2)}) %collective-permute-start.5) | collective-permute-done | bytes 131104 | tf_op jit(solution)/shard_map/ppermute | solution.py:37
  27.1 0.5 shard_map.120.total
  27.6 2.3 %collective-permute-done.7.refs_1_ = bf16[64,256]{1,0:T(8,128)(2,1)S(1)} collective-permute-done((bf16[64,256]{1,0:T(8,128)(2,1)S(1)}, bf16[64,256]{1,0:T(8,128)(2,1)S(1)}, u32[]{:S(2)}, u32[]{:S(2)}) %collective-permute-start.7) | collective-permute-done | bytes 32800 | tf_op jit(solution)/shard_map/ppermute | solution.py:37
  29.9 0.3 shard_map.121.refs_0_
  30.2 0.6 collective-permute-start.9
  30.8 0.1 copy-done.8
  30.9 0.2 shard_map.122
  31.1 0.1 collective-permute-start.12
  31.2 0.5 collective-permute-start.13
  31.7 0.1 collective-permute-start.8
  31.8 5.2 %collective-permute-done.9.refs_2_ = bf16[576,256]{1,0:T(8,128)(2,1)S(1)} collective-permute-done((bf16[576,256]{1,0:T(8,128)(2,1)S(1)}, bf16[576,256]{1,0:T(8,128)(2,1)S(1)}, u32[]{:S(2)}, u32[]{:S(2)}) %collective-permute-start.9) | collective-permute-done | bytes 294944 | tf_op jit(solution)/shard_map/ppermute | solution.py:37
  37.0 0.5 shard_map.123
  37.5 1.1 %collective-permute-done.10.refs_3_ = bf16[576,256]{1,0:T(8,128)(2,1)S(1)} collective-permute-done((bf16[576,256]{1,0:T(8,128)(2,1)S(1)}, bf16[576,256]{1,0:T(8,128)(2,1)S(1)}, u32[]{:S(2)}, u32[]{:S(2)}) %collective-permute-start.10) | collective-permute-done | bytes 294944 | tf_op jit(solution)/shard_map/ppermute | solution.py:37
  38.6 2.3 %shard_map.124 = (bf16[512,256]{1,0:T(8,128)(2,1)S(1)}, bf16[64,256]{1,0:T(8,128)(2,1)S(1)}) custom-call(bf16[576,256]{1,0:T(8,128)(2,1)S(1)} %shard_map.121.refs_0_, bf16[576,256]{1,0:T(8,128)(2,1)S(1)} %collective-permute-done.8.refs_1_, bf16[576,256]{1,0:T(8,128)(2,1)S(1)} %collective-permute-done.9.refs_2_, ...), custom_call_target="tpu_custom_call" | custom-call | flops 500000000 | bytes 6094848 | tf_op jit(solution)/shard_map/pallas_call | solution.py:20
  40.9 0.7 %collective-permute-start.18 = (bf16[512,256]{1,0:T(8,128)(2,1)S(1)}, bf16[512,256]{1,0:T(8,128)(2,1)S(1)}, u32[]{:S(2)}, u32[]{:S(2)}) collective-permute-start(bf16[512,256]{1,0:T(8,128)(2,1)S(1)} %get-tuple-element.77.cells), channel_id=1, source_target_pairs={{0,4},{4,0},{8,12},{12,8},{16,20},{20,16},{24,28},{28,24},{1,5},{5... | collective-permute-start | bytes 786440 | tf_op jit(solution)/shard_map/ppermute | solution.py:37
  41.6 0.3 shard_map.125
  41.9 0.4 collective-permute-start.14
  42.3 0.3 shard_map.126.total
  42.6 1.2 %collective-permute-start.16 = (bf16[256,256]{1,0:T(8,128)(2,1)S(1)}, bf16[256,256]{1,0:T(8,128)(2,1)S(1)}, u32[]{:S(2)}, u32[]{:S(2)}) collective-permute-start(bf16[256,256]{1,0:T(8,128)(2,1)S(1)} %get-tuple-element.85), channel_id=1, source_target_pairs={{0,4},{4,0},{8,12},{12,8},{16,20},{20,16},{24,28},{28,24},{1,5},{5... | collective-permute-start | bytes 393224 | tf_op jit(solution)/shard_map/ppermute | solution.py:37
  43.8 3.3 %collective-permute-done.14.refs_1_ = bf16[64,256]{1,0:T(8,128)(2,1)S(1)} collective-permute-done((bf16[64,256]{1,0:T(8,128)(2,1)S(1)}, bf16[64,256]{1,0:T(8,128)(2,1)S(1)}, u32[]{:S(2)}, u32[]{:S(2)}) %collective-permute-start.14) | collective-permute-done | bytes 32800 | tf_op jit(solution)/shard_map/ppermute | solution.py:37
  47.1 0.5 collective-permute-start.15
  47.6 3.8 %collective-permute-done.15.refs_1_ = bf16[128,256]{1,0:T(8,128)(2,1)S(1)} collective-permute-done((bf16[128,256]{1,0:T(8,128)(2,1)S(1)}, bf16[128,256]{1,0:T(8,128)(2,1)S(1)}, u32[]{:S(2)}, u32[]{:S(2)}) %collective-permute-start.15) | collective-permute-done | bytes 65568 | tf_op jit(solution)/shard_map/ppermute | solution.py:37
  51.4 0.6 collective-permute-start.20
  52.0 1.5 %collective-permute-start.19 = (bf16[256,256]{1,0:T(8,128)(2,1)S(1)}, bf16[256,256]{1,0:T(8,128)(2,1)S(1)}, u32[]{:S(2)}, u32[]{:S(2)}) collective-permute-start(bf16[256,256]{1,0:T(8,128)(2,1)S(1)} %shard_map.128.mine), channel_id=1, source_target_pairs={{0,4},{4,0},{8,12},{12,8},{16,20},{20,16},{24,28},{28,24},{1,5},{5... | collective-permute-start | bytes 393224 | tf_op jit(solution)/shard_map/ppermute | solution.py:37
  53.5 1.1 %collective-permute-start.17 = (bf16[128,256]{1,0:T(8,128)(2,1)S(1)}, bf16[128,256]{1,0:T(8,128)(2,1)S(1)}, u32[]{:S(2)}, u32[]{:S(2)}) collective-permute-start(bf16[128,256]{1,0:T(8,128)(2,1)S(1)} %get-tuple-element.88), channel_id=1, source_target_pairs={{0,8},{4,12},{8,0},{12,4},{16,24},{20,28},{24,16},{28,20},{1,9},{5... | collective-permute-start | bytes 196616 | tf_op jit(solution)/shard_map/ppermute | solution.py:37
  54.7 3.2 %collective-permute-done.17.arrived = bf16[128,256]{1,0:T(8,128)(2,1)S(1)} collective-permute-done((bf16[128,256]{1,0:T(8,128)(2,1)S(1)}, bf16[128,256]{1,0:T(8,128)(2,1)S(1)}, u32[]{:S(2)}, u32[]{:S(2)}) %collective-permute-start.17) | collective-permute-done | bytes 65568 | tf_op jit(solution)/shard_map/ppermute | solution.py:37
  57.9 1.9 %collective-permute-start.21 = (bf16[64,256]{1,0:T(8,128)(2,1)S(1)}, bf16[64,256]{1,0:T(8,128)(2,1)S(1)}, u32[]{:S(2)}, u32[]{:S(2)}) collective-permute-start(bf16[64,256]{1,0:T(8,128)(2,1)S(1)} %get-tuple-element.93), channel_id=1, source_target_pairs={{0,16},{4,20},{8,24},{12,28},{16,0},{20,4},{24,8},{28,12},{1,17},{... | collective-permute-start | bytes 98312 | tf_op jit(solution)/shard_map/ppermute | solution.py:37
  59.8 0.7 %collective-permute-done.19.theirs = bf16[256,256]{1,0:T(8,128)(2,1)S(1)} collective-permute-done((bf16[256,256]{1,0:T(8,128)(2,1)S(1)}, bf16[256,256]{1,0:T(8,128)(2,1)S(1)}, u32[]{:S(2)}, u32[]{:S(2)}) %collective-permute-start.19) | collective-permute-done | bytes 131104 | tf_op jit(solution)/shard_map/ppermute | solution.py:37
  60.5 0.5 shard_map.131.total
  61.0 1.8 %collective-permute-done.21.refs_0_ = bf16[64,256]{1,0:T(8,128)(2,1)S(1)} collective-permute-done((bf16[64,256]{1,0:T(8,128)(2,1)S(1)}, bf16[64,256]{1,0:T(8,128)(2,1)S(1)}, u32[]{:S(2)}, u32[]{:S(2)}) %collective-permute-start.21) | collective-permute-done | bytes 32800 | tf_op jit(solution)/shard_map/ppermute | solution.py:37
  62.8 0.6 shard_map.133
  63.4 1.1 %shard_map.132 = f32[512,256]{1,0:T(8,128)} custom-call(f32[512,256]{1,0:T(8,128)S(1)} %shard_map.131.total, bf16[512,512]{1,0:T(8,128)(2,1)S(1)} %get-tuple-element.64.far, bf16[512,256]{1,0:T(8,128)(2,1)S(1)} %collective-permute-done.20.other, f32[512,256]{1,0:T(8,128)S(1)} %get-tuple-element.68.refs_11_.scale), custom_call_target="tpu_custom_call" | custom-call | flops 500000000 | bytes 1835008 | tf_op jit(solution)/shard_map/pallas_call | solution.py:20
  (38 shorter events, 0.2 us)
Async XLA Ops:
  0.6 1.0 %copy-start.2 = (f32[512,256]{1,0:T(8,128)S(1)}, f32[512,256]{1,0:T(8,128)}, u32[]{:S(2)}) copy-start(f32[512,256]{1,0:T(8,128)} %cells.1) | copy-start | bytes 1572868
  1.7 3.1 %copy-start.4 = (bf16[512,512]{1,0:T(8,128)(2,1)S(1)}, bf16[512,512]{1,0:T(8,128)(2,1)}, u32[]{:S(2)}) copy-start(bf16[512,512]{1,0:T(8,128)(2,1)} %rows.3) | copy-start | bytes 1572868
  1.7 3.1 %copy-start.5 = (f32[64,256]{1,0:T(8,128)S(1)}, f32[64,256]{1,0:T(8,128)}, u32[]{:S(2)}) copy-start(f32[64,256]{1,0:T(8,128)} %refs_0_.1) | copy-start | bytes 196612
  1.7 6.0 %copy-start = (bf16[2,1024,256]{2,1,0:T(8,128)(2,1)S(1)}, bf16[2,1024,256]{2,1,0:T(8,128)(2,1)}, u32[]{:S(2)}) copy-start(bf16[2,1024,256]{2,1,0:T(8,128)(2,1)} %refs_10_.1) | copy-start | bytes 3145732
  1.7 7.7 %copy-start.1 = (bf16[32,128,128]{2,1,0:T(8,128)(2,1)S(1)}, bf16[32,128,128]{2,1,0:T(8,128)(2,1)}, u32[]{:S(2)}) copy-start(bf16[32,128,128]{2,1,0:T(8,128)(2,1)} %tiles.1) | copy-start | bytes 3145732
  1.7 14.7 %collective-permute-start.4 = (bf16[512,256]{1,0:T(8,128)(2,1)S(1)}, bf16[512,256]{1,0:T(8,128)(2,1)S(1)}, u32[]{:S(2)}, u32[]{:S(2)}) collective-permute-start(bf16[512,256]{1,0:T(8,128)(2,1)S(1)} %shard_map.113.cells), channel_id=1, source_target_pairs={{0,4},{4,0},{8,12},{12,8},{16,20},{20,16},{24,28},{28,24},{1,5},{5... | collective-permute-start | bytes 786440 | tf_op jit(solution)/shard_map/ppermute | solution.py:37
  5.1 4.3 %copy-start.3 = (bf16[512,512]{1,0:T(8,128)(2,1)S(1)}, bf16[512,512]{1,0:T(8,128)(2,1)}, u32[]{:S(2)}) copy-start(bf16[512,512]{1,0:T(8,128)(2,1)} %cols.1) | copy-start | bytes 1572868
  5.1 7.0 %collective-permute-start = (bf16[64,256]{1,0:T(8,128)(2,1)S(1)}, bf16[64,256]{1,0:T(8,128)(2,1)S(1)}, u32[]{:S(2)}, u32[]{:S(2)}) collective-permute-start(bf16[64,256]{1,0:T(8,128)(2,1)S(1)} %get-tuple-element.53.refs_0_), channel_id=1, source_target_pairs={{0,16},{4,20},{8,24},{12,28},{16,0},{20,4},{24,8},{28,12},{1,17},{... | collective-permute-start | bytes 98312 | tf_op jit(solution)/shard_map/ppermute | solution.py:37
  7.7 1.6 %copy-start.7 = (s32[512]{0:T(512)S(1)}, s32[512]{0:T(512)}, u32[]{:S(2)}) copy-start(s32[512]{0:T(512)} %param.16) | copy-start | bytes 6148
  7.8 23.3 %collective-permute-start.11 = (bf16[1024,256]{1,0:T(8,128)(2,1)S(1)}, bf16[1024,256]{1,0:T(8,128)(2,1)S(1)}, u32[]{:S(2)}, u32[]{:S(2)}) collective-permute-start(bf16[1024,256]{1,0:T(8,128)(2,1)S(1)} %slice_bitcast_fusion.refs_2_.refs_4_), channel_id=1, source_target_pairs={{0,2},{1,3},{2,0},{3,1},{4,6},{5,7},{6,4},{7,5},{8,10},{9,11},{10,... | collective-permute-start | bytes 1572872 | tf_op jit(solution)/shard_map/ppermute | solution.py:37
  9.4 0.7 %copy-start.6 = (s32[32,3]{0,1:T(4,128)S(1)}, s32[32,3]{0,1:T(4,128)}, u32[]{:S(2)}) copy-start(s32[32,3]{0,1:T(4,128)} %param.13) | copy-start | bytes 1156
  12.1 4.3 %collective-permute-start.1 = (bf16[128,256]{1,0:T(8,128)(2,1)S(1)}, bf16[128,256]{1,0:T(8,128)(2,1)S(1)}, u32[]{:S(2)}, u32[]{:S(2)}) collective-permute-start(bf16[128,256]{1,0:T(8,128)(2,1)S(1)} %shard_map.116.refs_0_), channel_id=1, source_target_pairs={{0,8},{4,12},{8,0},{12,4},{16,24},{20,28},{24,16},{28,20},{1,9},{5... | collective-permute-start | bytes 196616 | tf_op jit(solution)/shard_map/ppermute | solution.py:37
  13.9 6.4 %collective-permute-start.2 = (bf16[256,256]{1,0:T(8,128)(2,1)S(1)}, bf16[256,256]{1,0:T(8,128)(2,1)S(1)}, u32[]{:S(2)}, u32[]{:S(2)}) collective-permute-start(bf16[256,256]{1,0:T(8,128)(2,1)S(1)} %get-tuple-element.56), channel_id=1, source_target_pairs={{0,4},{4,0},{8,12},{12,8},{16,20},{20,16},{24,28},{28,24},{1,5},{5... | collective-permute-start | bytes 393224 | tf_op jit(solution)/shard_map/ppermute | solution.py:37
  16.5 13.4 %collective-permute-start.6 = (bf16[512,256]{1,0:T(8,128)(2,1)S(1)}, bf16[512,256]{1,0:T(8,128)(2,1)S(1)}, u32[]{:S(2)}, u32[]{:S(2)}) collective-permute-start(bf16[512,256]{1,0:T(8,128)(2,1)S(1)} %collective-permute-done.4.cells), channel_id=1, source_target_pairs={{0,8},{4,0},{8,16},{12,4},{16,24},{20,12},{24,28},{28,20},{1,9},{5... | collective-permute-start | bytes 786440 | tf_op jit(solution)/shard_map/ppermute | solution.py:48
  18.3 8.8 %collective-permute-start.5 = (bf16[256,256]{1,0:T(8,128)(2,1)S(1)}, bf16[256,256]{1,0:T(8,128)(2,1)S(1)}, u32[]{:S(2)}, u32[]{:S(2)}) collective-permute-start(bf16[256,256]{1,0:T(8,128)(2,1)S(1)} %shard_map.117.mine), channel_id=1, source_target_pairs={{0,4},{4,0},{8,12},{12,8},{16,20},{20,16},{24,28},{28,24},{1,5},{5... | collective-permute-start | bytes 393224 | tf_op jit(solution)/shard_map/ppermute | solution.py:37
  20.3 4.7 %collective-permute-start.3 = (bf16[128,256]{1,0:T(8,128)(2,1)S(1)}, bf16[128,256]{1,0:T(8,128)(2,1)S(1)}, u32[]{:S(2)}, u32[]{:S(2)}) collective-permute-start(bf16[128,256]{1,0:T(8,128)(2,1)S(1)} %get-tuple-element.59), channel_id=1, source_target_pairs={{0,8},{4,12},{8,0},{12,4},{16,24},{20,28},{24,16},{28,20},{1,9},{5... | collective-permute-start | bytes 196616 | tf_op jit(solution)/shard_map/ppermute | solution.py:37
  25.0 4.9 %collective-permute-start.7 = (bf16[64,256]{1,0:T(8,128)(2,1)S(1)}, bf16[64,256]{1,0:T(8,128)(2,1)S(1)}, u32[]{:S(2)}, u32[]{:S(2)}) collective-permute-start(bf16[64,256]{1,0:T(8,128)(2,1)S(1)} %get-tuple-element.66), channel_id=1, source_target_pairs={{0,16},{4,20},{8,24},{12,28},{16,0},{20,4},{24,8},{28,12},{1,17},{... | collective-permute-start | bytes 98312 | tf_op jit(solution)/shard_map/ppermute | solution.py:37
  29.9 0.9 %copy-start.9 = (s32[512]{0:T(512)S(1)}, s32[512]{0:T(512)}, u32[]{:S(2)}) copy-start(s32[512]{0:T(512)} %param.19) | copy-start | bytes 6148
  30.2 0.7 %copy-start.8 = (s32[512]{0:T(512)S(1)}, s32[512]{0:T(512)}, u32[]{:S(2)}) copy-start(s32[512]{0:T(512)} %param.18) | copy-start | bytes 6148
  30.2 6.8 %collective-permute-start.9 = (bf16[576,256]{1,0:T(8,128)(2,1)S(1)}, bf16[576,256]{1,0:T(8,128)(2,1)S(1)}, u32[]{:S(2)}, u32[]{:S(2)}) collective-permute-start(bf16[576,256]{1,0:T(8,128)(2,1)S(1)} %shard_map.121.refs_0_), channel_id=1, source_target_pairs={{0,2},{1,3},{2,0},{3,1},{4,6},{5,7},{6,4},{7,5},{8,10},{9,11},{10,... | collective-permute-start | bytes 884744 | tf_op jit(solution)/shard_map/ppermute | solution.py:37
  31.1 6.4 %collective-permute-start.12 = (bf16[1024,256]{1,0:T(8,128)(2,1)S(1)}, bf16[1024,256]{1,0:T(8,128)(2,1)S(1)}, u32[]{:S(2)}, u32[]{:S(2)}) collective-permute-start(bf16[1024,256]{1,0:T(8,128)(2,1)S(1)} %slice_bitcast_fusion.refs_2_.refs_4_), channel_id=1, source_target_pairs={{0,1},{1,0},{2,3},{3,2},{4,5},{5,4},{6,7},{7,6},{8,9},{9,8},{10,11... | collective-permute-start | bytes 1572872 | tf_op jit(solution)/shard_map/ppermute | solution.py:37
  31.2 6.3 %collective-permute-start.13 = (bf16[1024,256]{1,0:T(8,128)(2,1)S(1)}, bf16[1024,256]{1,0:T(8,128)(2,1)S(1)}, u32[]{:S(2)}, u32[]{:S(2)}) collective-permute-start(bf16[1024,256]{1,0:T(8,128)(2,1)S(1)} %collective-permute-done.11.refs_3_.refs_5_), channel_id=1, source_target_pairs={{0,1},{1,0},{2,3},{3,2},{4,5},{5,4},{6,7},{7,6},{8,9},{9,8},{10,11... | collective-permute-start | bytes 1572872 | tf_op jit(solution)/shard_map/ppermute | solution.py:37
  31.7 5.3 %collective-permute-start.8 = (bf16[576,256]{1,0:T(8,128)(2,1)S(1)}, bf16[576,256]{1,0:T(8,128)(2,1)S(1)}, u32[]{:S(2)}, u32[]{:S(2)}) collective-permute-start(bf16[576,256]{1,0:T(8,128)(2,1)S(1)} %shard_map.121.refs_0_), channel_id=1, source_target_pairs={{0,1},{1,0},{2,3},{3,2},{4,5},{5,4},{6,7},{7,6},{8,9},{9,8},{10,11... | collective-permute-start | bytes 884744 | tf_op jit(solution)/shard_map/ppermute | solution.py:37
  37.0 1.6 %collective-permute-start.10 = (bf16[576,256]{1,0:T(8,128)(2,1)S(1)}, bf16[576,256]{1,0:T(8,128)(2,1)S(1)}, u32[]{:S(2)}, u32[]{:S(2)}) collective-permute-start(bf16[576,256]{1,0:T(8,128)(2,1)S(1)} %collective-permute-done.9.refs_2_), channel_id=1, source_target_pairs={{0,1},{1,0},{2,3},{3,2},{4,5},{5,4},{6,7},{7,6},{8,9},{9,8},{10,11... | collective-permute-start | bytes 884744 | tf_op jit(solution)/shard_map/ppermute | solution.py:37
  40.9 10.5 %collective-permute-start.18 = (bf16[512,256]{1,0:T(8,128)(2,1)S(1)}, bf16[512,256]{1,0:T(8,128)(2,1)S(1)}, u32[]{:S(2)}, u32[]{:S(2)}) collective-permute-start(bf16[512,256]{1,0:T(8,128)(2,1)S(1)} %get-tuple-element.77.cells), channel_id=1, source_target_pairs={{0,4},{4,0},{8,12},{12,8},{16,20},{20,16},{24,28},{28,24},{1,5},{5... | collective-permute-start | bytes 786440 | tf_op jit(solution)/shard_map/ppermute | solution.py:37
  41.9 5.2 %collective-permute-start.14 = (bf16[64,256]{1,0:T(8,128)(2,1)S(1)}, bf16[64,256]{1,0:T(8,128)(2,1)S(1)}, u32[]{:S(2)}, u32[]{:S(2)}) collective-permute-start(bf16[64,256]{1,0:T(8,128)(2,1)S(1)} %get-tuple-element.82.refs_0_), channel_id=1, source_target_pairs={{0,16},{4,20},{8,24},{12,28},{16,0},{20,4},{24,8},{28,12},{1,17},{... | collective-permute-start | bytes 98312 | tf_op jit(solution)/shard_map/ppermute | solution.py:37
  42.6 10.9 %collective-permute-start.16 = (bf16[256,256]{1,0:T(8,128)(2,1)S(1)}, bf16[256,256]{1,0:T(8,128)(2,1)S(1)}, u32[]{:S(2)}, u32[]{:S(2)}) collective-permute-start(bf16[256,256]{1,0:T(8,128)(2,1)S(1)} %get-tuple-element.85), channel_id=1, source_target_pairs={{0,4},{4,0},{8,12},{12,8},{16,20},{20,16},{24,28},{28,24},{1,5},{5... | collective-permute-start | bytes 393224 | tf_op jit(solution)/shard_map/ppermute | solution.py:37
  47.1 4.3 %collective-permute-start.15 = (bf16[128,256]{1,0:T(8,128)(2,1)S(1)}, bf16[128,256]{1,0:T(8,128)(2,1)S(1)}, u32[]{:S(2)}, u32[]{:S(2)}) collective-permute-start(bf16[128,256]{1,0:T(8,128)(2,1)S(1)} %shard_map.127.refs_0_), channel_id=1, source_target_pairs={{0,8},{4,12},{8,0},{12,4},{16,24},{20,28},{24,16},{28,20},{1,9},{5... | collective-permute-start | bytes 196616 | tf_op jit(solution)/shard_map/ppermute | solution.py:37
  51.4 12.0 %collective-permute-start.20 = (bf16[512,256]{1,0:T(8,128)(2,1)S(1)}, bf16[512,256]{1,0:T(8,128)(2,1)S(1)}, u32[]{:S(2)}, u32[]{:S(2)}) collective-permute-start(bf16[512,256]{1,0:T(8,128)(2,1)S(1)} %collective-permute-done.18.cells), channel_id=1, source_target_pairs={{0,8},{4,0},{8,16},{12,4},{16,24},{20,12},{24,28},{28,20},{1,9},{5... | collective-permute-start | bytes 786440 | tf_op jit(solution)/shard_map/ppermute | solution.py:48
  52.0 8.5 %collective-permute-start.19 = (bf16[256,256]{1,0:T(8,128)(2,1)S(1)}, bf16[256,256]{1,0:T(8,128)(2,1)S(1)}, u32[]{:S(2)}, u32[]{:S(2)}) collective-permute-start(bf16[256,256]{1,0:T(8,128)(2,1)S(1)} %shard_map.128.mine), channel_id=1, source_target_pairs={{0,4},{4,0},{8,12},{12,8},{16,20},{20,16},{24,28},{28,24},{1,5},{5... | collective-permute-start | bytes 393224 | tf_op jit(solution)/shard_map/ppermute | solution.py:37
  53.5 4.3 %collective-permute-start.17 = (bf16[128,256]{1,0:T(8,128)(2,1)S(1)}, bf16[128,256]{1,0:T(8,128)(2,1)S(1)}, u32[]{:S(2)}, u32[]{:S(2)}) collective-permute-start(bf16[128,256]{1,0:T(8,128)(2,1)S(1)} %get-tuple-element.88), channel_id=1, source_target_pairs={{0,8},{4,12},{8,0},{12,4},{16,24},{20,28},{24,16},{28,20},{1,9},{5... | collective-permute-start | bytes 196616 | tf_op jit(solution)/shard_map/ppermute | solution.py:37
  57.9 4.9 %collective-permute-start.21 = (bf16[64,256]{1,0:T(8,128)(2,1)S(1)}, bf16[64,256]{1,0:T(8,128)(2,1)S(1)}, u32[]{:S(2)}, u32[]{:S(2)}) collective-permute-start(bf16[64,256]{1,0:T(8,128)(2,1)S(1)} %get-tuple-element.93), channel_id=1, source_target_pairs={{0,16},{4,20},{8,24},{12,28},{16,0},{20,4},{24,8},{28,12},{1,17},{... | collective-permute-start | bytes 98312 | tf_op jit(solution)/shard_map/ppermute | solution.py:37

commit v3 on v2

--- a/solution.py
+++ b/solution.py
@@ -10,10 +10,29 @@
 BF = jnp.bfloat16
 F32 = jnp.float32
 LIMIT = 16 * 1024 * 1024
-COST = 500_000_000
-
-
-def local(kernel, outs, scalars, args, scratch=(), flops=COST):
+WORK = {
+    "cast": 500_000_000,
+    "part1": 500_000_000,
+    "dense": 500_000_000,
+    "join1": 500_000_000,
+    "fold1": 2_000_000_000,
+    "sum1": 1_000_000,
+    "first": 500_000_000,
+    "scale": 500_000_000,
+    "begin": 1_000_000_000,
+    "mid": 500_000_000,
+    "end": 500_000_000,
+    "part2": 1_000_000,
+    "near": 500_000_000,
+    "join2": 500_000_000,
+    "fold2": 500_000_000,
+    "sum2": 500_000_000,
+    "last": 500_000_000,
+    "headout": 1_000_000,
+}
+
+
+def local(name, kernel, outs, scalars, args, scratch=()):
     vmem = pl.BlockSpec(memory_space=pltpu.VMEM)
     smem = pl.BlockSpec(memory_space=pltpu.SMEM)
     moved = sum(a.size * a.dtype.itemsize for a in args)
@@ -23,7 +42,7 @@
         in_specs=[smem] * len(scalars) + [vmem] * len(args),
         out_specs=[vmem] * len(outs),
         scratch_shapes=list(scratch),
-        cost_estimate=pl.CostEstimate(flops=flops, bytes_accessed=moved, transcendentals=0),
+        cost_estimate=pl.CostEstimate(flops=WORK[name], bytes_accessed=moved, transcendentals=0),
         compiler_params=pltpu.CompilerParams(vmem_limit_bytes=LIMIT),
     )(*scalars, *args)
 
@@ -186,7 +205,8 @@
 
 
 def mix_begin_kernel(*refs, early):
-    pieces, shards, outs = refs[:early], refs[early : early + 2], refs[early + 2 :]
+    half = (len(refs) - early) // 2
+    pieces, shards, outs = refs[:early], refs[early : early + half], refs[early + half :]
     for shard, out in zip(shards, outs):
         total = None
         for k, piece in enumerate(pieces):
@@ -196,9 +216,9 @@
 
 
 def mix_end_kernel(*refs, early, order, head_dev):
-    pieces, refs = refs[: 2 * early], refs[2 * early :]
+    pieces, refs = refs[:early], refs[early:]
     shards, refs = refs[: 2 * early], refs[2 * early :]
-    begun, refs = refs[:2], refs[2:]
+    begun, refs = refs[: 2 * early], refs[2 * early :]
     weights, band_scale, head_scale, *outs, scale = refs
     band, width = band_scale.shape
     scale[:band] = band_scale[...]
@@ -206,10 +226,9 @@
         scale[band:] = head_scale[...]
     result = None
     for n, (j, shard) in enumerate(zip(order, shards)):
-        total = begun[n][...] if n < 2 else None
-        for k in range(early if n < 2 else 0, 2 * early):
-            term = mm(pieces[k][...], shard[feature_rows(k, width)])
-            total = term if total is None else total + term
+        total = begun[n][...]
+        for k, piece in enumerate(pieces):
+            total = total + mm(piece[...], shard[feature_rows(early + k, width)])
         state = jnp.maximum(total * scale[...], 0.0).astype(BF)
         term = mm(state, weights[1, feature_rows(j, width)])
         result = term if result is None else result + term
@@ -267,25 +286,26 @@
     keep_shapes = [((part_rows, width), F32), ((part_rows, width), BF)]
     sum_up = functools.partial(sum_kernel, head_dev=size)
 
-    def partial_sums(cells, *head):
+    def partial_sums(name, cells, *head):
         outs = [(h.shape, BF) for h in head] + keep_shapes
         add_up = functools.partial(partial_kernel, head_dev=size)
-        return local(add_up, outs, (), (arrow_rows, cells, *head), [part_scratch])
-
-    def gather_heads(own, before):
+        return local(name, add_up, outs, (), (arrow_rows, cells, *head), [part_scratch])
+
+    def gather_heads(name, own, before):
         if not size:
             everyone = lax.all_gather(own, "rows", axis=0, tiled=True)
-            return everyone, everyone
-        mine = own
+            return everyone, everyone, everyone
+        mine, halfway = own, None
         bit = pairs // 2
         while bit:
             other = swap(mine, "rows", 2 * bit)
             rows = 2 * mine.shape[0]
-            (mine,) = local(join_kernel, [((rows, width), BF)], (), (after(mine, before), other))
+            (mine,) = local(name, join_kernel, [((rows, width), BF)], (), (after(mine, before), other))
+            halfway = mine if halfway is None else halfway
             bit //= 2
-        return mine, swap(mine, "rows", 1)
-
-    def scatter_heads(keep, send, before):
+        return halfway, mine, swap(mine, "rows", 1)
+
+    def scatter_heads(name, keep, send, before):
         if not size:
             return []
         bit = 1
@@ -294,37 +314,41 @@
             if bit < pairs:
                 rows = keep.shape[0] // 2
                 outs = [((rows, width), F32), ((rows, width), BF)]
-                keep, send = local(fold_kernel, outs, (), (after(keep, before), arrived))
+                keep, send = local(name, fold_kernel, outs, (), (after(keep, before), arrived))
             bit *= 2
         return [keep, arrived]
 
-    (cells,) = local(cast_kernel, [cells_shape], (), (band_feats,))
+    (cells,) = local("cast", cast_kernel, [cells_shape], (), (band_feats,))
     pair_cells = swap(cells, "rows", 1)
     first = after(mix_weights, cells)[0]
     across = swap(first, "feat", top_bit)
-    head_cells, keep, send = partial_sums(cells, head_feats)
+    head_cells, keep, send = partial_sums("part1", cells, head_feats)
     first_part = keep
     near, pair, far, masked, total = local(
+        "dense",
         functools.partial(dense_kernel, blocks=blocks),
         [((rows_dev, rows_dev), BF)] * 3 + [((rows_dev, heads), BF), ((rows_dev, width), F32)],
         (tile_place.T,),
         (tile_vals, arrow_cols, reach, after(cells, keep)),
         [pltpu.VMEM((rows_dev, 3 * rows_dev), F32)],
     )
-    mine, theirs = gather_heads(head_cells, total)
-    far_cells = forward(after(pair_cells, mine))
-    parts = scatter_heads(keep, send, mine)
+    halfway, mine, theirs = gather_heads("join1", head_cells, total)
+    far_cells = forward(after(pair_cells, total))
+    parts = scatter_heads("fold1", keep, send, total)
     total = after(total, *parts[:1])
-    (total,) = local(sum_up, band_sum, (), (total, pair, pair_cells, masked, mine, theirs), [head_scratch])
+    (total,) = local(
+        "sum1", sum_up, band_sum, (), (total, pair, pair_cells, masked, mine, theirs), [head_scratch]
+    )
     tall = rows_dev + size
     (joined,) = local(
-        first_sum_kernel, [((tall, width), BF)], (), (total, far, far_cells, *parts)
+        "first", first_sum_kernel, [((tall, width), BF)], (), (total, far, far_cells, *parts)
     )
 
     opposite = swap(joined, "feat", top_bit)
     band_degree = after(band_degree, joined)
     if size:
         scale, head_scale = local(
+            "scale",
             scale_kernel,
             band_sum + [head_sum],
             (),
@@ -332,7 +356,7 @@
             [pltpu.VMEM((heads, width), F32)],
         )
     else:
-        (scale,) = local(wide_scale_kernel, band_sum, (), (band_degree[None, :],))
+        (scale,) = local("scale", wide_scale_kernel, band_sum, (), (band_degree[None, :],))
         head_scale = lax.rsqrt(head_degree.astype(F32))[:, None] * jnp.ones((1, width), F32)
         head_scale = lax.dynamic_slice_in_dim(head_scale, lax.axis_index("rows") * head_dev, head_dev, 0)
     pieces = spread("feat", after(joined, scale), low_bits)
@@ -343,16 +367,26 @@
     shards.update({k | top_bit: w for k, w in spread("feat", after(across, scale), low_bits).items()})
     order = [0, top_bit] + [k for k in sorted(shards) if k not in (0, top_bit)]
     begun = local(
+        "begin",
         functools.partial(mix_begin_kernel, early=early),
         [((tall, width), F32)] * 2,
         (),
         (after(pieces[0], opposite), *pieces[1:early], shards[0], shards[top_bit]),
     )
+    if len(order) > 2:
+        begun += local(
+            "mid",
+            functools.partial(mix_begin_kernel, early=early),
+            [((tall, width), F32)] * (len(order) - 2),
+            (),
+            (after(pieces[0], begun[0]), *pieces[1:early], *[shards[k] for k in order[2:]]),
+        )
     cells, *head_x = local(
+        "end",
         functools.partial(mix_end_kernel, early=early, order=order, head_dev=size),
         [cells_shape] + ([((size, width), BF)] if size else []),
         (),
-        (*pieces, *[shards[k] for k in order], *begun, mix_weights, scale, head_scale),
+        (*pieces[early:], *[shards[k] for k in order], *begun, mix_weights, scale, head_scale),
         [pltpu.VMEM((tall, width), F32)],
     )
     if not size:
@@ -362,20 +396,21 @@
         head_state = jnp.maximum(mm(summed, full) * head_scale[:, :1], 0.0).astype(BF)
         head_x = [mm(head_state, mix_weights[1]).astype(BF)]
 
-    pair_cells = swap(cells, "rows", 1)
-    keep, send = partial_sums(cells)
-    (total,) = local(near_kernel, band_sum, (), (after(near, keep), cells))
-    mine, theirs = gather_heads(after(head_x[0], keep), total)
-    far_cells = forward(after(pair_cells, mine))
-    parts = scatter_heads(keep, send, mine)
+    keep, send = partial_sums("part2", cells)
+    pair_cells = swap(after(cells, keep), "rows", 1)
+    (total,) = local("near", near_kernel, band_sum, (), (after(near, keep), cells))
+    halfway, mine, theirs = gather_heads("join2", after(head_x[0], keep), total)
+    far_cells = forward(after(pair_cells, halfway))
+    parts = scatter_heads("fold2", keep, send, mine)
     (total,) = local(
-        sum_up, band_sum, (), (after(total, *parts[:1]), pair, pair_cells, masked, mine, theirs), [head_scratch]
-    )
+        "sum2", sum_up, band_sum, (), (after(total, *parts[:1]), pair, pair_cells, masked, mine, theirs), [head_scratch]
+    )
+    (band_out,) = local("last", last_sum_kernel, band_sum, (), (total, far, far_cells, scale))
     if size:
-        (head_out,) = local(head_out_kernel, [head_sum], (), (after(parts[0], total), *parts[1:], head_scale))
+        own = after(parts[0], band_out)
+        (head_out,) = local("headout", head_out_kernel, [head_sum], (), (own, *parts[1:], head_scale))
     else:
         head_out = jnp.maximum(lax.psum_scatter(keep, "rows", scatter_dimension=0, tiled=True) * head_scale, 0.0)
-    (band_out,) = local(last_sum_kernel, band_sum, (), (total, far, far_cells, scale))
     return band_out, head_out
 
 

time: 64.7 us -> 58.4 us (0.903)
  waiting for transfers between devices: 31.4 us -> 18.9 us
  starting transfers between devices: 21.4 us -> 28.1 us
    ppermute x20, waiting for transfers between devices: 31.4 us -> 18.9 us  [swap(): return lax.ppermute(cells, axis, [(i, i ^ bit) for i in range(count)])]
    ppermute x20, starting transfers between devices: 19 us -> 26.6 us  [swap(): return lax.ppermute(cells, axis, [(i, i ^ bit) for i in range(count)])]
    ppermute x2, starting transfers between devices: 2.34 us -> 1.49 us  [forward(): return lax.ppermute(cells, 'rows', pairs)]
    pallas_call x21 -> x22, Pallas kernels: 9.03 us -> 8.54 us  [local(): pl.pallas_call(kernel, out_shape=[jax.ShapeDtypeStruct(s, d) for s, d in...]
  transfers between devices with their start and end apart: 22 -> 22, of which waited for: 12 -> 10; matrix products, arithmetic and copies ran while one was open for 0% -> 0% of each run, Pallas kernels for 9% -> 11%
where the time goes in v3:
time: 58.4 us; the launch traced here: 58.2 us
  starting transfers between devices  28.1 us (48%)
  waiting for transfers between devices  18.9 us (32%)
  Pallas kernels  8.54 us (15%)
  local copies, waits for them, and re-layouts  1.84 us (3%)
  between operations  0.88 us (2%)
    ppermute x20, starting transfers between devices, swap(): return lax.ppermute(cells, axis, [(i, i ^ bit) for i in range(count)])  26.6 us
    ppermute x20, waiting for transfers between devices, swap(): return lax.ppermute(cells, axis, [(i, i ^ bit) for i in range(count)])  18.9 us
    pallas_call x22, Pallas kernels, local(): pl.pallas_call(kernel, out_shape=[jax.ShapeDtypeStruct(s, d) for s, d in...  8.54 us
    unnamed x20, local copies, waits for them, and re-layouts  1.8 us
    ppermute x2, starting transfers between devices, forward(): return lax.ppermute(cells, 'rows', pairs)  1.49 us
  transfers between devices with their start and end apart: 22, of which 10 were waited for; matrix products, arithmetic and copies ran while one was open for 0% of the time, Pallas kernels for 11%

profile of v3, /device:TPU:0, one launch (start us, length us, event | category | flops | bytes accessed | tf_op | source)
XLA Modules:
  0.0 58.2 jit_solution(6806805363765377660)
XLA Ops:
  0.6 1.1 %copy-done.3 = f32[512,256]{1,0:T(8,128)S(1)} copy-done((f32[512,256]{1,0:T(8,128)S(1)}, f32[512,256]{1,0:T(8,128)}, u32[]{:S(2)}) %copy-start.3) | copy-done | bytes 524312
  1.8 0.0 copy-start
  1.8 3.0 %collective-permute-start.2 = (bf16[512,256]{1,0:T(8,128)(2,1)S(1)}, bf16[512,256]{1,0:T(8,128)(2,1)S(1)}, u32[]{:S(2)}, u32[]{:S(2)}) collective-permute-start(bf16[512,256]{1,0:T(8,128)(2,1)S(1)} %shard_map.113.cells), channel_id=1, source_target_pairs={{0,4},{4,0},{8,12},{12,8},{16,20},{20,16},{24,28},{28,24},{1,5},{5... | collective-permute-start | bytes 786440 | tf_op jit(solution)/shard_map/ppermute | solution.py:56
  4.8 0.3 shard_map.114
  5.1 0.8 %collective-permute-start = (bf16[256,256]{1,0:T(8,128)(2,1)S(1)}, bf16[256,256]{1,0:T(8,128)(2,1)S(1)}, u32[]{:S(2)}, u32[]{:S(2)}) collective-permute-start(bf16[256,256]{1,0:T(8,128)(2,1)S(1)} %get-tuple-element.57), channel_id=1, source_target_pairs={{0,4},{4,0},{8,12},{12,8},{16,20},{20,16},{24,28},{28,24},{1,5},{5... | collective-permute-start | bytes 393224 | tf_op jit(solution)/shard_map/ppermute | solution.py:56
  5.9 2.6 %collective-permute-start.3 = (bf16[64,256]{1,0:T(8,128)(2,1)S(1)}, bf16[64,256]{1,0:T(8,128)(2,1)S(1)}, u32[]{:S(2)}, u32[]{:S(2)}) collective-permute-start(bf16[64,256]{1,0:T(8,128)(2,1)S(1)} %get-tuple-element.66.refs_0_), channel_id=1, source_target_pairs={{0,16},{4,20},{8,24},{12,28},{16,0},{20,4},{24,8},{28,12},{1,17},{... | collective-permute-start | bytes 98312 | tf_op jit(solution)/shard_map/ppermute | solution.py:56
  8.6 1.6 %collective-permute-start.10 = (bf16[1024,256]{1,0:T(8,128)(2,1)S(1)}, bf16[1024,256]{1,0:T(8,128)(2,1)S(1)}, u32[]{:S(2)}, u32[]{:S(2)}) collective-permute-start(bf16[1024,256]{1,0:T(8,128)(2,1)S(1)} %slice_bitcast_fusion.refs_2_), channel_id=1, source_target_pairs={{0,2},{1,3},{2,0},{3,1},{4,6},{5,7},{6,4},{7,5},{8,10},{9,11},{10,... | collective-permute-start | bytes 1572872 | tf_op jit(solution)/shard_map/ppermute | solution.py:56
  10.2 0.7 %copy-done.6 = s32[32,3]{0,1:T(4,128)S(1)} copy-done((s32[32,3]{0,1:T(4,128)S(1)}, s32[32,3]{0,1:T(4,128)}, u32[]{:S(2)}) %copy-start.6) | copy-done | bytes 408
  10.8 2.1 %shard_map.115 = (bf16[512,512]{1,0:T(8,128)(2,1)S(1)}, bf16[512,512]{1,0:T(8,128)(2,1)S(1)}, bf16[512,512]{1,0:T(8,128)(2,1)S(1)}, bf16[512,512]{1,0:T(8,128)(2,1)S(1)}, f32[512,256]{1,0:T(8,128)S(1)}) custom-call(s32[3,32]{1,0:T(4,128)S(1)} %bitcast.6, bf16[32,128,128]{2,1,0:T(8,128)(2,1)S(1)} %copy-done.2, bf16[512,512]{1,0:T(8,128)(2,1)S(1)} %copy-done.4, ...), custom_call_target="tpu_custom_call" | custom-call | flops 500000000 | bytes 1837056 | tf_op jit(solution)/shard_map/pallas_call | solution.py:39
  13.0 1.7 %collective-permute-start.4 = (bf16[128,256]{1,0:T(8,128)(2,1)S(1)}, bf16[128,256]{1,0:T(8,128)(2,1)S(1)}, u32[]{:S(2)}, u32[]{:S(2)}) collective-permute-start(bf16[128,256]{1,0:T(8,128)(2,1)S(1)} %shard_map.118.refs_0_), channel_id=1, source_target_pairs={{0,8},{4,12},{8,0},{12,4},{16,24},{20,28},{24,16},{28,20},{1,9},{5... | collective-permute-start | bytes 196616 | tf_op jit(solution)/shard_map/ppermute | solution.py:56
  14.7 1.1 %collective-permute-start.1 = (bf16[128,256]{1,0:T(8,128)(2,1)S(1)}, bf16[128,256]{1,0:T(8,128)(2,1)S(1)}, u32[]{:S(2)}, u32[]{:S(2)}) collective-permute-start(bf16[128,256]{1,0:T(8,128)(2,1)S(1)} %get-tuple-element.60), channel_id=1, source_target_pairs={{0,8},{4,12},{8,0},{12,4},{16,24},{20,28},{24,16},{28,20},{1,9},{5... | collective-permute-start | bytes 196616 | tf_op jit(solution)/shard_map/ppermute | solution.py:56
  15.8 1.0 %collective-permute-start.6 = (bf16[512,256]{1,0:T(8,128)(2,1)S(1)}, bf16[512,256]{1,0:T(8,128)(2,1)S(1)}, u32[]{:S(2)}, u32[]{:S(2)}) collective-permute-start(bf16[512,256]{1,0:T(8,128)(2,1)S(1)} %collective-permute-done.2.cells), channel_id=1, source_target_pairs={{0,8},{4,0},{8,16},{12,4},{16,24},{20,12},{24,28},{28,20},{1,9},{5... | collective-permute-start | bytes 786440 | tf_op jit(solution)/shard_map/ppermute | solution.py:67
  16.8 0.7 %collective-permute-done.4.refs_1_ = bf16[128,256]{1,0:T(8,128)(2,1)S(1)} collective-permute-done((bf16[128,256]{1,0:T(8,128)(2,1)S(1)}, bf16[128,256]{1,0:T(8,128)(2,1)S(1)}, u32[]{:S(2)}, u32[]{:S(2)}) %collective-permute-start.4) | collective-permute-done | bytes 65568 | tf_op jit(solution)/shard_map/ppermute | solution.py:56
  17.5 1.4 %collective-permute-start.5 = (bf16[256,256]{1,0:T(8,128)(2,1)S(1)}, bf16[256,256]{1,0:T(8,128)(2,1)S(1)}, u32[]{:S(2)}, u32[]{:S(2)}) collective-permute-start(bf16[256,256]{1,0:T(8,128)(2,1)S(1)} %shard_map.119.mine), channel_id=1, source_target_pairs={{0,4},{4,0},{8,12},{12,8},{16,20},{20,16},{24,28},{28,24},{1,5},{5... | collective-permute-start | bytes 393224 | tf_op jit(solution)/shard_map/ppermute | solution.py:56
  18.9 0.1 collective-permute-done.1.arrived
  19.1 2.1 %collective-permute-start.7 = (bf16[64,256]{1,0:T(8,128)(2,1)S(1)}, bf16[64,256]{1,0:T(8,128)(2,1)S(1)}, u32[]{:S(2)}, u32[]{:S(2)}) collective-permute-start(bf16[64,256]{1,0:T(8,128)(2,1)S(1)} %get-tuple-element.70), channel_id=1, source_target_pairs={{0,16},{4,20},{8,24},{12,28},{16,0},{20,4},{24,8},{28,12},{1,17},{... | collective-permute-start | bytes 98312 | tf_op jit(solution)/shard_map/ppermute | solution.py:56
  21.2 4.3 %collective-permute-done.5.theirs = bf16[256,256]{1,0:T(8,128)(2,1)S(1)} collective-permute-done((bf16[256,256]{1,0:T(8,128)(2,1)S(1)}, bf16[256,256]{1,0:T(8,128)(2,1)S(1)}, u32[]{:S(2)}, u32[]{:S(2)}) %collective-permute-start.5) | collective-permute-done | bytes 131104 | tf_op jit(solution)/shard_map/ppermute | solution.py:56
  25.5 0.5 shard_map.120.total
  26.0 0.3 shard_map.121.refs_0_
  26.4 1.6 %collective-permute-start.8 = (bf16[576,256]{1,0:T(8,128)(2,1)S(1)}, bf16[576,256]{1,0:T(8,128)(2,1)S(1)}, u32[]{:S(2)}, u32[]{:S(2)}) collective-permute-start(bf16[576,256]{1,0:T(8,128)(2,1)S(1)} %shard_map.121.refs_0_), channel_id=1, source_target_pairs={{0,2},{1,3},{2,0},{3,1},{4,6},{5,7},{6,4},{7,5},{8,10},{9,11},{10,... | collective-permute-start | bytes 884744 | tf_op jit(solution)/shard_map/ppermute | solution.py:56
  28.0 0.2 shard_map.122
  28.2 0.1 collective-permute-start.12
  28.3 0.5 collective-permute-start.11
  28.8 0.1 collective-permute-start.13
  28.8 4.3 %collective-permute-done.8.refs_0_ = bf16[576,256]{1,0:T(8,128)(2,1)S(1)} collective-permute-done((bf16[576,256]{1,0:T(8,128)(2,1)S(1)}, bf16[576,256]{1,0:T(8,128)(2,1)S(1)}, u32[]{:S(2)}, u32[]{:S(2)}) %collective-permute-start.8) | collective-permute-done | bytes 294944 | tf_op jit(solution)/shard_map/ppermute | solution.py:56
  33.2 0.5 shard_map.123
  33.7 0.5 shard_map.124
  34.1 0.6 %collective-permute-done.9.refs_1_ = bf16[576,256]{1,0:T(8,128)(2,1)S(1)} collective-permute-done((bf16[576,256]{1,0:T(8,128)(2,1)S(1)}, bf16[576,256]{1,0:T(8,128)(2,1)S(1)}, u32[]{:S(2)}, u32[]{:S(2)}) %collective-permute-start.9) | collective-permute-done | bytes 294944 | tf_op jit(solution)/shard_map/ppermute | solution.py:56
  34.7 1.2 %shard_map.125 = (bf16[512,256]{1,0:T(8,128)(2,1)S(1)}, bf16[64,256]{1,0:T(8,128)(2,1)S(1)}) custom-call(bf16[576,256]{1,0:T(8,128)(2,1)S(1)} %collective-permute-done.8.refs_0_, bf16[576,256]{1,0:T(8,128)(2,1)S(1)} %collective-permute-done.9.refs_1_, bf16[1024,256]{1,0:T(8,128)(2,1)S(1)} %slice_bitcast_fusion.refs_2_, ...), custom_call_target="tpu_custom_call" | custom-call | flops 500000000 | bytes 6684672 | tf_op jit(solution)/shard_map/pallas_call | solution.py:39
  36.0 0.3 shard_map.126
  36.3 0.2 collective-permute-start.18
  36.5 2.0 %collective-permute-start.14 = (bf16[64,256]{1,0:T(8,128)(2,1)S(1)}, bf16[64,256]{1,0:T(8,128)(2,1)S(1)}, u32[]{:S(2)}, u32[]{:S(2)}) collective-permute-start(bf16[64,256]{1,0:T(8,128)(2,1)S(1)} %get-tuple-element.89.refs_0_), channel_id=1, source_target_pairs={{0,16},{4,20},{8,24},{12,28},{16,0},{20,4},{24,8},{28,12},{1,17},{... | collective-permute-start | bytes 98312 | tf_op jit(solution)/shard_map/ppermute | solution.py:56
  38.5 0.3 shard_map.127.total
  38.8 1.1 %collective-permute-start.16 = (bf16[256,256]{1,0:T(8,128)(2,1)S(1)}, bf16[256,256]{1,0:T(8,128)(2,1)S(1)}, u32[]{:S(2)}, u32[]{:S(2)}) collective-permute-start(bf16[256,256]{1,0:T(8,128)(2,1)S(1)} %get-tuple-element.92), channel_id=1, source_target_pairs={{0,4},{4,0},{8,12},{12,8},{16,20},{20,16},{24,28},{28,24},{1,5},{5... | collective-permute-start | bytes 393224 | tf_op jit(solution)/shard_map/ppermute | solution.py:56
  39.9 1.4 %collective-permute-done.14.refs_1_ = bf16[64,256]{1,0:T(8,128)(2,1)S(1)} collective-permute-done((bf16[64,256]{1,0:T(8,128)(2,1)S(1)}, bf16[64,256]{1,0:T(8,128)(2,1)S(1)}, u32[]{:S(2)}, u32[]{:S(2)}) %collective-permute-start.14) | collective-permute-done | bytes 32800 | tf_op jit(solution)/shard_map/ppermute | solution.py:56
  41.3 2.4 %collective-permute-start.15 = (bf16[128,256]{1,0:T(8,128)(2,1)S(1)}, bf16[128,256]{1,0:T(8,128)(2,1)S(1)}, u32[]{:S(2)}, u32[]{:S(2)}) collective-permute-start(bf16[128,256]{1,0:T(8,128)(2,1)S(1)} %shard_map.128.refs_0_), channel_id=1, source_target_pairs={{0,8},{4,12},{8,0},{12,4},{16,24},{20,28},{24,16},{28,20},{1,9},{5... | collective-permute-start | bytes 196616 | tf_op jit(solution)/shard_map/ppermute | solution.py:56
  43.7 1.8 %collective-permute-done.18.cells = bf16[512,256]{1,0:T(8,128)(2,1)S(1)} collective-permute-done((bf16[512,256]{1,0:T(8,128)(2,1)S(1)}, bf16[512,256]{1,0:T(8,128)(2,1)S(1)}, u32[]{:S(2)}, u32[]{:S(2)}) %collective-permute-start.18) | collective-permute-done | bytes 262176 | tf_op jit(solution)/shard_map/ppermute | solution.py:56
  45.5 0.5 collective-permute-start.20
  46.0 2.3 %collective-permute-start.19 = (bf16[256,256]{1,0:T(8,128)(2,1)S(1)}, bf16[256,256]{1,0:T(8,128)(2,1)S(1)}, u32[]{:S(2)}, u32[]{:S(2)}) collective-permute-start(bf16[256,256]{1,0:T(8,128)(2,1)S(1)} %shard_map.129.mine), channel_id=1, source_target_pairs={{0,4},{4,0},{8,12},{12,8},{16,20},{20,16},{24,28},{28,24},{1,5},{5... | collective-permute-start | bytes 393224 | tf_op jit(solution)/shard_map/ppermute | solution.py:56
  48.3 0.0 collective-permute-done.16.arrived
  48.4 0.2 collective-permute-start.17
  48.5 4.2 %collective-permute-done.17.arrived = bf16[128,256]{1,0:T(8,128)(2,1)S(1)} collective-permute-done((bf16[128,256]{1,0:T(8,128)(2,1)S(1)}, bf16[128,256]{1,0:T(8,128)(2,1)S(1)}, u32[]{:S(2)}, u32[]{:S(2)}) %collective-permute-start.17) | collective-permute-done | bytes 65568 | tf_op jit(solution)/shard_map/ppermute | solution.py:56
  52.7 1.9 %collective-permute-start.21 = (bf16[64,256]{1,0:T(8,128)(2,1)S(1)}, bf16[64,256]{1,0:T(8,128)(2,1)S(1)}, u32[]{:S(2)}, u32[]{:S(2)}) collective-permute-start(bf16[64,256]{1,0:T(8,128)(2,1)S(1)} %get-tuple-element.101), channel_id=1, source_target_pairs={{0,16},{4,20},{8,24},{12,28},{16,0},{20,4},{24,8},{28,12},{1,17},{... | collective-permute-start | bytes 98312 | tf_op jit(solution)/shard_map/ppermute | solution.py:56
  54.6 1.3 %collective-permute-done.19.theirs = bf16[256,256]{1,0:T(8,128)(2,1)S(1)} collective-permute-done((bf16[256,256]{1,0:T(8,128)(2,1)S(1)}, bf16[256,256]{1,0:T(8,128)(2,1)S(1)}, u32[]{:S(2)}, u32[]{:S(2)}) %collective-permute-start.19) | collective-permute-done | bytes 131104 | tf_op jit(solution)/shard_map/ppermute | solution.py:56
  56.0 0.5 shard_map.132.total
  56.4 1.1 %shard_map.133 = f32[512,256]{1,0:T(8,128)} custom-call(f32[512,256]{1,0:T(8,128)S(1)} %shard_map.132.total, bf16[512,512]{1,0:T(8,128)(2,1)S(1)} %get-tuple-element.68.far, bf16[512,256]{1,0:T(8,128)(2,1)S(1)} %collective-permute-done.20.other, f32[512,256]{1,0:T(8,128)S(1)} %get-tuple-element.73.refs_11_.scale), custom_call_target="tpu_custom_call" | custom-call | flops 500000000 | bytes 1835008 | tf_op jit(solution)/shard_map/pallas_call | solution.py:39
  57.5 0.1 collective-permute-done.21.refs_0_
  57.6 0.6 %shard_map.134 = f32[64,256]{1,0:T(8,128)} custom-call(f32[64,256]{1,0:T(8,128)S(1)} %get-tuple-element.100.own, bf16[64,256]{1,0:T(8,128)(2,1)S(1)} %collective-permute-done.21.refs_0_, f32[64,256]{1,0:T(8,128)S(1)} %get-tuple-element.83.refs_12_.refs_1_), custom_call_target="tpu_custom_call" | custom-call | flops 1000000 | bytes 163840 | tf_op jit(solution)/shard_map/pallas_call | solution.py:39
  (39 shorter events, 0.2 us)
Async XLA Ops:
  0.6 4.2 %copy-start.1 = (bf16[512,512]{1,0:T(8,128)(2,1)S(1)}, bf16[512,512]{1,0:T(8,128)(2,1)}, u32[]{:S(2)}) copy-start(bf16[512,512]{1,0:T(8,128)(2,1)} %rows.3) | copy-start | bytes 1572868
  0.6 1.1 %copy-start.3 = (f32[512,256]{1,0:T(8,128)S(1)}, f32[512,256]{1,0:T(8,128)}, u32[]{:S(2)}) copy-start(f32[512,256]{1,0:T(8,128)} %cells.1) | copy-start | bytes 1572868
  1.7 3.1 %copy-start.5 = (f32[64,256]{1,0:T(8,128)S(1)}, f32[64,256]{1,0:T(8,128)}, u32[]{:S(2)}) copy-start(f32[64,256]{1,0:T(8,128)} %refs_0_.1) | copy-start | bytes 196612
  1.8 6.8 %copy-start = (bf16[2,1024,256]{2,1,0:T(8,128)(2,1)S(1)}, bf16[2,1024,256]{2,1,0:T(8,128)(2,1)}, u32[]{:S(2)}) copy-start(bf16[2,1024,256]{2,1,0:T(8,128)(2,1)} %refs_10_.1) | copy-start | bytes 3145732
  1.8 8.4 %copy-start.2 = (bf16[32,128,128]{2,1,0:T(8,128)(2,1)S(1)}, bf16[32,128,128]{2,1,0:T(8,128)(2,1)}, u32[]{:S(2)}) copy-start(bf16[32,128,128]{2,1,0:T(8,128)(2,1)} %tiles.1) | copy-start | bytes 3145732
  1.8 14.0 %collective-permute-start.2 = (bf16[512,256]{1,0:T(8,128)(2,1)S(1)}, bf16[512,256]{1,0:T(8,128)(2,1)S(1)}, u32[]{:S(2)}, u32[]{:S(2)}) collective-permute-start(bf16[512,256]{1,0:T(8,128)(2,1)S(1)} %shard_map.113.cells), channel_id=1, source_target_pairs={{0,4},{4,0},{8,12},{12,8},{16,20},{20,16},{24,28},{28,24},{1,5},{5... | collective-permute-start | bytes 786440 | tf_op jit(solution)/shard_map/ppermute | solution.py:56
  5.1 9.6 %collective-permute-start = (bf16[256,256]{1,0:T(8,128)(2,1)S(1)}, bf16[256,256]{1,0:T(8,128)(2,1)S(1)}, u32[]{:S(2)}, u32[]{:S(2)}) collective-permute-start(bf16[256,256]{1,0:T(8,128)(2,1)S(1)} %get-tuple-element.57), channel_id=1, source_target_pairs={{0,4},{4,0},{8,12},{12,8},{16,20},{20,16},{24,28},{28,24},{1,5},{5... | collective-permute-start | bytes 393224 | tf_op jit(solution)/shard_map/ppermute | solution.py:56
  5.9 4.2 %copy-start.4 = (bf16[512,512]{1,0:T(8,128)(2,1)S(1)}, bf16[512,512]{1,0:T(8,128)(2,1)}, u32[]{:S(2)}) copy-start(bf16[512,512]{1,0:T(8,128)(2,1)} %cols.1) | copy-start | bytes 1572868
  5.9 7.0 %collective-permute-start.3 = (bf16[64,256]{1,0:T(8,128)(2,1)S(1)}, bf16[64,256]{1,0:T(8,128)(2,1)S(1)}, u32[]{:S(2)}, u32[]{:S(2)}) collective-permute-start(bf16[64,256]{1,0:T(8,128)(2,1)S(1)} %get-tuple-element.66.refs_0_), channel_id=1, source_target_pairs={{0,16},{4,20},{8,24},{12,28},{16,0},{20,4},{24,8},{28,12},{1,17},{... | collective-permute-start | bytes 98312 | tf_op jit(solution)/shard_map/ppermute | solution.py:56
  8.5 1.6 %copy-start.7 = (s32[512]{0:T(512)S(1)}, s32[512]{0:T(512)}, u32[]{:S(2)}) copy-start(s32[512]{0:T(512)} %param.16) | copy-start | bytes 6148
  8.6 19.6 %collective-permute-start.10 = (bf16[1024,256]{1,0:T(8,128)(2,1)S(1)}, bf16[1024,256]{1,0:T(8,128)(2,1)S(1)}, u32[]{:S(2)}, u32[]{:S(2)}) collective-permute-start(bf16[1024,256]{1,0:T(8,128)(2,1)S(1)} %slice_bitcast_fusion.refs_2_), channel_id=1, source_target_pairs={{0,2},{1,3},{2,0},{3,1},{4,6},{5,7},{6,4},{7,5},{8,10},{9,11},{10,... | collective-permute-start | bytes 1572872 | tf_op jit(solution)/shard_map/ppermute | solution.py:56
  10.2 0.7 %copy-start.6 = (s32[32,3]{0,1:T(4,128)S(1)}, s32[32,3]{0,1:T(4,128)}, u32[]{:S(2)}) copy-start(s32[32,3]{0,1:T(4,128)} %param.13) | copy-start | bytes 1156
  13.0 4.5 %collective-permute-start.4 = (bf16[128,256]{1,0:T(8,128)(2,1)S(1)}, bf16[128,256]{1,0:T(8,128)(2,1)S(1)}, u32[]{:S(2)}, u32[]{:S(2)}) collective-permute-start(bf16[128,256]{1,0:T(8,128)(2,1)S(1)} %shard_map.118.refs_0_), channel_id=1, source_target_pairs={{0,8},{4,12},{8,0},{12,4},{16,24},{20,28},{24,16},{28,20},{1,9},{5... | collective-permute-start | bytes 196616 | tf_op jit(solution)/shard_map/ppermute | solution.py:56
  14.7 4.3 %collective-permute-start.1 = (bf16[128,256]{1,0:T(8,128)(2,1)S(1)}, bf16[128,256]{1,0:T(8,128)(2,1)S(1)}, u32[]{:S(2)}, u32[]{:S(2)}) collective-permute-start(bf16[128,256]{1,0:T(8,128)(2,1)S(1)} %get-tuple-element.60), channel_id=1, source_target_pairs={{0,8},{4,12},{8,0},{12,4},{16,24},{20,28},{24,16},{28,20},{1,9},{5... | collective-permute-start | bytes 196616 | tf_op jit(solution)/shard_map/ppermute | solution.py:56
  15.8 10.2 %collective-permute-start.6 = (bf16[512,256]{1,0:T(8,128)(2,1)S(1)}, bf16[512,256]{1,0:T(8,128)(2,1)S(1)}, u32[]{:S(2)}, u32[]{:S(2)}) collective-permute-start(bf16[512,256]{1,0:T(8,128)(2,1)S(1)} %collective-permute-done.2.cells), channel_id=1, source_target_pairs={{0,8},{4,0},{8,16},{12,4},{16,24},{20,12},{24,28},{28,20},{1,9},{5... | collective-permute-start | bytes 786440 | tf_op jit(solution)/shard_map/ppermute | solution.py:67
  17.5 8.0 %collective-permute-start.5 = (bf16[256,256]{1,0:T(8,128)(2,1)S(1)}, bf16[256,256]{1,0:T(8,128)(2,1)S(1)}, u32[]{:S(2)}, u32[]{:S(2)}) collective-permute-start(bf16[256,256]{1,0:T(8,128)(2,1)S(1)} %shard_map.119.mine), channel_id=1, source_target_pairs={{0,4},{4,0},{8,12},{12,8},{16,20},{20,16},{24,28},{28,24},{1,5},{5... | collective-permute-start | bytes 393224 | tf_op jit(solution)/shard_map/ppermute | solution.py:56
  19.1 6.9 %collective-permute-start.7 = (bf16[64,256]{1,0:T(8,128)(2,1)S(1)}, bf16[64,256]{1,0:T(8,128)(2,1)S(1)}, u32[]{:S(2)}, u32[]{:S(2)}) collective-permute-start(bf16[64,256]{1,0:T(8,128)(2,1)S(1)} %get-tuple-element.70), channel_id=1, source_target_pairs={{0,16},{4,20},{8,24},{12,28},{16,0},{20,4},{24,8},{28,12},{1,17},{... | collective-permute-start | bytes 98312 | tf_op jit(solution)/shard_map/ppermute | solution.py:56
  26.0 1.9 %copy-start.9 = (s32[512]{0:T(512)S(1)}, s32[512]{0:T(512)}, u32[]{:S(2)}) copy-start(s32[512]{0:T(512)} %param.19) | copy-start | bytes 6148
  26.4 1.6 %copy-start.8 = (s32[512]{0:T(512)S(1)}, s32[512]{0:T(512)}, u32[]{:S(2)}) copy-start(s32[512]{0:T(512)} %param.18) | copy-start | bytes 6148
  26.4 6.8 %collective-permute-start.8 = (bf16[576,256]{1,0:T(8,128)(2,1)S(1)}, bf16[576,256]{1,0:T(8,128)(2,1)S(1)}, u32[]{:S(2)}, u32[]{:S(2)}) collective-permute-start(bf16[576,256]{1,0:T(8,128)(2,1)S(1)} %shard_map.121.refs_0_), channel_id=1, source_target_pairs={{0,2},{1,3},{2,0},{3,1},{4,6},{5,7},{6,4},{7,5},{8,10},{9,11},{10,... | collective-permute-start | bytes 884744 | tf_op jit(solution)/shard_map/ppermute | solution.py:56
  28.2 5.5 %collective-permute-start.12 = (bf16[1024,256]{1,0:T(8,128)(2,1)S(1)}, bf16[1024,256]{1,0:T(8,128)(2,1)S(1)}, u32[]{:S(2)}, u32[]{:S(2)}) collective-permute-start(bf16[1024,256]{1,0:T(8,128)(2,1)S(1)} %collective-permute-done.10.refs_3_), channel_id=1, source_target_pairs={{0,1},{1,0},{2,3},{3,2},{4,5},{5,4},{6,7},{7,6},{8,9},{9,8},{10,11... | collective-permute-start | bytes 1572872 | tf_op jit(solution)/shard_map/ppermute | solution.py:56
  28.3 5.4 %collective-permute-start.11 = (bf16[1024,256]{1,0:T(8,128)(2,1)S(1)}, bf16[1024,256]{1,0:T(8,128)(2,1)S(1)}, u32[]{:S(2)}, u32[]{:S(2)}) collective-permute-start(bf16[1024,256]{1,0:T(8,128)(2,1)S(1)} %slice_bitcast_fusion.refs_2_), channel_id=1, source_target_pairs={{0,1},{1,0},{2,3},{3,2},{4,5},{5,4},{6,7},{7,6},{8,9},{9,8},{10,11... | collective-permute-start | bytes 1572872 | tf_op jit(solution)/shard_map/ppermute | solution.py:56
  28.8 4.4 %collective-permute-start.13 = (bf16[576,256]{1,0:T(8,128)(2,1)S(1)}, bf16[576,256]{1,0:T(8,128)(2,1)S(1)}, u32[]{:S(2)}, u32[]{:S(2)}) collective-permute-start(bf16[576,256]{1,0:T(8,128)(2,1)S(1)} %shard_map.121.refs_0_), channel_id=1, source_target_pairs={{0,1},{1,0},{2,3},{3,2},{4,5},{5,4},{6,7},{7,6},{8,9},{9,8},{10,11... | collective-permute-start | bytes 884744 | tf_op jit(solution)/shard_map/ppermute | solution.py:56
  33.2 1.6 %collective-permute-start.9 = (bf16[576,256]{1,0:T(8,128)(2,1)S(1)}, bf16[576,256]{1,0:T(8,128)(2,1)S(1)}, u32[]{:S(2)}, u32[]{:S(2)}) collective-permute-start(bf16[576,256]{1,0:T(8,128)(2,1)S(1)} %collective-permute-done.8.refs_0_), channel_id=1, source_target_pairs={{0,1},{1,0},{2,3},{3,2},{4,5},{5,4},{6,7},{7,6},{8,9},{9,8},{10,11... | collective-permute-start | bytes 884744 | tf_op jit(solution)/shard_map/ppermute | solution.py:56
  36.3 9.2 %collective-permute-start.18 = (bf16[512,256]{1,0:T(8,128)(2,1)S(1)}, bf16[512,256]{1,0:T(8,128)(2,1)S(1)}, u32[]{:S(2)}, u32[]{:S(2)}) collective-permute-start(bf16[512,256]{1,0:T(8,128)(2,1)S(1)} %get-tuple-element.98.cells), channel_id=1, source_target_pairs={{0,4},{4,0},{8,12},{12,8},{16,20},{20,16},{24,28},{28,24},{1,5},{5... | collective-permute-start | bytes 786440 | tf_op jit(solution)/shard_map/ppermute | solution.py:56
  36.5 4.8 %collective-permute-start.14 = (bf16[64,256]{1,0:T(8,128)(2,1)S(1)}, bf16[64,256]{1,0:T(8,128)(2,1)S(1)}, u32[]{:S(2)}, u32[]{:S(2)}) collective-permute-start(bf16[64,256]{1,0:T(8,128)(2,1)S(1)} %get-tuple-element.89.refs_0_), channel_id=1, source_target_pairs={{0,16},{4,20},{8,24},{12,28},{16,0},{20,4},{24,8},{28,12},{1,17},{... | collective-permute-start | bytes 98312 | tf_op jit(solution)/shard_map/ppermute | solution.py:56
  38.8 9.5 %collective-permute-start.16 = (bf16[256,256]{1,0:T(8,128)(2,1)S(1)}, bf16[256,256]{1,0:T(8,128)(2,1)S(1)}, u32[]{:S(2)}, u32[]{:S(2)}) collective-permute-start(bf16[256,256]{1,0:T(8,128)(2,1)S(1)} %get-tuple-element.92), channel_id=1, source_target_pairs={{0,4},{4,0},{8,12},{12,8},{16,20},{20,16},{24,28},{28,24},{1,5},{5... | collective-permute-start | bytes 393224 | tf_op jit(solution)/shard_map/ppermute | solution.py:56
  41.3 4.7 %collective-permute-start.15 = (bf16[128,256]{1,0:T(8,128)(2,1)S(1)}, bf16[128,256]{1,0:T(8,128)(2,1)S(1)}, u32[]{:S(2)}, u32[]{:S(2)}) collective-permute-start(bf16[128,256]{1,0:T(8,128)(2,1)S(1)} %shard_map.128.refs_0_), channel_id=1, source_target_pairs={{0,8},{4,12},{8,0},{12,4},{16,24},{20,28},{24,16},{28,20},{1,9},{5... | collective-permute-start | bytes 196616 | tf_op jit(solution)/shard_map/ppermute | solution.py:56
  45.5 10.9 %collective-permute-start.20 = (bf16[512,256]{1,0:T(8,128)(2,1)S(1)}, bf16[512,256]{1,0:T(8,128)(2,1)S(1)}, u32[]{:S(2)}, u32[]{:S(2)}) collective-permute-start(bf16[512,256]{1,0:T(8,128)(2,1)S(1)} %collective-permute-done.18.cells), channel_id=1, source_target_pairs={{0,8},{4,0},{8,16},{12,4},{16,24},{20,12},{24,28},{28,20},{1,9},{5... | collective-permute-start | bytes 786440 | tf_op jit(solution)/shard_map/ppermute | solution.py:67
  46.0 9.9 %collective-permute-start.19 = (bf16[256,256]{1,0:T(8,128)(2,1)S(1)}, bf16[256,256]{1,0:T(8,128)(2,1)S(1)}, u32[]{:S(2)}, u32[]{:S(2)}) collective-permute-start(bf16[256,256]{1,0:T(8,128)(2,1)S(1)} %shard_map.129.mine), channel_id=1, source_target_pairs={{0,4},{4,0},{8,12},{12,8},{16,20},{20,16},{24,28},{28,24},{1,5},{5... | collective-permute-start | bytes 393224 | tf_op jit(solution)/shard_map/ppermute | solution.py:56
  48.4 4.3 %collective-permute-start.17 = (bf16[128,256]{1,0:T(8,128)(2,1)S(1)}, bf16[128,256]{1,0:T(8,128)(2,1)S(1)}, u32[]{:S(2)}, u32[]{:S(2)}) collective-permute-start(bf16[128,256]{1,0:T(8,128)(2,1)S(1)} %get-tuple-element.95), channel_id=1, source_target_pairs={{0,8},{4,12},{8,0},{12,4},{16,24},{20,28},{24,16},{28,20},{1,9},{5... | collective-permute-start | bytes 196616 | tf_op jit(solution)/shard_map/ppermute | solution.py:56
  52.7 4.9 %collective-permute-start.21 = (bf16[64,256]{1,0:T(8,128)(2,1)S(1)}, bf16[64,256]{1,0:T(8,128)(2,1)S(1)}, u32[]{:S(2)}, u32[]{:S(2)}) collective-permute-start(bf16[64,256]{1,0:T(8,128)(2,1)S(1)} %get-tuple-element.101), channel_id=1, source_target_pairs={{0,16},{4,20},{8,24},{12,28},{16,0},{20,4},{24,8},{28,12},{1,17},{... | collective-permute-start | bytes 98312 | tf_op jit(solution)/shard_map/ppermute | solution.py:56

commit v4 on v3

--- a/solution.py
+++ b/solution.py
@@ -11,9 +11,9 @@
 F32 = jnp.float32
 LIMIT = 16 * 1024 * 1024
 WORK = {
-    "cast": 500_000_000,
-    "part1": 500_000_000,
-    "dense": 500_000_000,
+    "cast": 1_000_000,
+    "part1": 4_000_000_000,
+    "dense": 1_000_000,
     "join1": 500_000_000,
     "fold1": 2_000_000_000,
     "sum1": 1_000_000,
@@ -25,10 +25,13 @@
     "part2": 1_000_000,
     "near": 500_000_000,
     "join2": 500_000_000,
-    "fold2": 500_000_000,
+    "fold2": 1_000_000,
     "sum2": 500_000_000,
     "last": 500_000_000,
     "headout": 1_000_000,
+    "collect": 500_000_000,
+    "join3": 500_000_000,
+    "headmix": 500_000_000,
 }
 
 
@@ -93,29 +96,32 @@
     return order
 
 
-def split_partial(part, keep, send, head_dev):
+def split_partial(part, keep, send, head_dev, bits):
     if not head_dev:
         keep[...] = part[...]
         send[...] = part[...].astype(BF)
         return
-    pair, parity = lax.axis_index("rows") // 2, lax.axis_index("rows") % 2
-    for n, k in enumerate(xor_order(keep.shape[0] // head_dev)):
-        mine = pl.multiple_of((2 * (pair ^ k) + parity) * head_dev, head_dev)
-        theirs = pl.multiple_of((2 * (pair ^ k) + 1 - parity) * head_dev, head_dev)
-        keep[n * head_dev : (n + 1) * head_dev] = part[pl.ds(mine, head_dev)]
-        send[n * head_dev : (n + 1) * head_dev] = part[pl.ds(theirs, head_dev)].astype(BF)
+    half = len(bits) - 1
+    for n in range(2 << half):
+        owner = lax.axis_index("rows") ^ sum(bit for i, bit in enumerate(bits) if n >> (half - i) & 1)
+        rows = part[pl.ds(pl.multiple_of(owner * head_dev, head_dev), head_dev)]
+        if n < 1 << half:
+            keep[n * head_dev : (n + 1) * head_dev] = rows
+        else:
+            n -= 1 << half
+            send[n * head_dev : (n + 1) * head_dev] = rows.astype(BF)
 
 
 def cast_kernel(cells, out):
     out[...] = cells[...].astype(BF)
 
 
-def partial_kernel(rows, cells, *refs, head_dev):
+def partial_kernel(rows, cells, *refs, head_dev, bits):
     keep, send, part = refs[-3:]
     if len(refs) > 3:
         refs[1][...] = refs[0][...].astype(BF)
     part[...] = mm(rows[...], cells[...])
-    split_partial(part, keep, send, head_dev)
+    split_partial(part, keep, send, head_dev, bits)
 
 
 def dense_kernel(place, tiles, cols, reach, cells, near, pair, far, masked, own, window, *, blocks):
@@ -278,6 +284,8 @@
     reach = arrow_reach[None, :]
     size = head_dev if pairs <= 4 and head_dev % 16 == 0 else 0
     part_rows = heads // 2 if size else heads
+    index_bits = [1 << n for n in range(blocks.bit_length() - 1)]
+    bits, last_bits = [*index_bits[1:2], index_bits[0], *index_bits[2:]], [*index_bits[1:2], index_bits[0], *index_bits[2:]]
     part_scratch = pltpu.VMEM((heads, width), F32)
     head_scratch = pltpu.VMEM((heads, width), BF)
     band_sum = [((rows_dev, width), F32)]
@@ -286,56 +294,63 @@
     keep_shapes = [((part_rows, width), F32), ((part_rows, width), BF)]
     sum_up = functools.partial(sum_kernel, head_dev=size)
 
-    def partial_sums(name, cells, *head):
+    def partial_sums(name, bits, cells, *head):
         outs = [(h.shape, BF) for h in head] + keep_shapes
-        add_up = functools.partial(partial_kernel, head_dev=size)
+        add_up = functools.partial(partial_kernel, head_dev=size, bits=bits)
         return local(name, add_up, outs, (), (arrow_rows, cells, *head), [part_scratch])
 
-    def gather_heads(name, own, before):
+    def join(name, mine, other, before):
+        shape = ((2 * mine.shape[0], width), BF)
+        return local(name, join_kernel, [shape], (), (after(mine, before), other))[0]
+
+    def fold(name, keep, arrived, before):
+        rows = keep.shape[0] // 2
+        outs = [((rows, width), F32), ((rows, width), BF)]
+        return local(name, fold_kernel, outs, (), (after(keep, before), arrived))
+
+    def exchange(joining, folding, own, keep, send, before, bits, turns, pause, between):
         if not size:
+            between(before)
             everyone = lax.all_gather(own, "rows", axis=0, tiled=True)
-            return everyone, everyone, everyone
-        mine, halfway = own, None
-        bit = pairs // 2
-        while bit:
-            other = swap(mine, "rows", 2 * bit)
-            rows = 2 * mine.shape[0]
-            (mine,) = local(name, join_kernel, [((rows, width), BF)], (), (after(mine, before), other))
-            halfway = mine if halfway is None else halfway
-            bit //= 2
-        return halfway, mine, swap(mine, "rows", 1)
-
-    def scatter_heads(name, keep, send, before):
-        if not size:
-            return []
-        bit = 1
-        while bit <= pairs:
-            arrived = swap(send, "rows", bit)
-            if bit < pairs:
-                rows = keep.shape[0] // 2
-                outs = [((rows, width), F32), ((rows, width), BF)]
-                keep, send = local(name, fold_kernel, outs, (), (after(keep, before), arrived))
-            bit *= 2
-        return [keep, arrived]
+            return everyone, everyone, []
+        mine, gathers, halves = own, list(index_bits[:0:-1]), list(bits)
+        other = swap(mine, "rows", gathers.pop(0))
+        arrived = swap(send, "rows", halves.pop(0))
+        for n, turn in enumerate(turns):
+            if n == pause:
+                before = between(before)
+            if turn == "j":
+                mine = before = join(joining, mine, other, before)
+                other = swap(mine, "rows", gathers.pop(0) if gathers else 1)
+            else:
+                keep, send = fold(folding, keep, arrived, before)
+                before = keep
+                arrived = swap(send, "rows", halves.pop(0))
+        if pause == len(turns):
+            between(before)
+        return mine, other, [keep, arrived]
 
     (cells,) = local("cast", cast_kernel, [cells_shape], (), (band_feats,))
     pair_cells = swap(cells, "rows", 1)
     first = after(mix_weights, cells)[0]
     across = swap(first, "feat", top_bit)
-    head_cells, keep, send = partial_sums("part1", cells, head_feats)
+    head_cells, keep, send = partial_sums("part1", bits, cells, head_feats)
     first_part = keep
-    near, pair, far, masked, total = local(
-        "dense",
-        functools.partial(dense_kernel, blocks=blocks),
-        [((rows_dev, rows_dev), BF)] * 3 + [((rows_dev, heads), BF), ((rows_dev, width), F32)],
-        (tile_place.T,),
-        (tile_vals, arrow_cols, reach, after(cells, keep)),
-        [pltpu.VMEM((rows_dev, 3 * rows_dev), F32)],
-    )
-    halfway, mine, theirs = gather_heads("join1", head_cells, total)
-    far_cells = forward(after(pair_cells, total))
-    parts = scatter_heads("fold1", keep, send, total)
-    total = after(total, *parts[:1])
+    laid = []
+
+    def lay_out(before):
+        outs = [((rows_dev, rows_dev), BF)] * 3 + [((rows_dev, heads), BF)] + band_sum
+        args = (tile_vals, arrow_cols, reach, after(cells, before))
+        scratch = [pltpu.VMEM((rows_dev, 3 * rows_dev), F32)]
+        kernel = functools.partial(dense_kernel, blocks=blocks)
+        laid.extend(local("dense", kernel, outs, (tile_place.T,), args, scratch))
+        return laid[-1]
+
+    mine, theirs, parts = exchange(
+        "join1", "fold1", head_cells, keep, send, keep, bits, "jfjf", 3, lay_out
+    )
+    near, pair, far, masked, total = laid
+    far_cells = forward(after(pair_cells, first_part))
     (total,) = local(
         "sum1", sum_up, band_sum, (), (total, pair, pair_cells, masked, mine, theirs), [head_scratch]
     )
@@ -396,12 +411,19 @@
         head_state = jnp.maximum(mm(summed, full) * head_scale[:, :1], 0.0).astype(BF)
         head_x = [mm(head_state, mix_weights[1]).astype(BF)]
 
-    keep, send = partial_sums("part2", cells)
-    pair_cells = swap(after(cells, keep), "rows", 1)
-    (total,) = local("near", near_kernel, band_sum, (), (after(near, keep), cells))
-    halfway, mine, theirs = gather_heads("join2", after(head_x[0], keep), total)
-    far_cells = forward(after(pair_cells, halfway))
-    parts = scatter_heads("fold2", keep, send, mine)
+    pair_cells = swap(cells, "rows", 1)
+    keep, send = partial_sums("part2", last_bits, cells)
+    sums = []
+
+    def multiply(before):
+        sums.extend(local("near", near_kernel, band_sum, (), (after(near, before), cells)))
+        return sums[-1]
+
+    mine, theirs, parts = exchange(
+        "join2", "fold2", after(head_x[0], keep), keep, send, keep, last_bits, "fjfj", 0, multiply
+    )
+    (total,) = sums
+    far_cells = forward(after(pair_cells, total))
     (total,) = local(
         "sum2", sum_up, band_sum, (), (after(total, *parts[:1]), pair, pair_cells, masked, mine, theirs), [head_scratch]
     )

time: 58.4 us -> 56.7 us (0.971)
  starting transfers between devices: 28.1 us -> 27.4 us
  local copies, waits for them, and re-layouts: 1.84 us -> 1.19 us
    ppermute x20, starting transfers between devices: 26.6 us -> 23.6 us  [swap(): return lax.ppermute(cells, axis, [(i, i ^ bit) for i in range(count)])]
    ppermute x2, starting transfers between devices: 1.49 us -> 3.82 us  [forward(): return lax.ppermute(cells, 'rows', pairs)]
    unnamed x20, local copies, waits for them, and re-layouts: 1.8 us -> 1.16 us
  transfers between devices with their start and end apart: 22 -> 22, of which waited for: 10 -> 8; matrix products, arithmetic and copies ran while one was open for 0% -> 0% of each run, Pallas kernels for 11% -> 12%
where the time goes in v4:
time: 56.7 us; the launch traced here: 56.5 us
  starting transfers between devices  27.4 us (48%)
  waiting for transfers between devices  18.5 us (33%)
  Pallas kernels  8.47 us (15%)
  local copies, waits for them, and re-layouts  1.19 us (2%)
  between operations  0.89 us (2%)
    ppermute x20, starting transfers between devices, swap(): return lax.ppermute(cells, axis, [(i, i ^ bit) for i in range(count)])  23.6 us
    ppermute x20, waiting for transfers between devices, swap(): return lax.ppermute(cells, axis, [(i, i ^ bit) for i in range(count)])  18.5 us
    pallas_call x22, Pallas kernels, local(): pl.pallas_call(kernel, out_shape=[jax.ShapeDtypeStruct(s, d) for s, d in...  8.47 us
    ppermute x2, starting transfers between devices, forward(): return lax.ppermute(cells, 'rows', pairs)  3.82 us
    unnamed x20, local copies, waits for them, and re-layouts  1.16 us
  transfers between devices with their start and end apart: 22, of which 8 were waited for; matrix products, arithmetic and copies ran while one was open for 0% of the time, Pallas kernels for 12%

profile of v4, /device:TPU:0, one launch (start us, length us, event | category | flops | bytes accessed | tf_op | source)
XLA Modules:
  0.0 56.5 jit_solution(594489736138098783)
XLA Ops:
  0.6 1.0 %copy-done.3 = f32[512,256]{1,0:T(8,128)S(1)} copy-done((f32[512,256]{1,0:T(8,128)S(1)}, f32[512,256]{1,0:T(8,128)}, u32[]{:S(2)}) %copy-start.3) | copy-done | bytes 524312
  1.7 0.0 copy-start
  1.7 3.0 %collective-permute-start.3 = (bf16[512,256]{1,0:T(8,128)(2,1)S(1)}, bf16[512,256]{1,0:T(8,128)(2,1)S(1)}, u32[]{:S(2)}, u32[]{:S(2)}) collective-permute-start(bf16[512,256]{1,0:T(8,128)(2,1)S(1)} %shard_map.113.cells), channel_id=1, source_target_pairs={{0,4},{4,0},{8,12},{12,8},{16,20},{20,16},{24,28},{28,24},{1,5},{5... | collective-permute-start | bytes 786440 | tf_op jit(solution)/shard_map/ppermute | solution.py:59
  4.7 0.3 shard_map.114
  5.1 2.7 %collective-permute-start = (bf16[64,256]{1,0:T(8,128)(2,1)S(1)}, bf16[64,256]{1,0:T(8,128)(2,1)S(1)}, u32[]{:S(2)}, u32[]{:S(2)}) collective-permute-start(bf16[64,256]{1,0:T(8,128)(2,1)S(1)} %get-tuple-element.52.refs_0_), channel_id=1, source_target_pairs={{0,16},{4,20},{8,24},{12,28},{16,0},{20,4},{24,8},{28,12},{1,17},{... | collective-permute-start | bytes 98312 | tf_op jit(solution)/shard_map/ppermute | solution.py:59
  7.7 1.6 %collective-permute-start.1 = (bf16[256,256]{1,0:T(8,128)(2,1)S(1)}, bf16[256,256]{1,0:T(8,128)(2,1)S(1)}, u32[]{:S(2)}, u32[]{:S(2)}) collective-permute-start(bf16[256,256]{1,0:T(8,128)(2,1)S(1)} %get-tuple-element.54), channel_id=1, source_target_pairs={{0,8},{4,12},{8,0},{12,4},{16,24},{20,28},{24,16},{28,20},{1,9},{5... | collective-permute-start | bytes 393224 | tf_op jit(solution)/shard_map/ppermute | solution.py:59
  9.3 1.6 %collective-permute-start.10 = (bf16[1024,256]{1,0:T(8,128)(2,1)S(1)}, bf16[1024,256]{1,0:T(8,128)(2,1)S(1)}, u32[]{:S(2)}, u32[]{:S(2)}) collective-permute-start(bf16[1024,256]{1,0:T(8,128)(2,1)S(1)} %slice_bitcast_fusion.refs_2_), channel_id=1, source_target_pairs={{0,2},{1,3},{2,0},{3,1},{4,6},{5,7},{6,4},{7,5},{8,10},{9,11},{10,... | collective-permute-start | bytes 1572872 | tf_op jit(solution)/shard_map/ppermute | solution.py:59
  10.9 0.9 %collective-permute-start.2 = (bf16[128,256]{1,0:T(8,128)(2,1)S(1)}, bf16[128,256]{1,0:T(8,128)(2,1)S(1)}, u32[]{:S(2)}, u32[]{:S(2)}) collective-permute-start(bf16[128,256]{1,0:T(8,128)(2,1)S(1)} %shard_map.115.refs_0_), channel_id=1, source_target_pairs={{0,8},{4,12},{8,0},{12,4},{16,24},{20,28},{24,16},{28,20},{1,9},{5... | collective-permute-start | bytes 196616 | tf_op jit(solution)/shard_map/ppermute | solution.py:59
  11.9 1.3 %collective-permute-done.1.arrived = bf16[256,256]{1,0:T(8,128)(2,1)S(1)} collective-permute-done((bf16[256,256]{1,0:T(8,128)(2,1)S(1)}, bf16[256,256]{1,0:T(8,128)(2,1)S(1)}, u32[]{:S(2)}, u32[]{:S(2)}) %collective-permute-start.1) | collective-permute-done | bytes 131104 | tf_op jit(solution)/shard_map/ppermute | solution.py:59
  13.2 0.0 copy-start.1
  13.2 1.1 %collective-permute-start.6 = (bf16[128,256]{1,0:T(8,128)(2,1)S(1)}, bf16[128,256]{1,0:T(8,128)(2,1)S(1)}, u32[]{:S(2)}, u32[]{:S(2)}) collective-permute-start(bf16[128,256]{1,0:T(8,128)(2,1)S(1)} %get-tuple-element.65), channel_id=1, source_target_pairs={{0,4},{4,0},{8,12},{12,8},{16,20},{20,16},{24,28},{28,24},{1,5},{5... | collective-permute-start | bytes 196616 | tf_op jit(solution)/shard_map/ppermute | solution.py:59
  14.4 1.8 %collective-permute-start.5 = (bf16[512,256]{1,0:T(8,128)(2,1)S(1)}, bf16[512,256]{1,0:T(8,128)(2,1)S(1)}, u32[]{:S(2)}, u32[]{:S(2)}) collective-permute-start(bf16[512,256]{1,0:T(8,128)(2,1)S(1)} %collective-permute-done.3.cells), channel_id=1, source_target_pairs={{0,8},{4,0},{8,16},{12,4},{16,24},{20,12},{24,28},{28,20},{1,9},{5... | collective-permute-start | bytes 786440 | tf_op jit(solution)/shard_map/ppermute | solution.py:70
  16.2 0.6 %collective-permute-start.4 = (bf16[256,256]{1,0:T(8,128)(2,1)S(1)}, bf16[256,256]{1,0:T(8,128)(2,1)S(1)}, u32[]{:S(2)}, u32[]{:S(2)}) collective-permute-start(bf16[256,256]{1,0:T(8,128)(2,1)S(1)} %shard_map.117.mine), channel_id=1, source_target_pairs={{0,4},{4,0},{8,12},{12,8},{16,20},{20,16},{24,28},{28,24},{1,5},{5... | collective-permute-start | bytes 393224 | tf_op jit(solution)/shard_map/ppermute | solution.py:59
  16.8 0.1 copy-done.6
  16.9 0.0 copy-done.5
  16.9 2.0 %shard_map.118 = (bf16[512,512]{1,0:T(8,128)(2,1)S(1)}, bf16[512,512]{1,0:T(8,128)(2,1)S(1)}, bf16[512,512]{1,0:T(8,128)(2,1)S(1)}, bf16[512,512]{1,0:T(8,128)(2,1)S(1)}, f32[512,256]{1,0:T(8,128)S(1)}) custom-call(s32[3,32]{1,0:T(4,128)S(1)} %bitcast.6, bf16[32,128,128]{2,1,0:T(8,128)(2,1)S(1)} %copy-done.1, bf16[512,512]{1,0:T(8,128)(2,1)S(1)} %copy-done.2, ...), custom_call_target="tpu_custom_call" | custom-call | flops 1000000 | bytes 1837056 | tf_op jit(solution)/shard_map/pallas_call | solution.py:42
  19.0 2.1 %collective-permute-start.7 = (bf16[64,256]{1,0:T(8,128)(2,1)S(1)}, bf16[64,256]{1,0:T(8,128)(2,1)S(1)}, u32[]{:S(2)}, u32[]{:S(2)}) collective-permute-start(bf16[64,256]{1,0:T(8,128)(2,1)S(1)} %get-tuple-element.67), channel_id=1, source_target_pairs={{0,16},{4,20},{8,24},{12,28},{16,0},{20,4},{24,8},{28,12},{1,17},{... | collective-permute-start | bytes 98312 | tf_op jit(solution)/shard_map/ppermute | solution.py:59
  21.0 3.4 %collective-permute-done.4.theirs = bf16[256,256]{1,0:T(8,128)(2,1)S(1)} collective-permute-done((bf16[256,256]{1,0:T(8,128)(2,1)S(1)}, bf16[256,256]{1,0:T(8,128)(2,1)S(1)}, u32[]{:S(2)}, u32[]{:S(2)}) %collective-permute-start.4) | collective-permute-done | bytes 131104 | tf_op jit(solution)/shard_map/ppermute | solution.py:59
  24.4 0.5 shard_map.119.total
  24.9 0.0 copy-start.9
  24.9 0.3 shard_map.121.refs_0_
  25.2 1.6 %collective-permute-start.8 = (bf16[576,256]{1,0:T(8,128)(2,1)S(1)}, bf16[576,256]{1,0:T(8,128)(2,1)S(1)}, u32[]{:S(2)}, u32[]{:S(2)}) collective-permute-start(bf16[576,256]{1,0:T(8,128)(2,1)S(1)} %shard_map.121.refs_0_), channel_id=1, source_target_pairs={{0,2},{1,3},{2,0},{3,1},{4,6},{5,7},{6,4},{7,5},{8,10},{9,11},{10,... | collective-permute-start | bytes 884744 | tf_op jit(solution)/shard_map/ppermute | solution.py:59
  26.8 0.2 shard_map.122
  27.0 0.1 collective-permute-start.12
  27.1 0.5 collective-permute-start.11
  27.6 0.1 collective-permute-start.13
  27.7 4.3 %collective-permute-done.8.refs_0_ = bf16[576,256]{1,0:T(8,128)(2,1)S(1)} collective-permute-done((bf16[576,256]{1,0:T(8,128)(2,1)S(1)}, bf16[576,256]{1,0:T(8,128)(2,1)S(1)}, u32[]{:S(2)}, u32[]{:S(2)}) %collective-permute-start.8) | collective-permute-done | bytes 294944 | tf_op jit(solution)/shard_map/ppermute | solution.py:59
  32.0 0.5 shard_map.123
  32.5 0.5 shard_map.124
  33.0 0.6 %collective-permute-done.9.refs_1_ = bf16[576,256]{1,0:T(8,128)(2,1)S(1)} collective-permute-done((bf16[576,256]{1,0:T(8,128)(2,1)S(1)}, bf16[576,256]{1,0:T(8,128)(2,1)S(1)}, u32[]{:S(2)}, u32[]{:S(2)}) %collective-permute-start.9) | collective-permute-done | bytes 294944 | tf_op jit(solution)/shard_map/ppermute | solution.py:59
  33.6 1.2 %shard_map.125 = (bf16[512,256]{1,0:T(8,128)(2,1)S(1)}, bf16[64,256]{1,0:T(8,128)(2,1)S(1)}) custom-call(bf16[576,256]{1,0:T(8,128)(2,1)S(1)} %collective-permute-done.8.refs_0_, bf16[576,256]{1,0:T(8,128)(2,1)S(1)} %collective-permute-done.9.refs_1_, bf16[1024,256]{1,0:T(8,128)(2,1)S(1)} %slice_bitcast_fusion.refs_2_, ...), custom_call_target="tpu_custom_call" | custom-call | flops 500000000 | bytes 6684672 | tf_op jit(solution)/shard_map/pallas_call | solution.py:42
  34.8 0.6 %collective-permute-start.17 = (bf16[512,256]{1,0:T(8,128)(2,1)S(1)}, bf16[512,256]{1,0:T(8,128)(2,1)S(1)}, u32[]{:S(2)}, u32[]{:S(2)}) collective-permute-start(bf16[512,256]{1,0:T(8,128)(2,1)S(1)} %get-tuple-element.81.cells), channel_id=1, source_target_pairs={{0,4},{4,0},{8,12},{12,8},{16,20},{20,16},{24,28},{28,24},{1,5},{5... | collective-permute-start | bytes 786440 | tf_op jit(solution)/shard_map/ppermute | solution.py:59
  35.4 0.3 shard_map.126
  35.8 0.3 collective-permute-start.14
  36.1 2.9 %collective-permute-start.15 = (bf16[64,256]{1,0:T(8,128)(2,1)S(1)}, bf16[64,256]{1,0:T(8,128)(2,1)S(1)}, u32[]{:S(2)}, u32[]{:S(2)}) collective-permute-start(bf16[64,256]{1,0:T(8,128)(2,1)S(1)} %get-tuple-element.89.refs_0_), channel_id=1, source_target_pairs={{0,16},{4,20},{8,24},{12,28},{16,0},{20,4},{24,8},{28,12},{1,17},{... | collective-permute-start | bytes 98312 | tf_op jit(solution)/shard_map/ppermute | solution.py:59
  39.0 0.3 shard_map.127.total
  39.3 2.5 %collective-permute-done.14.arrived = bf16[256,256]{1,0:T(8,128)(2,1)S(1)} collective-permute-done((bf16[256,256]{1,0:T(8,128)(2,1)S(1)}, bf16[256,256]{1,0:T(8,128)(2,1)S(1)}, u32[]{:S(2)}, u32[]{:S(2)}) %collective-permute-start.14) | collective-permute-done | bytes 131104 | tf_op jit(solution)/shard_map/ppermute | solution.py:59
  41.8 1.5 %collective-permute-start.16 = (bf16[128,256]{1,0:T(8,128)(2,1)S(1)}, bf16[128,256]{1,0:T(8,128)(2,1)S(1)}, u32[]{:S(2)}, u32[]{:S(2)}) collective-permute-start(bf16[128,256]{1,0:T(8,128)(2,1)S(1)} %get-tuple-element.91), channel_id=1, source_target_pairs={{0,4},{4,0},{8,12},{12,8},{16,20},{20,16},{24,28},{28,24},{1,5},{5... | collective-permute-start | bytes 196616 | tf_op jit(solution)/shard_map/ppermute | solution.py:59
  43.4 0.1 collective-permute-start.18
  43.5 2.0 %collective-permute-start.20 = (bf16[512,256]{1,0:T(8,128)(2,1)S(1)}, bf16[512,256]{1,0:T(8,128)(2,1)S(1)}, u32[]{:S(2)}, u32[]{:S(2)}) collective-permute-start(bf16[512,256]{1,0:T(8,128)(2,1)S(1)} %collective-permute-done.17.cells), channel_id=1, source_target_pairs={{0,8},{4,0},{8,16},{12,4},{16,24},{20,12},{24,28},{28,20},{1,9},{5... | collective-permute-start | bytes 786440 | tf_op jit(solution)/shard_map/ppermute | solution.py:70
  45.5 1.4 %collective-permute-done.16.arrived = bf16[128,256]{1,0:T(8,128)(2,1)S(1)} collective-permute-done((bf16[128,256]{1,0:T(8,128)(2,1)S(1)}, bf16[128,256]{1,0:T(8,128)(2,1)S(1)}, u32[]{:S(2)}, u32[]{:S(2)}) %collective-permute-start.16) | collective-permute-done | bytes 65568 | tf_op jit(solution)/shard_map/ppermute | solution.py:59
  46.9 0.8 %collective-permute-done.18.refs_1_ = bf16[128,256]{1,0:T(8,128)(2,1)S(1)} collective-permute-done((bf16[128,256]{1,0:T(8,128)(2,1)S(1)}, bf16[128,256]{1,0:T(8,128)(2,1)S(1)}, u32[]{:S(2)}, u32[]{:S(2)}) %collective-permute-start.18) | collective-permute-done | bytes 65568 | tf_op jit(solution)/shard_map/ppermute | solution.py:59
  47.7 1.4 %collective-permute-start.19 = (bf16[256,256]{1,0:T(8,128)(2,1)S(1)}, bf16[256,256]{1,0:T(8,128)(2,1)S(1)}, u32[]{:S(2)}, u32[]{:S(2)}) collective-permute-start(bf16[256,256]{1,0:T(8,128)(2,1)S(1)} %shard_map.131.mine), channel_id=1, source_target_pairs={{0,4},{4,0},{8,12},{12,8},{16,20},{20,16},{24,28},{28,24},{1,5},{5... | collective-permute-start | bytes 393224 | tf_op jit(solution)/shard_map/ppermute | solution.py:59
  49.1 1.0 %collective-permute-start.21 = (bf16[64,256]{1,0:T(8,128)(2,1)S(1)}, bf16[64,256]{1,0:T(8,128)(2,1)S(1)}, u32[]{:S(2)}, u32[]{:S(2)}) collective-permute-start(bf16[64,256]{1,0:T(8,128)(2,1)S(1)} %get-tuple-element.97), channel_id=1, source_target_pairs={{0,16},{4,20},{8,24},{12,28},{16,0},{20,4},{24,8},{28,12},{1,17},{... | collective-permute-start | bytes 98312 | tf_op jit(solution)/shard_map/ppermute | solution.py:59
  50.1 4.2 %collective-permute-done.19.theirs = bf16[256,256]{1,0:T(8,128)(2,1)S(1)} collective-permute-done((bf16[256,256]{1,0:T(8,128)(2,1)S(1)}, bf16[256,256]{1,0:T(8,128)(2,1)S(1)}, u32[]{:S(2)}, u32[]{:S(2)}) %collective-permute-start.19) | collective-permute-done | bytes 131104 | tf_op jit(solution)/shard_map/ppermute | solution.py:59
  54.3 0.5 shard_map.132.total
  54.8 1.1 %shard_map.133 = f32[512,256]{1,0:T(8,128)} custom-call(f32[512,256]{1,0:T(8,128)S(1)} %shard_map.132.total, bf16[512,512]{1,0:T(8,128)(2,1)S(1)} %get-tuple-element.62.far, bf16[512,256]{1,0:T(8,128)(2,1)S(1)} %collective-permute-done.20.other, f32[512,256]{1,0:T(8,128)S(1)} %get-tuple-element.70.refs_11_.scale), custom_call_target="tpu_custom_call" | custom-call | flops 500000000 | bytes 1835008 | tf_op jit(solution)/shard_map/pallas_call | solution.py:42
  55.9 0.6 %shard_map.134 = f32[64,256]{1,0:T(8,128)} custom-call(f32[64,256]{1,0:T(8,128)S(1)} %get-tuple-element.96.own, bf16[64,256]{1,0:T(8,128)(2,1)S(1)} %collective-permute-done.21.refs_0_, f32[64,256]{1,0:T(8,128)S(1)} %get-tuple-element.80.refs_12_.refs_1_), custom_call_target="tpu_custom_call" | custom-call | flops 1000000 | bytes 163840 | tf_op jit(solution)/shard_map/pallas_call | solution.py:42
  (39 shorter events, 0.2 us)
Async XLA Ops:
  0.6 1.0 %copy-start.3 = (f32[512,256]{1,0:T(8,128)S(1)}, f32[512,256]{1,0:T(8,128)}, u32[]{:S(2)}) copy-start(f32[512,256]{1,0:T(8,128)} %cells.1) | copy-start | bytes 1572868
  1.7 3.1 %copy-start.4 = (bf16[512,512]{1,0:T(8,128)(2,1)S(1)}, bf16[512,512]{1,0:T(8,128)(2,1)}, u32[]{:S(2)}) copy-start(bf16[512,512]{1,0:T(8,128)(2,1)} %rows.3) | copy-start | bytes 1572868
  1.7 3.1 %copy-start.7 = (f32[64,256]{1,0:T(8,128)S(1)}, f32[64,256]{1,0:T(8,128)}, u32[]{:S(2)}) copy-start(f32[64,256]{1,0:T(8,128)} %refs_0_.1) | copy-start | bytes 196612
  1.7 7.6 %copy-start = (bf16[2,1024,256]{2,1,0:T(8,128)(2,1)S(1)}, bf16[2,1024,256]{2,1,0:T(8,128)(2,1)}, u32[]{:S(2)}) copy-start(bf16[2,1024,256]{2,1,0:T(8,128)(2,1)} %refs_10_.1) | copy-start | bytes 3145732
  1.7 12.7 %collective-permute-start.3 = (bf16[512,256]{1,0:T(8,128)(2,1)S(1)}, bf16[512,256]{1,0:T(8,128)(2,1)S(1)}, u32[]{:S(2)}, u32[]{:S(2)}) collective-permute-start(bf16[512,256]{1,0:T(8,128)(2,1)S(1)} %shard_map.113.cells), channel_id=1, source_target_pairs={{0,4},{4,0},{8,12},{12,8},{16,20},{20,16},{24,28},{28,24},{1,5},{5... | collective-permute-start | bytes 786440 | tf_op jit(solution)/shard_map/ppermute | solution.py:59
  5.1 5.9 %collective-permute-start = (bf16[64,256]{1,0:T(8,128)(2,1)S(1)}, bf16[64,256]{1,0:T(8,128)(2,1)S(1)}, u32[]{:S(2)}, u32[]{:S(2)}) collective-permute-start(bf16[64,256]{1,0:T(8,128)(2,1)S(1)} %get-tuple-element.52.refs_0_), channel_id=1, source_target_pairs={{0,16},{4,20},{8,24},{12,28},{16,0},{20,4},{24,8},{28,12},{1,17},{... | collective-permute-start | bytes 98312 | tf_op jit(solution)/shard_map/ppermute | solution.py:59
  7.7 5.5 %collective-permute-start.1 = (bf16[256,256]{1,0:T(8,128)(2,1)S(1)}, bf16[256,256]{1,0:T(8,128)(2,1)S(1)}, u32[]{:S(2)}, u32[]{:S(2)}) collective-permute-start(bf16[256,256]{1,0:T(8,128)(2,1)S(1)} %get-tuple-element.54), channel_id=1, source_target_pairs={{0,8},{4,12},{8,0},{12,4},{16,24},{20,28},{24,16},{28,20},{1,9},{5... | collective-permute-start | bytes 393224 | tf_op jit(solution)/shard_map/ppermute | solution.py:59
  9.3 17.7 %collective-permute-start.10 = (bf16[1024,256]{1,0:T(8,128)(2,1)S(1)}, bf16[1024,256]{1,0:T(8,128)(2,1)S(1)}, u32[]{:S(2)}, u32[]{:S(2)}) collective-permute-start(bf16[1024,256]{1,0:T(8,128)(2,1)S(1)} %slice_bitcast_fusion.refs_2_), channel_id=1, source_target_pairs={{0,2},{1,3},{2,0},{3,1},{4,6},{5,7},{6,4},{7,5},{8,10},{9,11},{10,... | collective-permute-start | bytes 1572872 | tf_op jit(solution)/shard_map/ppermute | solution.py:59
  10.9 5.3 %collective-permute-start.2 = (bf16[128,256]{1,0:T(8,128)(2,1)S(1)}, bf16[128,256]{1,0:T(8,128)(2,1)S(1)}, u32[]{:S(2)}, u32[]{:S(2)}) collective-permute-start(bf16[128,256]{1,0:T(8,128)(2,1)S(1)} %shard_map.115.refs_0_), channel_id=1, source_target_pairs={{0,8},{4,12},{8,0},{12,4},{16,24},{20,28},{24,16},{28,20},{1,9},{5... | collective-permute-start | bytes 196616 | tf_op jit(solution)/shard_map/ppermute | solution.py:59
  13.2 3.6 %copy-start.1 = (bf16[32,128,128]{2,1,0:T(8,128)(2,1)S(1)}, bf16[32,128,128]{2,1,0:T(8,128)(2,1)}, u32[]{:S(2)}) copy-start(bf16[32,128,128]{2,1,0:T(8,128)(2,1)} %tiles.1) | copy-start | bytes 3145732
  13.2 5.7 %collective-permute-start.6 = (bf16[128,256]{1,0:T(8,128)(2,1)S(1)}, bf16[128,256]{1,0:T(8,128)(2,1)S(1)}, u32[]{:S(2)}, u32[]{:S(2)}) collective-permute-start(bf16[128,256]{1,0:T(8,128)(2,1)S(1)} %get-tuple-element.65), channel_id=1, source_target_pairs={{0,4},{4,0},{8,12},{12,8},{16,20},{20,16},{24,28},{28,24},{1,5},{5... | collective-permute-start | bytes 196616 | tf_op jit(solution)/shard_map/ppermute | solution.py:59
  14.4 2.4 %copy-start.2 = (bf16[512,512]{1,0:T(8,128)(2,1)S(1)}, bf16[512,512]{1,0:T(8,128)(2,1)}, u32[]{:S(2)}) copy-start(bf16[512,512]{1,0:T(8,128)(2,1)} %cols.1) | copy-start | bytes 1572868
  14.4 10.5 %collective-permute-start.5 = (bf16[512,256]{1,0:T(8,128)(2,1)S(1)}, bf16[512,256]{1,0:T(8,128)(2,1)S(1)}, u32[]{:S(2)}, u32[]{:S(2)}) collective-permute-start(bf16[512,256]{1,0:T(8,128)(2,1)S(1)} %collective-permute-done.3.cells), channel_id=1, source_target_pairs={{0,8},{4,0},{8,16},{12,4},{16,24},{20,12},{24,28},{28,20},{1,9},{5... | collective-permute-start | bytes 786440 | tf_op jit(solution)/shard_map/ppermute | solution.py:70
  16.2 0.7 %copy-start.6 = (s32[512]{0:T(512)S(1)}, s32[512]{0:T(512)}, u32[]{:S(2)}) copy-start(s32[512]{0:T(512)} %param.16) | copy-start | bytes 6148
  16.2 0.7 %copy-start.5 = (s32[32,3]{0,1:T(4,128)S(1)}, s32[32,3]{0,1:T(4,128)}, u32[]{:S(2)}) copy-start(s32[32,3]{0,1:T(4,128)} %param.13) | copy-start | bytes 1156
  16.2 8.2 %collective-permute-start.4 = (bf16[256,256]{1,0:T(8,128)(2,1)S(1)}, bf16[256,256]{1,0:T(8,128)(2,1)S(1)}, u32[]{:S(2)}, u32[]{:S(2)}) collective-permute-start(bf16[256,256]{1,0:T(8,128)(2,1)S(1)} %shard_map.117.mine), channel_id=1, source_target_pairs={{0,4},{4,0},{8,12},{12,8},{16,20},{20,16},{24,28},{28,24},{1,5},{5... | collective-permute-start | bytes 393224 | tf_op jit(solution)/shard_map/ppermute | solution.py:59
  19.0 5.9 %collective-permute-start.7 = (bf16[64,256]{1,0:T(8,128)(2,1)S(1)}, bf16[64,256]{1,0:T(8,128)(2,1)S(1)}, u32[]{:S(2)}, u32[]{:S(2)}) collective-permute-start(bf16[64,256]{1,0:T(8,128)(2,1)S(1)} %get-tuple-element.67), channel_id=1, source_target_pairs={{0,16},{4,20},{8,24},{12,28},{16,0},{20,4},{24,8},{28,12},{1,17},{... | collective-permute-start | bytes 98312 | tf_op jit(solution)/shard_map/ppermute | solution.py:59
  24.9 1.9 %copy-start.9 = (s32[512]{0:T(512)S(1)}, s32[512]{0:T(512)}, u32[]{:S(2)}) copy-start(s32[512]{0:T(512)} %param.19) | copy-start | bytes 6148
  25.2 1.6 %copy-start.8 = (s32[512]{0:T(512)S(1)}, s32[512]{0:T(512)}, u32[]{:S(2)}) copy-start(s32[512]{0:T(512)} %param.18) | copy-start | bytes 6148
  25.2 6.8 %collective-permute-start.8 = (bf16[576,256]{1,0:T(8,128)(2,1)S(1)}, bf16[576,256]{1,0:T(8,128)(2,1)S(1)}, u32[]{:S(2)}, u32[]{:S(2)}) collective-permute-start(bf16[576,256]{1,0:T(8,128)(2,1)S(1)} %shard_map.121.refs_0_), channel_id=1, source_target_pairs={{0,2},{1,3},{2,0},{3,1},{4,6},{5,7},{6,4},{7,5},{8,10},{9,11},{10,... | collective-permute-start | bytes 884744 | tf_op jit(solution)/shard_map/ppermute | solution.py:59
  27.0 5.5 %collective-permute-start.12 = (bf16[1024,256]{1,0:T(8,128)(2,1)S(1)}, bf16[1024,256]{1,0:T(8,128)(2,1)S(1)}, u32[]{:S(2)}, u32[]{:S(2)}) collective-permute-start(bf16[1024,256]{1,0:T(8,128)(2,1)S(1)} %collective-permute-done.10.refs_3_), channel_id=1, source_target_pairs={{0,1},{1,0},{2,3},{3,2},{4,5},{5,4},{6,7},{7,6},{8,9},{9,8},{10,11... | collective-permute-start | bytes 1572872 | tf_op jit(solution)/shard_map/ppermute | solution.py:59
  27.1 5.4 %collective-permute-start.11 = (bf16[1024,256]{1,0:T(8,128)(2,1)S(1)}, bf16[1024,256]{1,0:T(8,128)(2,1)S(1)}, u32[]{:S(2)}, u32[]{:S(2)}) collective-permute-start(bf16[1024,256]{1,0:T(8,128)(2,1)S(1)} %slice_bitcast_fusion.refs_2_), channel_id=1, source_target_pairs={{0,1},{1,0},{2,3},{3,2},{4,5},{5,4},{6,7},{7,6},{8,9},{9,8},{10,11... | collective-permute-start | bytes 1572872 | tf_op jit(solution)/shard_map/ppermute | solution.py:59
  27.6 4.4 %collective-permute-start.13 = (bf16[576,256]{1,0:T(8,128)(2,1)S(1)}, bf16[576,256]{1,0:T(8,128)(2,1)S(1)}, u32[]{:S(2)}, u32[]{:S(2)}) collective-permute-start(bf16[576,256]{1,0:T(8,128)(2,1)S(1)} %shard_map.121.refs_0_), channel_id=1, source_target_pairs={{0,1},{1,0},{2,3},{3,2},{4,5},{5,4},{6,7},{7,6},{8,9},{9,8},{10,11... | collective-permute-start | bytes 884744 | tf_op jit(solution)/shard_map/ppermute | solution.py:59
  32.0 1.6 %collective-permute-start.9 = (bf16[576,256]{1,0:T(8,128)(2,1)S(1)}, bf16[576,256]{1,0:T(8,128)(2,1)S(1)}, u32[]{:S(2)}, u32[]{:S(2)}) collective-permute-start(bf16[576,256]{1,0:T(8,128)(2,1)S(1)} %collective-permute-done.8.refs_0_), channel_id=1, source_target_pairs={{0,1},{1,0},{2,3},{3,2},{4,5},{5,4},{6,7},{7,6},{8,9},{9,8},{10,11... | collective-permute-start | bytes 884744 | tf_op jit(solution)/shard_map/ppermute | solution.py:59
  34.8 8.6 %collective-permute-start.17 = (bf16[512,256]{1,0:T(8,128)(2,1)S(1)}, bf16[512,256]{1,0:T(8,128)(2,1)S(1)}, u32[]{:S(2)}, u32[]{:S(2)}) collective-permute-start(bf16[512,256]{1,0:T(8,128)(2,1)S(1)} %get-tuple-element.81.cells), channel_id=1, source_target_pairs={{0,4},{4,0},{8,12},{12,8},{16,20},{20,16},{24,28},{28,24},{1,5},{5... | collective-permute-start | bytes 786440 | tf_op jit(solution)/shard_map/ppermute | solution.py:59
  35.8 6.0 %collective-permute-start.14 = (bf16[256,256]{1,0:T(8,128)(2,1)S(1)}, bf16[256,256]{1,0:T(8,128)(2,1)S(1)}, u32[]{:S(2)}, u32[]{:S(2)}) collective-permute-start(bf16[256,256]{1,0:T(8,128)(2,1)S(1)} %get-tuple-element.85), channel_id=1, source_target_pairs={{0,8},{4,12},{8,0},{12,4},{16,24},{20,28},{24,16},{28,20},{1,9},{5... | collective-permute-start | bytes 393224 | tf_op jit(solution)/shard_map/ppermute | solution.py:59
  36.1 7.3 %collective-permute-start.15 = (bf16[64,256]{1,0:T(8,128)(2,1)S(1)}, bf16[64,256]{1,0:T(8,128)(2,1)S(1)}, u32[]{:S(2)}, u32[]{:S(2)}) collective-permute-start(bf16[64,256]{1,0:T(8,128)(2,1)S(1)} %get-tuple-element.89.refs_0_), channel_id=1, source_target_pairs={{0,16},{4,20},{8,24},{12,28},{16,0},{20,4},{24,8},{28,12},{1,17},{... | collective-permute-start | bytes 98312 | tf_op jit(solution)/shard_map/ppermute | solution.py:59
  41.8 5.0 %collective-permute-start.16 = (bf16[128,256]{1,0:T(8,128)(2,1)S(1)}, bf16[128,256]{1,0:T(8,128)(2,1)S(1)}, u32[]{:S(2)}, u32[]{:S(2)}) collective-permute-start(bf16[128,256]{1,0:T(8,128)(2,1)S(1)} %get-tuple-element.91), channel_id=1, source_target_pairs={{0,4},{4,0},{8,12},{12,8},{16,20},{20,16},{24,28},{28,24},{1,5},{5... | collective-permute-start | bytes 196616 | tf_op jit(solution)/shard_map/ppermute | solution.py:59
  43.4 4.3 %collective-permute-start.18 = (bf16[128,256]{1,0:T(8,128)(2,1)S(1)}, bf16[128,256]{1,0:T(8,128)(2,1)S(1)}, u32[]{:S(2)}, u32[]{:S(2)}) collective-permute-start(bf16[128,256]{1,0:T(8,128)(2,1)S(1)} %shard_map.129.refs_0_), channel_id=1, source_target_pairs={{0,8},{4,12},{8,0},{12,4},{16,24},{20,28},{24,16},{28,20},{1,9},{5... | collective-permute-start | bytes 196616 | tf_op jit(solution)/shard_map/ppermute | solution.py:59
  43.5 11.3 %collective-permute-start.20 = (bf16[512,256]{1,0:T(8,128)(2,1)S(1)}, bf16[512,256]{1,0:T(8,128)(2,1)S(1)}, u32[]{:S(2)}, u32[]{:S(2)}) collective-permute-start(bf16[512,256]{1,0:T(8,128)(2,1)S(1)} %collective-permute-done.17.cells), channel_id=1, source_target_pairs={{0,8},{4,0},{8,16},{12,4},{16,24},{20,12},{24,28},{28,20},{1,9},{5... | collective-permute-start | bytes 786440 | tf_op jit(solution)/shard_map/ppermute | solution.py:70
  47.7 6.5 %collective-permute-start.19 = (bf16[256,256]{1,0:T(8,128)(2,1)S(1)}, bf16[256,256]{1,0:T(8,128)(2,1)S(1)}, u32[]{:S(2)}, u32[]{:S(2)}) collective-permute-start(bf16[256,256]{1,0:T(8,128)(2,1)S(1)} %shard_map.131.mine), channel_id=1, source_target_pairs={{0,4},{4,0},{8,12},{12,8},{16,20},{20,16},{24,28},{28,24},{1,5},{5... | collective-permute-start | bytes 393224 | tf_op jit(solution)/shard_map/ppermute | solution.py:59
  49.1 6.7 %collective-permute-start.21 = (bf16[64,256]{1,0:T(8,128)(2,1)S(1)}, bf16[64,256]{1,0:T(8,128)(2,1)S(1)}, u32[]{:S(2)}, u32[]{:S(2)}) collective-permute-start(bf16[64,256]{1,0:T(8,128)(2,1)S(1)} %get-tuple-element.97), channel_id=1, source_target_pairs={{0,16},{4,20},{8,24},{12,28},{16,0},{20,4},{24,8},{28,12},{1,17},{... | collective-permute-start | bytes 98312 | tf_op jit(solution)/shard_map/ppermute | solution.py:59

commit v5 on v4

--- a/solution.py
+++ b/solution.py
@@ -12,23 +12,22 @@
 LIMIT = 16 * 1024 * 1024
 WORK = {
     "cast": 1_000_000,
-    "part1": 4_000_000_000,
+    "part1": 2_000_000_000,
     "dense": 1_000_000,
-    "join1": 500_000_000,
+    "join1": 200_000_000,
     "fold1": 2_000_000_000,
     "sum1": 1_000_000,
-    "first": 500_000_000,
+    "first": 1_000_000,
     "scale": 500_000_000,
-    "begin": 1_000_000_000,
-    "mid": 500_000_000,
+    "begin": 1_000_000,
+    "mid": 200_000_000,
     "end": 500_000_000,
     "part2": 1_000_000,
     "near": 500_000_000,
-    "join2": 500_000_000,
-    "fold2": 1_000_000,
-    "sum2": 500_000_000,
+    "join2": 10_000,
+    "fold2": 4_000_000_000,
+    "sum2": 2_000_000_000,
     "last": 500_000_000,
-    "headout": 1_000_000,
     "collect": 500_000_000,
     "join3": 500_000_000,
     "headmix": 500_000_000,
@@ -202,8 +201,19 @@
         out[rows:] = extra.astype(BF)
 
 
-def last_sum_kernel(total, far, other, scale, out):
-    out[...] = jnp.maximum((total[...] + mm(far[...], other[...])) * scale[...], 0.0)
+def add_kernel(total, pair, cells, out):
+    out[...] = total[...] + mm(pair[...], cells[...])
+
+
+def last_kernel(total, far, other, masked, mine, theirs, scale, *refs, head_dev):
+    if head_dev:
+        own, arrived, head_scale, out, head_out, heads = refs
+        head_out[...] = jnp.maximum((own[...] + arrived[...].astype(F32)) * head_scale[...], 0.0)
+    else:
+        out, heads = refs
+    whole_heads(mine, theirs, heads, head_dev)
+    band = total[...] + mm(far[...], other[...]) + mm(masked[...], heads[...])
+    out[...] = jnp.maximum(band * scale[...], 0.0)
 
 
 def feature_rows(k, width):
@@ -252,14 +262,6 @@
 
 def wide_scale_kernel(degree, scale):
     scale[...] = lax.rsqrt(column(degree[...], scale.shape[1]))
-
-
-def head_out_kernel(own, *refs):
-    arrived, (scale, out) = refs[:-2], refs[-2:]
-    total = own[...]
-    for ref in arrived:
-        total = total + ref[...].astype(F32)
-    out[...] = jnp.maximum(total * scale[...], 0.0)
 
 
 def body(
@@ -411,8 +413,8 @@
         head_state = jnp.maximum(mm(summed, full) * head_scale[:, :1], 0.0).astype(BF)
         head_x = [mm(head_state, mix_weights[1]).astype(BF)]
 
-    pair_cells = swap(cells, "rows", 1)
     keep, send = partial_sums("part2", last_bits, cells)
+    pair_cells = swap(after(cells, keep), "rows", 1)
     sums = []
 
     def multiply(before):
@@ -420,17 +422,23 @@
         return sums[-1]
 
     mine, theirs, parts = exchange(
-        "join2", "fold2", after(head_x[0], keep), keep, send, keep, last_bits, "fjfj", 0, multiply
+        "join2", "fold2", after(head_x[0], keep), keep, send, keep, last_bits, "fjfj", 2, multiply
     )
     (total,) = sums
     far_cells = forward(after(pair_cells, total))
-    (total,) = local(
-        "sum2", sum_up, band_sum, (), (after(total, *parts[:1]), pair, pair_cells, masked, mine, theirs), [head_scratch]
-    )
-    (band_out,) = local("last", last_sum_kernel, band_sum, (), (total, far, far_cells, scale))
+    (total,) = local("sum2", add_kernel, band_sum, (), (after(total, mine), pair, pair_cells))
+    outs = band_sum + ([head_sum] if size else [])
+    sums = (*parts, head_scale) if size else ()
+    band_out, *head_out = local(
+        "last",
+        functools.partial(last_kernel, head_dev=size),
+        outs,
+        (),
+        (total, far, far_cells, masked, mine, theirs, scale, *sums),
+        [head_scratch],
+    )
     if size:
-        own = after(parts[0], band_out)
-        (head_out,) = local("headout", head_out_kernel, [head_sum], (), (own, *parts[1:], head_scale))
+        (head_out,) = head_out
     else:
         head_out = jnp.maximum(lax.psum_scatter(keep, "rows", scatter_dimension=0, tiled=True) * head_scale, 0.0)
     return band_out, head_out

time: 56.7 us -> 55.7 us (0.982)
  Pallas kernels: 8.47 us -> 7.79 us
  waiting for transfers between devices: 18.5 us -> 17.9 us
    pallas_call x22 -> x21, Pallas kernels: 8.47 us -> 7.79 us  [local(): pl.pallas_call(kernel, out_shape=[jax.ShapeDtypeStruct(s, d) for s, d in...]
    ppermute x20, waiting for transfers between devices: 18.5 us -> 17.9 us  [swap(): return lax.ppermute(cells, axis, [(i, i ^ bit) for i in range(count)])]
  transfers between devices with their start and end apart: 22 -> 22, of which waited for: 8 -> 9; matrix products, arithmetic and copies ran while one was open for 0% -> 0% of each run, Pallas kernels for 12% -> 9%
where the time goes in v5:
time: 55.7 us; the launch traced here: 55.5 us
  starting transfers between devices  27.7 us (50%)
  waiting for transfers between devices  17.9 us (32%)
  Pallas kernels  7.79 us (14%)
  local copies, waits for them, and re-layouts  1.19 us (2%)
  between operations  0.9 us (2%)
    ppermute x20, starting transfers between devices, swap(): return lax.ppermute(cells, axis, [(i, i ^ bit) for i in range(count)])  24 us
    ppermute x20, waiting for transfers between devices, swap(): return lax.ppermute(cells, axis, [(i, i ^ bit) for i in range(count)])  17.9 us
    pallas_call x21, Pallas kernels, local(): pl.pallas_call(kernel, out_shape=[jax.ShapeDtypeStruct(s, d) for s, d in...  7.79 us
    ppermute x2, starting transfers between devices, forward(): return lax.ppermute(cells, 'rows', pairs)  3.71 us
    unnamed x20, local copies, waits for them, and re-layouts  1.16 us
  transfers between devices with their start and end apart: 22, of which 9 were waited for; matrix products, arithmetic and copies ran while one was open for 0% of the time, Pallas kernels for 9%

profile of v5, /device:TPU:0, one launch (start us, length us, event | category | flops | bytes accessed | tf_op | source)
XLA Modules:
  0.0 55.5 jit_solution(7737355898202404619)
XLA Ops:
  0.6 1.0 %copy-done.3 = f32[512,256]{1,0:T(8,128)S(1)} copy-done((f32[512,256]{1,0:T(8,128)S(1)}, f32[512,256]{1,0:T(8,128)}, u32[]{:S(2)}) %copy-start.3) | copy-done | bytes 524312
  1.7 0.0 copy-start
  1.7 3.0 %collective-permute-start.3 = (bf16[512,256]{1,0:T(8,128)(2,1)S(1)}, bf16[512,256]{1,0:T(8,128)(2,1)S(1)}, u32[]{:S(2)}, u32[]{:S(2)}) collective-permute-start(bf16[512,256]{1,0:T(8,128)(2,1)S(1)} %shard_map.113.cells), channel_id=1, source_target_pairs={{0,4},{4,0},{8,12},{12,8},{16,20},{20,16},{24,28},{28,24},{1,5},{5... | collective-permute-start | bytes 786440 | tf_op jit(solution)/shard_map/ppermute | solution.py:58
  4.7 0.3 shard_map.114
  5.1 2.7 %collective-permute-start = (bf16[64,256]{1,0:T(8,128)(2,1)S(1)}, bf16[64,256]{1,0:T(8,128)(2,1)S(1)}, u32[]{:S(2)}, u32[]{:S(2)}) collective-permute-start(bf16[64,256]{1,0:T(8,128)(2,1)S(1)} %get-tuple-element.52.refs_0_), channel_id=1, source_target_pairs={{0,16},{4,20},{8,24},{12,28},{16,0},{20,4},{24,8},{28,12},{1,17},{... | collective-permute-start | bytes 98312 | tf_op jit(solution)/shard_map/ppermute | solution.py:58
  7.7 1.6 %collective-permute-start.1 = (bf16[256,256]{1,0:T(8,128)(2,1)S(1)}, bf16[256,256]{1,0:T(8,128)(2,1)S(1)}, u32[]{:S(2)}, u32[]{:S(2)}) collective-permute-start(bf16[256,256]{1,0:T(8,128)(2,1)S(1)} %get-tuple-element.54), channel_id=1, source_target_pairs={{0,8},{4,12},{8,0},{12,4},{16,24},{20,28},{24,16},{28,20},{1,9},{5... | collective-permute-start | bytes 393224 | tf_op jit(solution)/shard_map/ppermute | solution.py:58
  9.3 1.6 %collective-permute-start.10 = (bf16[1024,256]{1,0:T(8,128)(2,1)S(1)}, bf16[1024,256]{1,0:T(8,128)(2,1)S(1)}, u32[]{:S(2)}, u32[]{:S(2)}) collective-permute-start(bf16[1024,256]{1,0:T(8,128)(2,1)S(1)} %slice_bitcast_fusion.refs_2_), channel_id=1, source_target_pairs={{0,2},{1,3},{2,0},{3,1},{4,6},{5,7},{6,4},{7,5},{8,10},{9,11},{10,... | collective-permute-start | bytes 1572872 | tf_op jit(solution)/shard_map/ppermute | solution.py:58
  10.9 0.9 %collective-permute-start.2 = (bf16[128,256]{1,0:T(8,128)(2,1)S(1)}, bf16[128,256]{1,0:T(8,128)(2,1)S(1)}, u32[]{:S(2)}, u32[]{:S(2)}) collective-permute-start(bf16[128,256]{1,0:T(8,128)(2,1)S(1)} %shard_map.115.refs_0_), channel_id=1, source_target_pairs={{0,8},{4,12},{8,0},{12,4},{16,24},{20,28},{24,16},{28,20},{1,9},{5... | collective-permute-start | bytes 196616 | tf_op jit(solution)/shard_map/ppermute | solution.py:58
  11.9 1.3 %collective-permute-done.1.arrived = bf16[256,256]{1,0:T(8,128)(2,1)S(1)} collective-permute-done((bf16[256,256]{1,0:T(8,128)(2,1)S(1)}, bf16[256,256]{1,0:T(8,128)(2,1)S(1)}, u32[]{:S(2)}, u32[]{:S(2)}) %collective-permute-start.1) | collective-permute-done | bytes 131104 | tf_op jit(solution)/shard_map/ppermute | solution.py:58
  13.2 0.0 copy-start.2
  13.2 1.1 %collective-permute-start.6 = (bf16[128,256]{1,0:T(8,128)(2,1)S(1)}, bf16[128,256]{1,0:T(8,128)(2,1)S(1)}, u32[]{:S(2)}, u32[]{:S(2)}) collective-permute-start(bf16[128,256]{1,0:T(8,128)(2,1)S(1)} %get-tuple-element.65), channel_id=1, source_target_pairs={{0,4},{4,0},{8,12},{12,8},{16,20},{20,16},{24,28},{28,24},{1,5},{5... | collective-permute-start | bytes 196616 | tf_op jit(solution)/shard_map/ppermute | solution.py:58
  14.4 1.8 %collective-permute-start.5 = (bf16[512,256]{1,0:T(8,128)(2,1)S(1)}, bf16[512,256]{1,0:T(8,128)(2,1)S(1)}, u32[]{:S(2)}, u32[]{:S(2)}) collective-permute-start(bf16[512,256]{1,0:T(8,128)(2,1)S(1)} %collective-permute-done.3.cells), channel_id=1, source_target_pairs={{0,8},{4,0},{8,16},{12,4},{16,24},{20,12},{24,28},{28,20},{1,9},{5... | collective-permute-start | bytes 786440 | tf_op jit(solution)/shard_map/ppermute | solution.py:69
  16.2 0.6 %collective-permute-start.4 = (bf16[256,256]{1,0:T(8,128)(2,1)S(1)}, bf16[256,256]{1,0:T(8,128)(2,1)S(1)}, u32[]{:S(2)}, u32[]{:S(2)}) collective-permute-start(bf16[256,256]{1,0:T(8,128)(2,1)S(1)} %shard_map.117.mine), channel_id=1, source_target_pairs={{0,4},{4,0},{8,12},{12,8},{16,20},{20,16},{24,28},{28,24},{1,5},{5... | collective-permute-start | bytes 393224 | tf_op jit(solution)/shard_map/ppermute | solution.py:58
  16.8 0.1 copy-done.6
  16.9 0.0 copy-done.5
  16.9 2.0 %shard_map.118 = (bf16[512,512]{1,0:T(8,128)(2,1)S(1)}, bf16[512,512]{1,0:T(8,128)(2,1)S(1)}, bf16[512,512]{1,0:T(8,128)(2,1)S(1)}, bf16[512,512]{1,0:T(8,128)(2,1)S(1)}, f32[512,256]{1,0:T(8,128)S(1)}) custom-call(s32[3,32]{1,0:T(4,128)S(1)} %bitcast.6, bf16[32,128,128]{2,1,0:T(8,128)(2,1)S(1)} %copy-done.1, bf16[512,512]{1,0:T(8,128)(2,1)S(1)} %copy-done.2, ...), custom_call_target="tpu_custom_call" | custom-call | flops 1000000 | bytes 1837056 | tf_op jit(solution)/shard_map/pallas_call | solution.py:41
  18.9 2.1 %collective-permute-start.7 = (bf16[64,256]{1,0:T(8,128)(2,1)S(1)}, bf16[64,256]{1,0:T(8,128)(2,1)S(1)}, u32[]{:S(2)}, u32[]{:S(2)}) collective-permute-start(bf16[64,256]{1,0:T(8,128)(2,1)S(1)} %get-tuple-element.67), channel_id=1, source_target_pairs={{0,16},{4,20},{8,24},{12,28},{16,0},{20,4},{24,8},{28,12},{1,17},{... | collective-permute-start | bytes 98312 | tf_op jit(solution)/shard_map/ppermute | solution.py:58
  21.0 3.4 %collective-permute-done.4.theirs = bf16[256,256]{1,0:T(8,128)(2,1)S(1)} collective-permute-done((bf16[256,256]{1,0:T(8,128)(2,1)S(1)}, bf16[256,256]{1,0:T(8,128)(2,1)S(1)}, u32[]{:S(2)}, u32[]{:S(2)}) %collective-permute-start.4) | collective-permute-done | bytes 131104 | tf_op jit(solution)/shard_map/ppermute | solution.py:58
  24.4 0.5 shard_map.119.total
  24.9 0.3 shard_map.121.refs_0_
  25.2 0.0 copy-start.8
  25.2 1.6 %collective-permute-start.8 = (bf16[576,256]{1,0:T(8,128)(2,1)S(1)}, bf16[576,256]{1,0:T(8,128)(2,1)S(1)}, u32[]{:S(2)}, u32[]{:S(2)}) collective-permute-start(bf16[576,256]{1,0:T(8,128)(2,1)S(1)} %shard_map.121.refs_0_), channel_id=1, source_target_pairs={{0,2},{1,3},{2,0},{3,1},{4,6},{5,7},{6,4},{7,5},{8,10},{9,11},{10,... | collective-permute-start | bytes 884744 | tf_op jit(solution)/shard_map/ppermute | solution.py:58
  26.8 0.2 shard_map.122
  27.0 0.1 collective-permute-start.12
  27.1 0.5 collective-permute-start.11
  27.6 0.1 collective-permute-start.13
  27.7 4.3 %collective-permute-done.8.refs_0_ = bf16[576,256]{1,0:T(8,128)(2,1)S(1)} collective-permute-done((bf16[576,256]{1,0:T(8,128)(2,1)S(1)}, bf16[576,256]{1,0:T(8,128)(2,1)S(1)}, u32[]{:S(2)}, u32[]{:S(2)}) %collective-permute-start.8) | collective-permute-done | bytes 294944 | tf_op jit(solution)/shard_map/ppermute | solution.py:58
  32.0 0.5 shard_map.123
  32.5 0.5 shard_map.124
  33.0 0.6 %collective-permute-done.9.refs_1_ = bf16[576,256]{1,0:T(8,128)(2,1)S(1)} collective-permute-done((bf16[576,256]{1,0:T(8,128)(2,1)S(1)}, bf16[576,256]{1,0:T(8,128)(2,1)S(1)}, u32[]{:S(2)}, u32[]{:S(2)}) %collective-permute-start.9) | collective-permute-done | bytes 294944 | tf_op jit(solution)/shard_map/ppermute | solution.py:58
  33.6 1.2 %shard_map.125 = (bf16[512,256]{1,0:T(8,128)(2,1)S(1)}, bf16[64,256]{1,0:T(8,128)(2,1)S(1)}) custom-call(bf16[576,256]{1,0:T(8,128)(2,1)S(1)} %collective-permute-done.8.refs_0_, bf16[576,256]{1,0:T(8,128)(2,1)S(1)} %collective-permute-done.9.refs_1_, bf16[1024,256]{1,0:T(8,128)(2,1)S(1)} %slice_bitcast_fusion.refs_2_, ...), custom_call_target="tpu_custom_call" | custom-call | flops 500000000 | bytes 6684672 | tf_op jit(solution)/shard_map/pallas_call | solution.py:41
  34.8 0.3 shard_map.126
  35.1 0.1 collective-permute-start.14
  35.2 0.7 %collective-permute-start.18 = (bf16[512,256]{1,0:T(8,128)(2,1)S(1)}, bf16[512,256]{1,0:T(8,128)(2,1)S(1)}, u32[]{:S(2)}, u32[]{:S(2)}) collective-permute-start(bf16[512,256]{1,0:T(8,128)(2,1)S(1)} %get-tuple-element.95.cells), channel_id=1, source_target_pairs={{0,4},{4,0},{8,12},{12,8},{16,20},{20,16},{24,28},{28,24},{1,5},{5... | collective-permute-start | bytes 786440 | tf_op jit(solution)/shard_map/ppermute | solution.py:58
  36.0 2.9 %collective-permute-start.15 = (bf16[64,256]{1,0:T(8,128)(2,1)S(1)}, bf16[64,256]{1,0:T(8,128)(2,1)S(1)}, u32[]{:S(2)}, u32[]{:S(2)}) collective-permute-start(bf16[64,256]{1,0:T(8,128)(2,1)S(1)} %get-tuple-element.88.refs_0_), channel_id=1, source_target_pairs={{0,16},{4,20},{8,24},{12,28},{16,0},{20,4},{24,8},{28,12},{1,17},{... | collective-permute-start | bytes 98312 | tf_op jit(solution)/shard_map/ppermute | solution.py:58
  38.9 2.6 %collective-permute-done.14.arrived = bf16[256,256]{1,0:T(8,128)(2,1)S(1)} collective-permute-done((bf16[256,256]{1,0:T(8,128)(2,1)S(1)}, bf16[256,256]{1,0:T(8,128)(2,1)S(1)}, u32[]{:S(2)}, u32[]{:S(2)}) %collective-permute-start.14) | collective-permute-done | bytes 131104 | tf_op jit(solution)/shard_map/ppermute | solution.py:58
  41.5 0.3 collective-permute-start.16
  41.7 0.8 %collective-permute-start.17 = (bf16[128,256]{1,0:T(8,128)(2,1)S(1)}, bf16[128,256]{1,0:T(8,128)(2,1)S(1)}, u32[]{:S(2)}, u32[]{:S(2)}) collective-permute-start(bf16[128,256]{1,0:T(8,128)(2,1)S(1)} %shard_map.128.refs_0_), channel_id=1, source_target_pairs={{0,8},{4,12},{8,0},{12,4},{16,24},{20,28},{24,16},{28,20},{1,9},{5... | collective-permute-start | bytes 196616 | tf_op jit(solution)/shard_map/ppermute | solution.py:58
  42.6 0.3 shard_map.129.total
  42.9 1.2 %collective-permute-done.18.cells = bf16[512,256]{1,0:T(8,128)(2,1)S(1)} collective-permute-done((bf16[512,256]{1,0:T(8,128)(2,1)S(1)}, bf16[512,256]{1,0:T(8,128)(2,1)S(1)}, u32[]{:S(2)}, u32[]{:S(2)}) %collective-permute-start.18) | collective-permute-done | bytes 262176 | tf_op jit(solution)/shard_map/ppermute | solution.py:58
  44.1 1.9 %collective-permute-start.19 = (bf16[512,256]{1,0:T(8,128)(2,1)S(1)}, bf16[512,256]{1,0:T(8,128)(2,1)S(1)}, u32[]{:S(2)}, u32[]{:S(2)}) collective-permute-start(bf16[512,256]{1,0:T(8,128)(2,1)S(1)} %collective-permute-done.18.cells), channel_id=1, source_target_pairs={{0,8},{4,0},{8,16},{12,4},{16,24},{20,12},{24,28},{28,20},{1,9},{5... | collective-permute-start | bytes 786440 | tf_op jit(solution)/shard_map/ppermute | solution.py:69
  46.0 0.2 collective-permute-done.16.arrived
  46.2 2.5 %collective-permute-start.20 = (bf16[256,256]{1,0:T(8,128)(2,1)S(1)}, bf16[256,256]{1,0:T(8,128)(2,1)S(1)}, u32[]{:S(2)}, u32[]{:S(2)}) collective-permute-start(bf16[256,256]{1,0:T(8,128)(2,1)S(1)} %shard_map.131.mine), channel_id=1, source_target_pairs={{0,4},{4,0},{8,12},{12,8},{16,20},{20,16},{24,28},{28,24},{1,5},{5... | collective-permute-start | bytes 393224 | tf_op jit(solution)/shard_map/ppermute | solution.py:58
  48.7 0.9 %collective-permute-start.21 = (bf16[64,256]{1,0:T(8,128)(2,1)S(1)}, bf16[64,256]{1,0:T(8,128)(2,1)S(1)}, u32[]{:S(2)}, u32[]{:S(2)}) collective-permute-start(bf16[64,256]{1,0:T(8,128)(2,1)S(1)} %get-tuple-element.97), channel_id=1, source_target_pairs={{0,16},{4,20},{8,24},{12,28},{16,0},{20,4},{24,8},{28,12},{1,17},{... | collective-permute-start | bytes 98312 | tf_op jit(solution)/shard_map/ppermute | solution.py:58
  49.6 0.3 shard_map.132.total
  49.9 3.6 %collective-permute-done.21.refs_1_ = bf16[64,256]{1,0:T(8,128)(2,1)S(1)} collective-permute-done((bf16[64,256]{1,0:T(8,128)(2,1)S(1)}, bf16[64,256]{1,0:T(8,128)(2,1)S(1)}, u32[]{:S(2)}, u32[]{:S(2)}) %collective-permute-start.21) | collective-permute-done | bytes 32800 | tf_op jit(solution)/shard_map/ppermute | solution.py:58
  53.6 0.7 %collective-permute-done.20.theirs = bf16[256,256]{1,0:T(8,128)(2,1)S(1)} collective-permute-done((bf16[256,256]{1,0:T(8,128)(2,1)S(1)}, bf16[256,256]{1,0:T(8,128)(2,1)S(1)}, u32[]{:S(2)}, u32[]{:S(2)}) %collective-permute-start.20) | collective-permute-done | bytes 131104 | tf_op jit(solution)/shard_map/ppermute | solution.py:58
  54.2 1.3 %shard_map.133 = (f32[512,256]{1,0:T(8,128)}, f32[64,256]{1,0:T(8,128)}) custom-call(f32[512,256]{1,0:T(8,128)S(1)} %shard_map.132.total, bf16[512,512]{1,0:T(8,128)(2,1)S(1)} %get-tuple-element.62.far, bf16[512,256]{1,0:T(8,128)(2,1)S(1)} %collective-permute-done.19.other, bf16[512,512]{1,0:T(8,128)(2,1)S(1)} %get-tuple-element.61.masked, ...), custom_call_target="tpu_custom_call" | custom-call | flops 500000000 | bytes 2785280 | tf_op jit(solution)/shard_map/pallas_call | solution.py:41
  (38 shorter events, 0.2 us)
Async XLA Ops:
  0.6 1.0 %copy-start.3 = (f32[512,256]{1,0:T(8,128)S(1)}, f32[512,256]{1,0:T(8,128)}, u32[]{:S(2)}) copy-start(f32[512,256]{1,0:T(8,128)} %cells.1) | copy-start | bytes 1572868
  1.7 3.1 %copy-start.4 = (bf16[512,512]{1,0:T(8,128)(2,1)S(1)}, bf16[512,512]{1,0:T(8,128)(2,1)}, u32[]{:S(2)}) copy-start(bf16[512,512]{1,0:T(8,128)(2,1)} %rows.3) | copy-start | bytes 1572868
  1.7 3.1 %copy-start.7 = (f32[64,256]{1,0:T(8,128)S(1)}, f32[64,256]{1,0:T(8,128)}, u32[]{:S(2)}) copy-start(f32[64,256]{1,0:T(8,128)} %refs_0_.1) | copy-start | bytes 196612
  1.7 7.6 %copy-start = (bf16[2,1024,256]{2,1,0:T(8,128)(2,1)S(1)}, bf16[2,1024,256]{2,1,0:T(8,128)(2,1)}, u32[]{:S(2)}) copy-start(bf16[2,1024,256]{2,1,0:T(8,128)(2,1)} %refs_10_.1) | copy-start | bytes 3145732
  1.7 12.7 %collective-permute-start.3 = (bf16[512,256]{1,0:T(8,128)(2,1)S(1)}, bf16[512,256]{1,0:T(8,128)(2,1)S(1)}, u32[]{:S(2)}, u32[]{:S(2)}) collective-permute-start(bf16[512,256]{1,0:T(8,128)(2,1)S(1)} %shard_map.113.cells), channel_id=1, source_target_pairs={{0,4},{4,0},{8,12},{12,8},{16,20},{20,16},{24,28},{28,24},{1,5},{5... | collective-permute-start | bytes 786440 | tf_op jit(solution)/shard_map/ppermute | solution.py:58
  5.1 5.9 %collective-permute-start = (bf16[64,256]{1,0:T(8,128)(2,1)S(1)}, bf16[64,256]{1,0:T(8,128)(2,1)S(1)}, u32[]{:S(2)}, u32[]{:S(2)}) collective-permute-start(bf16[64,256]{1,0:T(8,128)(2,1)S(1)} %get-tuple-element.52.refs_0_), channel_id=1, source_target_pairs={{0,16},{4,20},{8,24},{12,28},{16,0},{20,4},{24,8},{28,12},{1,17},{... | collective-permute-start | bytes 98312 | tf_op jit(solution)/shard_map/ppermute | solution.py:58
  7.7 5.5 %collective-permute-start.1 = (bf16[256,256]{1,0:T(8,128)(2,1)S(1)}, bf16[256,256]{1,0:T(8,128)(2,1)S(1)}, u32[]{:S(2)}, u32[]{:S(2)}) collective-permute-start(bf16[256,256]{1,0:T(8,128)(2,1)S(1)} %get-tuple-element.54), channel_id=1, source_target_pairs={{0,8},{4,12},{8,0},{12,4},{16,24},{20,28},{24,16},{28,20},{1,9},{5... | collective-permute-start | bytes 393224 | tf_op jit(solution)/shard_map/ppermute | solution.py:58
  9.3 17.7 %collective-permute-start.10 = (bf16[1024,256]{1,0:T(8,128)(2,1)S(1)}, bf16[1024,256]{1,0:T(8,128)(2,1)S(1)}, u32[]{:S(2)}, u32[]{:S(2)}) collective-permute-start(bf16[1024,256]{1,0:T(8,128)(2,1)S(1)} %slice_bitcast_fusion.refs_2_), channel_id=1, source_target_pairs={{0,2},{1,3},{2,0},{3,1},{4,6},{5,7},{6,4},{7,5},{8,10},{9,11},{10,... | collective-permute-start | bytes 1572872 | tf_op jit(solution)/shard_map/ppermute | solution.py:58
  10.9 5.3 %collective-permute-start.2 = (bf16[128,256]{1,0:T(8,128)(2,1)S(1)}, bf16[128,256]{1,0:T(8,128)(2,1)S(1)}, u32[]{:S(2)}, u32[]{:S(2)}) collective-permute-start(bf16[128,256]{1,0:T(8,128)(2,1)S(1)} %shard_map.115.refs_0_), channel_id=1, source_target_pairs={{0,8},{4,12},{8,0},{12,4},{16,24},{20,28},{24,16},{28,20},{1,9},{5... | collective-permute-start | bytes 196616 | tf_op jit(solution)/shard_map/ppermute | solution.py:58
  13.2 3.6 %copy-start.1 = (bf16[32,128,128]{2,1,0:T(8,128)(2,1)S(1)}, bf16[32,128,128]{2,1,0:T(8,128)(2,1)}, u32[]{:S(2)}) copy-start(bf16[32,128,128]{2,1,0:T(8,128)(2,1)} %tiles.1) | copy-start | bytes 3145732
  13.2 3.6 %copy-start.2 = (bf16[512,512]{1,0:T(8,128)(2,1)S(1)}, bf16[512,512]{1,0:T(8,128)(2,1)}, u32[]{:S(2)}) copy-start(bf16[512,512]{1,0:T(8,128)(2,1)} %cols.1) | copy-start | bytes 1572868
  13.2 5.7 %collective-permute-start.6 = (bf16[128,256]{1,0:T(8,128)(2,1)S(1)}, bf16[128,256]{1,0:T(8,128)(2,1)S(1)}, u32[]{:S(2)}, u32[]{:S(2)}) collective-permute-start(bf16[128,256]{1,0:T(8,128)(2,1)S(1)} %get-tuple-element.65), channel_id=1, source_target_pairs={{0,4},{4,0},{8,12},{12,8},{16,20},{20,16},{24,28},{28,24},{1,5},{5... | collective-permute-start | bytes 196616 | tf_op jit(solution)/shard_map/ppermute | solution.py:58
  14.4 10.5 %collective-permute-start.5 = (bf16[512,256]{1,0:T(8,128)(2,1)S(1)}, bf16[512,256]{1,0:T(8,128)(2,1)S(1)}, u32[]{:S(2)}, u32[]{:S(2)}) collective-permute-start(bf16[512,256]{1,0:T(8,128)(2,1)S(1)} %collective-permute-done.3.cells), channel_id=1, source_target_pairs={{0,8},{4,0},{8,16},{12,4},{16,24},{20,12},{24,28},{28,20},{1,9},{5... | collective-permute-start | bytes 786440 | tf_op jit(solution)/shard_map/ppermute | solution.py:69
  16.2 0.7 %copy-start.6 = (s32[512]{0:T(512)S(1)}, s32[512]{0:T(512)}, u32[]{:S(2)}) copy-start(s32[512]{0:T(512)} %param.16) | copy-start | bytes 6148
  16.2 0.7 %copy-start.5 = (s32[32,3]{0,1:T(4,128)S(1)}, s32[32,3]{0,1:T(4,128)}, u32[]{:S(2)}) copy-start(s32[32,3]{0,1:T(4,128)} %param.13) | copy-start | bytes 1156
  16.2 8.2 %collective-permute-start.4 = (bf16[256,256]{1,0:T(8,128)(2,1)S(1)}, bf16[256,256]{1,0:T(8,128)(2,1)S(1)}, u32[]{:S(2)}, u32[]{:S(2)}) collective-permute-start(bf16[256,256]{1,0:T(8,128)(2,1)S(1)} %shard_map.117.mine), channel_id=1, source_target_pairs={{0,4},{4,0},{8,12},{12,8},{16,20},{20,16},{24,28},{28,24},{1,5},{5... | collective-permute-start | bytes 393224 | tf_op jit(solution)/shard_map/ppermute | solution.py:58
  18.9 5.9 %collective-permute-start.7 = (bf16[64,256]{1,0:T(8,128)(2,1)S(1)}, bf16[64,256]{1,0:T(8,128)(2,1)S(1)}, u32[]{:S(2)}, u32[]{:S(2)}) collective-permute-start(bf16[64,256]{1,0:T(8,128)(2,1)S(1)} %get-tuple-element.67), channel_id=1, source_target_pairs={{0,16},{4,20},{8,24},{12,28},{16,0},{20,4},{24,8},{28,12},{1,17},{... | collective-permute-start | bytes 98312 | tf_op jit(solution)/shard_map/ppermute | solution.py:58
  24.9 1.9 %copy-start.9 = (s32[512]{0:T(512)S(1)}, s32[512]{0:T(512)}, u32[]{:S(2)}) copy-start(s32[512]{0:T(512)} %param.19) | copy-start | bytes 6148
  25.2 1.6 %copy-start.8 = (s32[512]{0:T(512)S(1)}, s32[512]{0:T(512)}, u32[]{:S(2)}) copy-start(s32[512]{0:T(512)} %param.18) | copy-start | bytes 6148
  25.2 6.8 %collective-permute-start.8 = (bf16[576,256]{1,0:T(8,128)(2,1)S(1)}, bf16[576,256]{1,0:T(8,128)(2,1)S(1)}, u32[]{:S(2)}, u32[]{:S(2)}) collective-permute-start(bf16[576,256]{1,0:T(8,128)(2,1)S(1)} %shard_map.121.refs_0_), channel_id=1, source_target_pairs={{0,2},{1,3},{2,0},{3,1},{4,6},{5,7},{6,4},{7,5},{8,10},{9,11},{10,... | collective-permute-start | bytes 884744 | tf_op jit(solution)/shard_map/ppermute | solution.py:58
  27.0 5.5 %collective-permute-start.12 = (bf16[1024,256]{1,0:T(8,128)(2,1)S(1)}, bf16[1024,256]{1,0:T(8,128)(2,1)S(1)}, u32[]{:S(2)}, u32[]{:S(2)}) collective-permute-start(bf16[1024,256]{1,0:T(8,128)(2,1)S(1)} %collective-permute-done.10.refs_3_), channel_id=1, source_target_pairs={{0,1},{1,0},{2,3},{3,2},{4,5},{5,4},{6,7},{7,6},{8,9},{9,8},{10,11... | collective-permute-start | bytes 1572872 | tf_op jit(solution)/shard_map/ppermute | solution.py:58
  27.1 5.4 %collective-permute-start.11 = (bf16[1024,256]{1,0:T(8,128)(2,1)S(1)}, bf16[1024,256]{1,0:T(8,128)(2,1)S(1)}, u32[]{:S(2)}, u32[]{:S(2)}) collective-permute-start(bf16[1024,256]{1,0:T(8,128)(2,1)S(1)} %slice_bitcast_fusion.refs_2_), channel_id=1, source_target_pairs={{0,1},{1,0},{2,3},{3,2},{4,5},{5,4},{6,7},{7,6},{8,9},{9,8},{10,11... | collective-permute-start | bytes 1572872 | tf_op jit(solution)/shard_map/ppermute | solution.py:58
  27.6 4.4 %collective-permute-start.13 = (bf16[576,256]{1,0:T(8,128)(2,1)S(1)}, bf16[576,256]{1,0:T(8,128)(2,1)S(1)}, u32[]{:S(2)}, u32[]{:S(2)}) collective-permute-start(bf16[576,256]{1,0:T(8,128)(2,1)S(1)} %shard_map.121.refs_0_), channel_id=1, source_target_pairs={{0,1},{1,0},{2,3},{3,2},{4,5},{5,4},{6,7},{7,6},{8,9},{9,8},{10,11... | collective-permute-start | bytes 884744 | tf_op jit(solution)/shard_map/ppermute | solution.py:58
  32.0 1.6 %collective-permute-start.9 = (bf16[576,256]{1,0:T(8,128)(2,1)S(1)}, bf16[576,256]{1,0:T(8,128)(2,1)S(1)}, u32[]{:S(2)}, u32[]{:S(2)}) collective-permute-start(bf16[576,256]{1,0:T(8,128)(2,1)S(1)} %collective-permute-done.8.refs_0_), channel_id=1, source_target_pairs={{0,1},{1,0},{2,3},{3,2},{4,5},{5,4},{6,7},{7,6},{8,9},{9,8},{10,11... | collective-permute-start | bytes 884744 | tf_op jit(solution)/shard_map/ppermute | solution.py:58
  35.1 6.3 %collective-permute-start.14 = (bf16[256,256]{1,0:T(8,128)(2,1)S(1)}, bf16[256,256]{1,0:T(8,128)(2,1)S(1)}, u32[]{:S(2)}, u32[]{:S(2)}) collective-permute-start(bf16[256,256]{1,0:T(8,128)(2,1)S(1)} %get-tuple-element.86), channel_id=1, source_target_pairs={{0,8},{4,12},{8,0},{12,4},{16,24},{20,28},{24,16},{28,20},{1,9},{5... | collective-permute-start | bytes 393224 | tf_op jit(solution)/shard_map/ppermute | solution.py:58
  35.2 8.9 %collective-permute-start.18 = (bf16[512,256]{1,0:T(8,128)(2,1)S(1)}, bf16[512,256]{1,0:T(8,128)(2,1)S(1)}, u32[]{:S(2)}, u32[]{:S(2)}) collective-permute-start(bf16[512,256]{1,0:T(8,128)(2,1)S(1)} %get-tuple-element.95.cells), channel_id=1, source_target_pairs={{0,4},{4,0},{8,12},{12,8},{16,20},{20,16},{24,28},{28,24},{1,5},{5... | collective-permute-start | bytes 786440 | tf_op jit(solution)/shard_map/ppermute | solution.py:58
  36.0 5.8 %collective-permute-start.15 = (bf16[64,256]{1,0:T(8,128)(2,1)S(1)}, bf16[64,256]{1,0:T(8,128)(2,1)S(1)}, u32[]{:S(2)}, u32[]{:S(2)}) collective-permute-start(bf16[64,256]{1,0:T(8,128)(2,1)S(1)} %get-tuple-element.88.refs_0_), channel_id=1, source_target_pairs={{0,16},{4,20},{8,24},{12,28},{16,0},{20,4},{24,8},{28,12},{1,17},{... | collective-permute-start | bytes 98312 | tf_op jit(solution)/shard_map/ppermute | solution.py:58
  41.5 4.7 %collective-permute-start.16 = (bf16[128,256]{1,0:T(8,128)(2,1)S(1)}, bf16[128,256]{1,0:T(8,128)(2,1)S(1)}, u32[]{:S(2)}, u32[]{:S(2)}) collective-permute-start(bf16[128,256]{1,0:T(8,128)(2,1)S(1)} %get-tuple-element.91), channel_id=1, source_target_pairs={{0,4},{4,0},{8,12},{12,8},{16,20},{20,16},{24,28},{28,24},{1,5},{5... | collective-permute-start | bytes 196616 | tf_op jit(solution)/shard_map/ppermute | solution.py:58
  41.7 4.4 %collective-permute-start.17 = (bf16[128,256]{1,0:T(8,128)(2,1)S(1)}, bf16[128,256]{1,0:T(8,128)(2,1)S(1)}, u32[]{:S(2)}, u32[]{:S(2)}) collective-permute-start(bf16[128,256]{1,0:T(8,128)(2,1)S(1)} %shard_map.128.refs_0_), channel_id=1, source_target_pairs={{0,8},{4,12},{8,0},{12,4},{16,24},{20,28},{24,16},{28,20},{1,9},{5... | collective-permute-start | bytes 196616 | tf_op jit(solution)/shard_map/ppermute | solution.py:58
  44.1 10.1 %collective-permute-start.19 = (bf16[512,256]{1,0:T(8,128)(2,1)S(1)}, bf16[512,256]{1,0:T(8,128)(2,1)S(1)}, u32[]{:S(2)}, u32[]{:S(2)}) collective-permute-start(bf16[512,256]{1,0:T(8,128)(2,1)S(1)} %collective-permute-done.18.cells), channel_id=1, source_target_pairs={{0,8},{4,0},{8,16},{12,4},{16,24},{20,12},{24,28},{28,20},{1,9},{5... | collective-permute-start | bytes 786440 | tf_op jit(solution)/shard_map/ppermute | solution.py:69
  46.2 8.0 %collective-permute-start.20 = (bf16[256,256]{1,0:T(8,128)(2,1)S(1)}, bf16[256,256]{1,0:T(8,128)(2,1)S(1)}, u32[]{:S(2)}, u32[]{:S(2)}) collective-permute-start(bf16[256,256]{1,0:T(8,128)(2,1)S(1)} %shard_map.131.mine), channel_id=1, source_target_pairs={{0,4},{4,0},{8,12},{12,8},{16,20},{20,16},{24,28},{28,24},{1,5},{5... | collective-permute-start | bytes 393224 | tf_op jit(solution)/shard_map/ppermute | solution.py:58
  48.7 4.8 %collective-permute-start.21 = (bf16[64,256]{1,0:T(8,128)(2,1)S(1)}, bf16[64,256]{1,0:T(8,128)(2,1)S(1)}, u32[]{:S(2)}, u32[]{:S(2)}) collective-permute-start(bf16[64,256]{1,0:T(8,128)(2,1)S(1)} %get-tuple-element.97), channel_id=1, source_target_pairs={{0,16},{4,20},{8,24},{12,28},{16,0},{20,4},{24,8},{28,12},{1,17},{... | collective-permute-start | bytes 98312 | tf_op jit(solution)/shard_map/ppermute | solution.py:58

commit v6 on v5

--- a/solution.py
+++ b/solution.py
@@ -13,6 +13,7 @@
 WORK = {
     "cast": 1_000_000,
     "part1": 2_000_000_000,
+    "own": 10_000,
     "dense": 1_000_000,
     "join1": 200_000_000,
     "fold1": 2_000_000_000,
@@ -123,7 +124,7 @@
     split_partial(part, keep, send, head_dev, bits)
 
 
-def dense_kernel(place, tiles, cols, reach, cells, near, pair, far, masked, own, window, *, blocks):
+def dense_kernel(place, tiles, near, pair, far, window, *, blocks):
     tile = tiles.shape[1]
     rows = window.shape[0]
     tile_rows = rows // tile
@@ -148,6 +149,10 @@
     near[...] = window[:, :rows].astype(BF)
     pair[...] = window[:, rows : 2 * rows].astype(BF)
     far[...] = window[:, 2 * rows :].astype(BF)
+
+
+def own_kernel(cols, reach, near, cells, masked, own):
+    rows = masked.shape[0]
     limit = column(reach[...], 128)
     for g in range(cols.shape[1] // 128):
         here = slice(g * 128, (g + 1) * 128)
@@ -341,17 +346,24 @@
     laid = []
 
     def lay_out(before):
-        outs = [((rows_dev, rows_dev), BF)] * 3 + [((rows_dev, heads), BF)] + band_sum
-        args = (tile_vals, arrow_cols, reach, after(cells, before))
+        outs = [((rows_dev, rows_dev), BF)] * 3
+        args = (after(tile_vals, before),)
         scratch = [pltpu.VMEM((rows_dev, 3 * rows_dev), F32)]
         kernel = functools.partial(dense_kernel, blocks=blocks)
         laid.extend(local("dense", kernel, outs, (tile_place.T,), args, scratch))
         return laid[-1]
 
     mine, theirs, parts = exchange(
-        "join1", "fold1", head_cells, keep, send, keep, bits, "jfjf", 3, lay_out
-    )
-    near, pair, far, masked, total = laid
+        "join1", "fold1", head_cells, keep, send, keep, bits, "jfjf", 2, lay_out
+    )
+    near, pair, far = laid
+    masked, total = local(
+        "own",
+        own_kernel,
+        [((rows_dev, heads), BF)] + band_sum,
+        (),
+        (arrow_cols, reach, after(near, *parts[:1]), cells),
+    )
     far_cells = forward(after(pair_cells, first_part))
     (total,) = local(
         "sum1", sum_up, band_sum, (), (total, pair, pair_cells, masked, mine, theirs), [head_scratch]

time: 55.7 us -> 55.7 us (level)
  starting transfers between devices: 27.7 us -> 26.4 us
  waiting for transfers between devices: 17.9 us -> 18.5 us
  local copies, waits for them, and re-layouts: 1.19 us -> 1.79 us
    ppermute x20, starting transfers between devices: 24 us -> 22.7 us  [swap(): return lax.ppermute(cells, axis, [(i, i ^ bit) for i in range(count)])]
    unnamed x20, local copies, waits for them, and re-layouts: 1.16 us -> 1.76 us
    ppermute x20, waiting for transfers between devices: 17.9 us -> 18.5 us  [swap(): return lax.ppermute(cells, axis, [(i, i ^ bit) for i in range(count)])]
    pallas_call x21 -> x22, Pallas kernels: 7.79 us -> 7.87 us  [local(): pl.pallas_call(kernel, out_shape=[jax.ShapeDtypeStruct(s, d) for s, d in...]
where the time goes in v6:
time: 55.7 us; the launch traced here: 55.5 us
  starting transfers between devices  26.4 us (47%)
  waiting for transfers between devices  18.5 us (33%)
  Pallas kernels  7.87 us (14%)
  local copies, waits for them, and re-layouts  1.79 us (3%)
  between operations  0.92 us (2%)
    ppermute x20, starting transfers between devices, swap(): return lax.ppermute(cells, axis, [(i, i ^ bit) for i in range(count)])  22.7 us
    ppermute x20, waiting for transfers between devices, swap(): return lax.ppermute(cells, axis, [(i, i ^ bit) for i in range(count)])  18.5 us
    pallas_call x22, Pallas kernels, local(): pl.pallas_call(kernel, out_shape=[jax.ShapeDtypeStruct(s, d) for s, d in...  7.87 us
    ppermute x2, starting transfers between devices, forward(): return lax.ppermute(cells, 'rows', pairs)  3.73 us
    unnamed x20, local copies, waits for them, and re-layouts  1.76 us
  transfers between devices with their start and end apart: 22, of which 9 were waited for; matrix products, arithmetic and copies ran while one was open for 0% of the time, Pallas kernels for 9%

profile of v6, /device:TPU:0, one launch (start us, length us, event | category | flops | bytes accessed | tf_op | source)
XLA Modules:
  0.0 55.5 jit_solution(16771304661316872997)
XLA Ops:
  0.6 1.0 %copy-done.3 = f32[512,256]{1,0:T(8,128)S(1)} copy-done((f32[512,256]{1,0:T(8,128)S(1)}, f32[512,256]{1,0:T(8,128)}, u32[]{:S(2)}) %copy-start.3) | copy-done | bytes 524312
  1.7 0.0 copy-start
  1.7 3.0 %collective-permute-start.4 = (bf16[512,256]{1,0:T(8,128)(2,1)S(1)}, bf16[512,256]{1,0:T(8,128)(2,1)S(1)}, u32[]{:S(2)}, u32[]{:S(2)}) collective-permute-start(bf16[512,256]{1,0:T(8,128)(2,1)S(1)} %shard_map.113.cells), channel_id=1, source_target_pairs={{0,4},{4,0},{8,12},{12,8},{16,20},{20,16},{24,28},{28,24},{1,5},{5... | collective-permute-start | bytes 786440 | tf_op jit(solution)/shard_map/ppermute | solution.py:59
  4.7 0.3 shard_map.114
  5.1 2.7 %collective-permute-start = (bf16[64,256]{1,0:T(8,128)(2,1)S(1)}, bf16[64,256]{1,0:T(8,128)(2,1)S(1)}, u32[]{:S(2)}, u32[]{:S(2)}) collective-permute-start(bf16[64,256]{1,0:T(8,128)(2,1)S(1)} %get-tuple-element.53.refs_0_), channel_id=1, source_target_pairs={{0,16},{4,20},{8,24},{12,28},{16,0},{20,4},{24,8},{28,12},{1,17},{... | collective-permute-start | bytes 98312 | tf_op jit(solution)/shard_map/ppermute | solution.py:59
  7.7 1.6 %collective-permute-start.1 = (bf16[256,256]{1,0:T(8,128)(2,1)S(1)}, bf16[256,256]{1,0:T(8,128)(2,1)S(1)}, u32[]{:S(2)}, u32[]{:S(2)}) collective-permute-start(bf16[256,256]{1,0:T(8,128)(2,1)S(1)} %get-tuple-element.55), channel_id=1, source_target_pairs={{0,8},{4,12},{8,0},{12,4},{16,24},{20,28},{24,16},{28,20},{1,9},{5... | collective-permute-start | bytes 393224 | tf_op jit(solution)/shard_map/ppermute | solution.py:59
  9.3 1.6 %collective-permute-start.10 = (bf16[1024,256]{1,0:T(8,128)(2,1)S(1)}, bf16[1024,256]{1,0:T(8,128)(2,1)S(1)}, u32[]{:S(2)}, u32[]{:S(2)}) collective-permute-start(bf16[1024,256]{1,0:T(8,128)(2,1)S(1)} %slice_bitcast_fusion.refs_2_), channel_id=1, source_target_pairs={{0,2},{1,3},{2,0},{3,1},{4,6},{5,7},{6,4},{7,5},{8,10},{9,11},{10,... | collective-permute-start | bytes 1572872 | tf_op jit(solution)/shard_map/ppermute | solution.py:59
  10.9 1.0 %collective-permute-start.2 = (bf16[128,256]{1,0:T(8,128)(2,1)S(1)}, bf16[128,256]{1,0:T(8,128)(2,1)S(1)}, u32[]{:S(2)}, u32[]{:S(2)}) collective-permute-start(bf16[128,256]{1,0:T(8,128)(2,1)S(1)} %shard_map.115.refs_0_), channel_id=1, source_target_pairs={{0,8},{4,12},{8,0},{12,4},{16,24},{20,28},{24,16},{28,20},{1,9},{5... | collective-permute-start | bytes 196616 | tf_op jit(solution)/shard_map/ppermute | solution.py:59
  11.9 1.2 %collective-permute-done.1.arrived = bf16[256,256]{1,0:T(8,128)(2,1)S(1)} collective-permute-done((bf16[256,256]{1,0:T(8,128)(2,1)S(1)}, bf16[256,256]{1,0:T(8,128)(2,1)S(1)}, u32[]{:S(2)}, u32[]{:S(2)}) %collective-permute-start.1) | collective-permute-done | bytes 131104 | tf_op jit(solution)/shard_map/ppermute | solution.py:59
  13.2 1.1 %collective-permute-start.3 = (bf16[128,256]{1,0:T(8,128)(2,1)S(1)}, bf16[128,256]{1,0:T(8,128)(2,1)S(1)}, u32[]{:S(2)}, u32[]{:S(2)}) collective-permute-start(bf16[128,256]{1,0:T(8,128)(2,1)S(1)} %get-tuple-element.62), channel_id=1, source_target_pairs={{0,4},{4,0},{8,12},{12,8},{16,20},{20,16},{24,28},{28,24},{1,5},{5... | collective-permute-start | bytes 196616 | tf_op jit(solution)/shard_map/ppermute | solution.py:59
  14.4 1.8 %collective-permute-start.6 = (bf16[512,256]{1,0:T(8,128)(2,1)S(1)}, bf16[512,256]{1,0:T(8,128)(2,1)S(1)}, u32[]{:S(2)}, u32[]{:S(2)}) collective-permute-start(bf16[512,256]{1,0:T(8,128)(2,1)S(1)} %collective-permute-done.4.cells), channel_id=1, source_target_pairs={{0,8},{4,0},{8,16},{12,4},{16,24},{20,12},{24,28},{28,20},{1,9},{5... | collective-permute-start | bytes 786440 | tf_op jit(solution)/shard_map/ppermute | solution.py:70
  16.2 1.8 %shard_map.117 = (bf16[512,512]{1,0:T(8,128)(2,1)S(1)}, bf16[512,512]{1,0:T(8,128)(2,1)S(1)}, bf16[512,512]{1,0:T(8,128)(2,1)S(1)}) custom-call(s32[3,32]{1,0:T(4,128)S(1)} %bitcast.6, bf16[32,128,128]{2,1,0:T(8,128)(2,1)S(1)} %copy-done.1), custom_call_target="tpu_custom_call" | custom-call | flops 1000000 | bytes 1048576 | tf_op jit(solution)/shard_map/pallas_call | solution.py:42
  18.0 0.0 copy-start.2
  18.0 0.4 collective-permute-start.5
  18.5 2.3 %collective-permute-start.7 = (bf16[64,256]{1,0:T(8,128)(2,1)S(1)}, bf16[64,256]{1,0:T(8,128)(2,1)S(1)}, u32[]{:S(2)}, u32[]{:S(2)}) collective-permute-start(bf16[64,256]{1,0:T(8,128)(2,1)S(1)} %get-tuple-element.69), channel_id=1, source_target_pairs={{0,16},{4,20},{8,24},{12,28},{16,0},{20,4},{24,8},{28,12},{1,17},{... | collective-permute-start | bytes 98312 | tf_op jit(solution)/shard_map/ppermute | solution.py:59
  20.8 0.7 %copy-done.6 = s32[512]{0:T(512)S(1)} copy-done((s32[512]{0:T(512)S(1)}, s32[512]{0:T(512)}, u32[]{:S(2)}) %copy-start.6) | copy-done | bytes 2072
  21.4 0.3 shard_map.120
  21.8 2.6 %collective-permute-done.5.theirs = bf16[256,256]{1,0:T(8,128)(2,1)S(1)} collective-permute-done((bf16[256,256]{1,0:T(8,128)(2,1)S(1)}, bf16[256,256]{1,0:T(8,128)(2,1)S(1)}, u32[]{:S(2)}, u32[]{:S(2)}) %collective-permute-start.5) | collective-permute-done | bytes 131104 | tf_op jit(solution)/shard_map/ppermute | solution.py:59
  24.4 0.5 shard_map.121.total
  24.9 0.0 copy-start.9
  24.9 0.3 shard_map.122.refs_0_
  25.2 0.0 copy-start.8
  25.2 1.6 %collective-permute-start.8 = (bf16[576,256]{1,0:T(8,128)(2,1)S(1)}, bf16[576,256]{1,0:T(8,128)(2,1)S(1)}, u32[]{:S(2)}, u32[]{:S(2)}) collective-permute-start(bf16[576,256]{1,0:T(8,128)(2,1)S(1)} %shard_map.122.refs_0_), channel_id=1, source_target_pairs={{0,2},{1,3},{2,0},{3,1},{4,6},{5,7},{6,4},{7,5},{8,10},{9,11},{10,... | collective-permute-start | bytes 884744 | tf_op jit(solution)/shard_map/ppermute | solution.py:59
  26.8 0.2 shard_map.123
  27.0 0.1 collective-permute-start.12
  27.1 0.5 collective-permute-start.11
  27.6 0.1 collective-permute-start.13
  27.7 4.3 %collective-permute-done.8.refs_0_ = bf16[576,256]{1,0:T(8,128)(2,1)S(1)} collective-permute-done((bf16[576,256]{1,0:T(8,128)(2,1)S(1)}, bf16[576,256]{1,0:T(8,128)(2,1)S(1)}, u32[]{:S(2)}, u32[]{:S(2)}) %collective-permute-start.8) | collective-permute-done | bytes 294944 | tf_op jit(solution)/shard_map/ppermute | solution.py:59
  32.0 0.5 shard_map.124
  32.5 0.5 shard_map.125
  33.0 0.6 %collective-permute-done.9.refs_1_ = bf16[576,256]{1,0:T(8,128)(2,1)S(1)} collective-permute-done((bf16[576,256]{1,0:T(8,128)(2,1)S(1)}, bf16[576,256]{1,0:T(8,128)(2,1)S(1)}, u32[]{:S(2)}, u32[]{:S(2)}) %collective-permute-start.9) | collective-permute-done | bytes 294944 | tf_op jit(solution)/shard_map/ppermute | solution.py:59
  33.6 1.2 %shard_map.126 = (bf16[512,256]{1,0:T(8,128)(2,1)S(1)}, bf16[64,256]{1,0:T(8,128)(2,1)S(1)}) custom-call(bf16[576,256]{1,0:T(8,128)(2,1)S(1)} %collective-permute-done.8.refs_0_, bf16[576,256]{1,0:T(8,128)(2,1)S(1)} %collective-permute-done.9.refs_1_, bf16[1024,256]{1,0:T(8,128)(2,1)S(1)} %slice_bitcast_fusion.refs_2_, ...), custom_call_target="tpu_custom_call" | custom-call | flops 500000000 | bytes 6684672 | tf_op jit(solution)/shard_map/pallas_call | solution.py:42
  34.8 0.3 shard_map.127
  35.1 0.2 collective-permute-start.14
  35.3 1.0 %collective-permute-start.18 = (bf16[512,256]{1,0:T(8,128)(2,1)S(1)}, bf16[512,256]{1,0:T(8,128)(2,1)S(1)}, u32[]{:S(2)}, u32[]{:S(2)}) collective-permute-start(bf16[512,256]{1,0:T(8,128)(2,1)S(1)} %get-tuple-element.97.cells), channel_id=1, source_target_pairs={{0,4},{4,0},{8,12},{12,8},{16,20},{20,16},{24,28},{28,24},{1,5},{5... | collective-permute-start | bytes 786440 | tf_op jit(solution)/shard_map/ppermute | solution.py:59
  36.4 2.2 %collective-permute-start.15 = (bf16[64,256]{1,0:T(8,128)(2,1)S(1)}, bf16[64,256]{1,0:T(8,128)(2,1)S(1)}, u32[]{:S(2)}, u32[]{:S(2)}) collective-permute-start(bf16[64,256]{1,0:T(8,128)(2,1)S(1)} %get-tuple-element.90.refs_0_), channel_id=1, source_target_pairs={{0,16},{4,20},{8,24},{12,28},{16,0},{20,4},{24,8},{28,12},{1,17},{... | collective-permute-start | bytes 98312 | tf_op jit(solution)/shard_map/ppermute | solution.py:59
  38.6 2.9 %collective-permute-done.14.arrived = bf16[256,256]{1,0:T(8,128)(2,1)S(1)} collective-permute-done((bf16[256,256]{1,0:T(8,128)(2,1)S(1)}, bf16[256,256]{1,0:T(8,128)(2,1)S(1)}, u32[]{:S(2)}, u32[]{:S(2)}) %collective-permute-start.14) | collective-permute-done | bytes 131104 | tf_op jit(solution)/shard_map/ppermute | solution.py:59
  41.5 0.1 collective-permute-start.16
  41.6 0.8 %collective-permute-start.17 = (bf16[128,256]{1,0:T(8,128)(2,1)S(1)}, bf16[128,256]{1,0:T(8,128)(2,1)S(1)}, u32[]{:S(2)}, u32[]{:S(2)}) collective-permute-start(bf16[128,256]{1,0:T(8,128)(2,1)S(1)} %shard_map.129.refs_0_), channel_id=1, source_target_pairs={{0,8},{4,12},{8,0},{12,4},{16,24},{20,28},{24,16},{28,20},{1,9},{5... | collective-permute-start | bytes 196616 | tf_op jit(solution)/shard_map/ppermute | solution.py:59
  42.4 0.3 shard_map.130.total
  42.7 1.4 %collective-permute-done.18.cells = bf16[512,256]{1,0:T(8,128)(2,1)S(1)} collective-permute-done((bf16[512,256]{1,0:T(8,128)(2,1)S(1)}, bf16[512,256]{1,0:T(8,128)(2,1)S(1)}, u32[]{:S(2)}, u32[]{:S(2)}) %collective-permute-start.18) | collective-permute-done | bytes 262176 | tf_op jit(solution)/shard_map/ppermute | solution.py:59
  44.1 1.9 %collective-permute-start.19 = (bf16[512,256]{1,0:T(8,128)(2,1)S(1)}, bf16[512,256]{1,0:T(8,128)(2,1)S(1)}, u32[]{:S(2)}, u32[]{:S(2)}) collective-permute-start(bf16[512,256]{1,0:T(8,128)(2,1)S(1)} %collective-permute-done.18.cells), channel_id=1, source_target_pairs={{0,8},{4,0},{8,16},{12,4},{16,24},{20,12},{24,28},{28,20},{1,9},{5... | collective-permute-start | bytes 786440 | tf_op jit(solution)/shard_map/ppermute | solution.py:70
  46.0 0.2 collective-permute-done.16.arrived
  46.2 2.5 %collective-permute-start.20 = (bf16[256,256]{1,0:T(8,128)(2,1)S(1)}, bf16[256,256]{1,0:T(8,128)(2,1)S(1)}, u32[]{:S(2)}, u32[]{:S(2)}) collective-permute-start(bf16[256,256]{1,0:T(8,128)(2,1)S(1)} %shard_map.132.mine), channel_id=1, source_target_pairs={{0,4},{4,0},{8,12},{12,8},{16,20},{20,16},{24,28},{28,24},{1,5},{5... | collective-permute-start | bytes 393224 | tf_op jit(solution)/shard_map/ppermute | solution.py:59
  48.7 0.3 shard_map.133.total
  49.0 4.5 %collective-permute-done.21.refs_1_ = bf16[64,256]{1,0:T(8,128)(2,1)S(1)} collective-permute-done((bf16[64,256]{1,0:T(8,128)(2,1)S(1)}, bf16[64,256]{1,0:T(8,128)(2,1)S(1)}, u32[]{:S(2)}, u32[]{:S(2)}) %collective-permute-start.21) | collective-permute-done | bytes 32800 | tf_op jit(solution)/shard_map/ppermute | solution.py:59
  53.5 0.7 %collective-permute-done.20.theirs = bf16[256,256]{1,0:T(8,128)(2,1)S(1)} collective-permute-done((bf16[256,256]{1,0:T(8,128)(2,1)S(1)}, bf16[256,256]{1,0:T(8,128)(2,1)S(1)}, u32[]{:S(2)}, u32[]{:S(2)}) %collective-permute-start.20) | collective-permute-done | bytes 131104 | tf_op jit(solution)/shard_map/ppermute | solution.py:59
  54.2 1.3 %shard_map.134 = (f32[512,256]{1,0:T(8,128)}, f32[64,256]{1,0:T(8,128)}) custom-call(f32[512,256]{1,0:T(8,128)S(1)} %shard_map.133.total, bf16[512,512]{1,0:T(8,128)(2,1)S(1)} %get-tuple-element.59.far, bf16[512,256]{1,0:T(8,128)(2,1)S(1)} %collective-permute-done.19.other, bf16[512,512]{1,0:T(8,128)(2,1)S(1)} %get-tuple-element.67.masked, ...), custom_call_target="tpu_custom_call" | custom-call | flops 500000000 | bytes 2785280 | tf_op jit(solution)/shard_map/pallas_call | solution.py:42
  (39 shorter events, 0.2 us)
Async XLA Ops:
  0.6 1.0 %copy-start.3 = (f32[512,256]{1,0:T(8,128)S(1)}, f32[512,256]{1,0:T(8,128)}, u32[]{:S(2)}) copy-start(f32[512,256]{1,0:T(8,128)} %cells.1) | copy-start | bytes 1572868
  1.7 3.1 %copy-start.4 = (bf16[512,512]{1,0:T(8,128)(2,1)S(1)}, bf16[512,512]{1,0:T(8,128)(2,1)}, u32[]{:S(2)}) copy-start(bf16[512,512]{1,0:T(8,128)(2,1)} %rows.3) | copy-start | bytes 1572868
  1.7 3.1 %copy-start.7 = (f32[64,256]{1,0:T(8,128)S(1)}, f32[64,256]{1,0:T(8,128)}, u32[]{:S(2)}) copy-start(f32[64,256]{1,0:T(8,128)} %refs_0_.1) | copy-start | bytes 196612
  1.7 7.6 %copy-start = (bf16[2,1024,256]{2,1,0:T(8,128)(2,1)S(1)}, bf16[2,1024,256]{2,1,0:T(8,128)(2,1)}, u32[]{:S(2)}) copy-start(bf16[2,1024,256]{2,1,0:T(8,128)(2,1)} %refs_10_.1) | copy-start | bytes 3145732
  1.7 12.6 %collective-permute-start.4 = (bf16[512,256]{1,0:T(8,128)(2,1)S(1)}, bf16[512,256]{1,0:T(8,128)(2,1)S(1)}, u32[]{:S(2)}, u32[]{:S(2)}) collective-permute-start(bf16[512,256]{1,0:T(8,128)(2,1)S(1)} %shard_map.113.cells), channel_id=1, source_target_pairs={{0,4},{4,0},{8,12},{12,8},{16,20},{20,16},{24,28},{28,24},{1,5},{5... | collective-permute-start | bytes 786440 | tf_op jit(solution)/shard_map/ppermute | solution.py:59
  5.1 5.9 %collective-permute-start = (bf16[64,256]{1,0:T(8,128)(2,1)S(1)}, bf16[64,256]{1,0:T(8,128)(2,1)S(1)}, u32[]{:S(2)}, u32[]{:S(2)}) collective-permute-start(bf16[64,256]{1,0:T(8,128)(2,1)S(1)} %get-tuple-element.53.refs_0_), channel_id=1, source_target_pairs={{0,16},{4,20},{8,24},{12,28},{16,0},{20,4},{24,8},{28,12},{1,17},{... | collective-permute-start | bytes 98312 | tf_op jit(solution)/shard_map/ppermute | solution.py:59
  7.7 5.4 %collective-permute-start.1 = (bf16[256,256]{1,0:T(8,128)(2,1)S(1)}, bf16[256,256]{1,0:T(8,128)(2,1)S(1)}, u32[]{:S(2)}, u32[]{:S(2)}) collective-permute-start(bf16[256,256]{1,0:T(8,128)(2,1)S(1)} %get-tuple-element.55), channel_id=1, source_target_pairs={{0,8},{4,12},{8,0},{12,4},{16,24},{20,28},{24,16},{28,20},{1,9},{5... | collective-permute-start | bytes 393224 | tf_op jit(solution)/shard_map/ppermute | solution.py:59
  9.3 17.7 %collective-permute-start.10 = (bf16[1024,256]{1,0:T(8,128)(2,1)S(1)}, bf16[1024,256]{1,0:T(8,128)(2,1)S(1)}, u32[]{:S(2)}, u32[]{:S(2)}) collective-permute-start(bf16[1024,256]{1,0:T(8,128)(2,1)S(1)} %slice_bitcast_fusion.refs_2_), channel_id=1, source_target_pairs={{0,2},{1,3},{2,0},{3,1},{4,6},{5,7},{6,4},{7,5},{8,10},{9,11},{10,... | collective-permute-start | bytes 1572872 | tf_op jit(solution)/shard_map/ppermute | solution.py:59
  10.9 5.3 %copy-start.1 = (bf16[32,128,128]{2,1,0:T(8,128)(2,1)S(1)}, bf16[32,128,128]{2,1,0:T(8,128)(2,1)}, u32[]{:S(2)}) copy-start(bf16[32,128,128]{2,1,0:T(8,128)(2,1)} %tiles) | copy-start | bytes 3145732
  10.9 7.0 %collective-permute-start.2 = (bf16[128,256]{1,0:T(8,128)(2,1)S(1)}, bf16[128,256]{1,0:T(8,128)(2,1)S(1)}, u32[]{:S(2)}, u32[]{:S(2)}) collective-permute-start(bf16[128,256]{1,0:T(8,128)(2,1)S(1)} %shard_map.115.refs_0_), channel_id=1, source_target_pairs={{0,8},{4,12},{8,0},{12,4},{16,24},{20,28},{24,16},{28,20},{1,9},{5... | collective-permute-start | bytes 196616 | tf_op jit(solution)/shard_map/ppermute | solution.py:59
  13.2 3.0 %copy-start.5 = (s32[32,3]{0,1:T(4,128)S(1)}, s32[32,3]{0,1:T(4,128)}, u32[]{:S(2)}) copy-start(s32[32,3]{0,1:T(4,128)} %param.13) | copy-start | bytes 1156
  13.2 5.2 %collective-permute-start.3 = (bf16[128,256]{1,0:T(8,128)(2,1)S(1)}, bf16[128,256]{1,0:T(8,128)(2,1)S(1)}, u32[]{:S(2)}, u32[]{:S(2)}) collective-permute-start(bf16[128,256]{1,0:T(8,128)(2,1)S(1)} %get-tuple-element.62), channel_id=1, source_target_pairs={{0,4},{4,0},{8,12},{12,8},{16,20},{20,16},{24,28},{28,24},{1,5},{5... | collective-permute-start | bytes 196616 | tf_op jit(solution)/shard_map/ppermute | solution.py:59
  14.4 10.5 %collective-permute-start.6 = (bf16[512,256]{1,0:T(8,128)(2,1)S(1)}, bf16[512,256]{1,0:T(8,128)(2,1)S(1)}, u32[]{:S(2)}, u32[]{:S(2)}) collective-permute-start(bf16[512,256]{1,0:T(8,128)(2,1)S(1)} %collective-permute-done.4.cells), channel_id=1, source_target_pairs={{0,8},{4,0},{8,16},{12,4},{16,24},{20,12},{24,28},{28,20},{1,9},{5... | collective-permute-start | bytes 786440 | tf_op jit(solution)/shard_map/ppermute | solution.py:70
  18.0 2.8 %copy-start.2 = (bf16[512,512]{1,0:T(8,128)(2,1)S(1)}, bf16[512,512]{1,0:T(8,128)(2,1)}, u32[]{:S(2)}) copy-start(bf16[512,512]{1,0:T(8,128)(2,1)} %cols.1) | copy-start | bytes 1572868
  18.0 6.4 %collective-permute-start.5 = (bf16[256,256]{1,0:T(8,128)(2,1)S(1)}, bf16[256,256]{1,0:T(8,128)(2,1)S(1)}, u32[]{:S(2)}, u32[]{:S(2)}) collective-permute-start(bf16[256,256]{1,0:T(8,128)(2,1)S(1)} %shard_map.118.mine), channel_id=1, source_target_pairs={{0,4},{4,0},{8,12},{12,8},{16,20},{20,16},{24,28},{28,24},{1,5},{5... | collective-permute-start | bytes 393224 | tf_op jit(solution)/shard_map/ppermute | solution.py:59
  18.5 6.4 %collective-permute-start.7 = (bf16[64,256]{1,0:T(8,128)(2,1)S(1)}, bf16[64,256]{1,0:T(8,128)(2,1)S(1)}, u32[]{:S(2)}, u32[]{:S(2)}) collective-permute-start(bf16[64,256]{1,0:T(8,128)(2,1)S(1)} %get-tuple-element.69), channel_id=1, source_target_pairs={{0,16},{4,20},{8,24},{12,28},{16,0},{20,4},{24,8},{28,12},{1,17},{... | collective-permute-start | bytes 98312 | tf_op jit(solution)/shard_map/ppermute | solution.py:59
  20.8 0.7 %copy-start.6 = (s32[512]{0:T(512)S(1)}, s32[512]{0:T(512)}, u32[]{:S(2)}) copy-start(s32[512]{0:T(512)} %param.16) | copy-start | bytes 6148
  24.9 1.9 %copy-start.9 = (s32[512]{0:T(512)S(1)}, s32[512]{0:T(512)}, u32[]{:S(2)}) copy-start(s32[512]{0:T(512)} %param.19) | copy-start | bytes 6148
  25.2 1.6 %copy-start.8 = (s32[512]{0:T(512)S(1)}, s32[512]{0:T(512)}, u32[]{:S(2)}) copy-start(s32[512]{0:T(512)} %param.18) | copy-start | bytes 6148
  25.2 6.8 %collective-permute-start.8 = (bf16[576,256]{1,0:T(8,128)(2,1)S(1)}, bf16[576,256]{1,0:T(8,128)(2,1)S(1)}, u32[]{:S(2)}, u32[]{:S(2)}) collective-permute-start(bf16[576,256]{1,0:T(8,128)(2,1)S(1)} %shard_map.122.refs_0_), channel_id=1, source_target_pairs={{0,2},{1,3},{2,0},{3,1},{4,6},{5,7},{6,4},{7,5},{8,10},{9,11},{10,... | collective-permute-start | bytes 884744 | tf_op jit(solution)/shard_map/ppermute | solution.py:59
  27.0 5.5 %collective-permute-start.12 = (bf16[1024,256]{1,0:T(8,128)(2,1)S(1)}, bf16[1024,256]{1,0:T(8,128)(2,1)S(1)}, u32[]{:S(2)}, u32[]{:S(2)}) collective-permute-start(bf16[1024,256]{1,0:T(8,128)(2,1)S(1)} %collective-permute-done.10.refs_3_), channel_id=1, source_target_pairs={{0,1},{1,0},{2,3},{3,2},{4,5},{5,4},{6,7},{7,6},{8,9},{9,8},{10,11... | collective-permute-start | bytes 1572872 | tf_op jit(solution)/shard_map/ppermute | solution.py:59
  27.1 5.4 %collective-permute-start.11 = (bf16[1024,256]{1,0:T(8,128)(2,1)S(1)}, bf16[1024,256]{1,0:T(8,128)(2,1)S(1)}, u32[]{:S(2)}, u32[]{:S(2)}) collective-permute-start(bf16[1024,256]{1,0:T(8,128)(2,1)S(1)} %slice_bitcast_fusion.refs_2_), channel_id=1, source_target_pairs={{0,1},{1,0},{2,3},{3,2},{4,5},{5,4},{6,7},{7,6},{8,9},{9,8},{10,11... | collective-permute-start | bytes 1572872 | tf_op jit(solution)/shard_map/ppermute | solution.py:59
  27.6 4.4 %collective-permute-start.13 = (bf16[576,256]{1,0:T(8,128)(2,1)S(1)}, bf16[576,256]{1,0:T(8,128)(2,1)S(1)}, u32[]{:S(2)}, u32[]{:S(2)}) collective-permute-start(bf16[576,256]{1,0:T(8,128)(2,1)S(1)} %shard_map.122.refs_0_), channel_id=1, source_target_pairs={{0,1},{1,0},{2,3},{3,2},{4,5},{5,4},{6,7},{7,6},{8,9},{9,8},{10,11... | collective-permute-start | bytes 884744 | tf_op jit(solution)/shard_map/ppermute | solution.py:59
  32.0 1.6 %collective-permute-start.9 = (bf16[576,256]{1,0:T(8,128)(2,1)S(1)}, bf16[576,256]{1,0:T(8,128)(2,1)S(1)}, u32[]{:S(2)}, u32[]{:S(2)}) collective-permute-start(bf16[576,256]{1,0:T(8,128)(2,1)S(1)} %collective-permute-done.8.refs_0_), channel_id=1, source_target_pairs={{0,1},{1,0},{2,3},{3,2},{4,5},{5,4},{6,7},{7,6},{8,9},{9,8},{10,11... | collective-permute-start | bytes 884744 | tf_op jit(solution)/shard_map/ppermute | solution.py:59
  35.1 6.3 %collective-permute-start.14 = (bf16[256,256]{1,0:T(8,128)(2,1)S(1)}, bf16[256,256]{1,0:T(8,128)(2,1)S(1)}, u32[]{:S(2)}, u32[]{:S(2)}) collective-permute-start(bf16[256,256]{1,0:T(8,128)(2,1)S(1)} %get-tuple-element.88), channel_id=1, source_target_pairs={{0,8},{4,12},{8,0},{12,4},{16,24},{20,28},{24,16},{28,20},{1,9},{5... | collective-permute-start | bytes 393224 | tf_op jit(solution)/shard_map/ppermute | solution.py:59
  35.3 8.8 %collective-permute-start.18 = (bf16[512,256]{1,0:T(8,128)(2,1)S(1)}, bf16[512,256]{1,0:T(8,128)(2,1)S(1)}, u32[]{:S(2)}, u32[]{:S(2)}) collective-permute-start(bf16[512,256]{1,0:T(8,128)(2,1)S(1)} %get-tuple-element.97.cells), channel_id=1, source_target_pairs={{0,4},{4,0},{8,12},{12,8},{16,20},{20,16},{24,28},{28,24},{1,5},{5... | collective-permute-start | bytes 786440 | tf_op jit(solution)/shard_map/ppermute | solution.py:59
  36.4 5.2 %collective-permute-start.15 = (bf16[64,256]{1,0:T(8,128)(2,1)S(1)}, bf16[64,256]{1,0:T(8,128)(2,1)S(1)}, u32[]{:S(2)}, u32[]{:S(2)}) collective-permute-start(bf16[64,256]{1,0:T(8,128)(2,1)S(1)} %get-tuple-element.90.refs_0_), channel_id=1, source_target_pairs={{0,16},{4,20},{8,24},{12,28},{16,0},{20,4},{24,8},{28,12},{1,17},{... | collective-permute-start | bytes 98312 | tf_op jit(solution)/shard_map/ppermute | solution.py:59
  41.5 4.7 %collective-permute-start.16 = (bf16[128,256]{1,0:T(8,128)(2,1)S(1)}, bf16[128,256]{1,0:T(8,128)(2,1)S(1)}, u32[]{:S(2)}, u32[]{:S(2)}) collective-permute-start(bf16[128,256]{1,0:T(8,128)(2,1)S(1)} %get-tuple-element.93), channel_id=1, source_target_pairs={{0,4},{4,0},{8,12},{12,8},{16,20},{20,16},{24,28},{28,24},{1,5},{5... | collective-permute-start | bytes 196616 | tf_op jit(solution)/shard_map/ppermute | solution.py:59
  41.6 4.6 %collective-permute-start.17 = (bf16[128,256]{1,0:T(8,128)(2,1)S(1)}, bf16[128,256]{1,0:T(8,128)(2,1)S(1)}, u32[]{:S(2)}, u32[]{:S(2)}) collective-permute-start(bf16[128,256]{1,0:T(8,128)(2,1)S(1)} %shard_map.129.refs_0_), channel_id=1, source_target_pairs={{0,8},{4,12},{8,0},{12,4},{16,24},{20,28},{24,16},{28,20},{1,9},{5... | collective-permute-start | bytes 196616 | tf_op jit(solution)/shard_map/ppermute | solution.py:59
  44.1 10.1 %collective-permute-start.19 = (bf16[512,256]{1,0:T(8,128)(2,1)S(1)}, bf16[512,256]{1,0:T(8,128)(2,1)S(1)}, u32[]{:S(2)}, u32[]{:S(2)}) collective-permute-start(bf16[512,256]{1,0:T(8,128)(2,1)S(1)} %collective-permute-done.18.cells), channel_id=1, source_target_pairs={{0,8},{4,0},{8,16},{12,4},{16,24},{20,12},{24,28},{28,20},{1,9},{5... | collective-permute-start | bytes 786440 | tf_op jit(solution)/shard_map/ppermute | solution.py:70
  46.2 8.0 %collective-permute-start.20 = (bf16[256,256]{1,0:T(8,128)(2,1)S(1)}, bf16[256,256]{1,0:T(8,128)(2,1)S(1)}, u32[]{:S(2)}, u32[]{:S(2)}) collective-permute-start(bf16[256,256]{1,0:T(8,128)(2,1)S(1)} %shard_map.132.mine), channel_id=1, source_target_pairs={{0,4},{4,0},{8,12},{12,8},{16,20},{20,16},{24,28},{28,24},{1,5},{5... | collective-permute-start | bytes 393224 | tf_op jit(solution)/shard_map/ppermute | solution.py:59
  48.7 4.8 %collective-permute-start.21 = (bf16[64,256]{1,0:T(8,128)(2,1)S(1)}, bf16[64,256]{1,0:T(8,128)(2,1)S(1)}, u32[]{:S(2)}, u32[]{:S(2)}) collective-permute-start(bf16[64,256]{1,0:T(8,128)(2,1)S(1)} %get-tuple-element.99), channel_id=1, source_target_pairs={{0,16},{4,20},{8,24},{12,28},{16,0},{20,4},{24,8},{28,12},{1,17},{... | collective-permute-start | bytes 98312 | tf_op jit(solution)/shard_map/ppermute | solution.py:59
